TPU v7x, 256 devices: a whole 4x4x8 slice. The times are simulated.
256 devices in a mesh: pair: 32 (over z, y), fock: 8 (over x, core).
Axes of the slice: x: 4, y: 4, z: 8, core: 2. Of those that a mesh axis runs over, the one named last changes fastest.
Arguments:
- geminal: bfloat16 [32, 12288, 128], P('pair', 'fock'), may hold values from -9 to 9
- fock_matrix: bfloat16 [8, 32, 48, 12288], P(None, 'pair', None, 'fock'), as said below
- slot_occupied_pair: int32 [32], replicated, may hold values from 0 to 1
- slot_column_block: int32 [32], replicated, may hold values from 0 to 7
- slot_live: int32 [32], replicated, may hold values from 0 to 1, as said below
Outputs:
- fock_geminal: bfloat16 [32, 12288, 128], P(None, ('fock', 'pair'))
- bmat: float32 [2, 2], replicated
Inputs may be any that keep to these rules, and one draw needn't show every extreme that they name: `slot_live`: exactly 24 slots are 1. `fock_matrix`: the matrix read as in the first step is symmetric.
All inputs are finite; a program needn't handle non-finite values.
Results may differ from a plain program's by a relative error of at most 0.001.
Values may be sent and summed in bfloat16 or wider, within the bound.
No kernel may reach another device: no remote copies, remote signals or barrier semaphores. Data moves between devices by JAX's collectives and lax.ppermute only.
A program may use at most 128 MiB of HBM per device.

v0:
```python
import jax
import jax.numpy as jnp
from jax import lax
from jax.sharding import PartitionSpec as P

HIGHEST = lax.Precision.HIGHEST


def panel_total(products):
    row_width = products.shape[1] // lax.axis_size("fock")
    summed = lax.psum(products, "fock")
    return lax.dynamic_slice_in_dim(summed, lax.axis_index("fock") * row_width, row_width, 1)


def on_device(geminal, fock_matrix, slot_occupied_pair, slot_column_block, slot_live):
    n_fock = lax.axis_size("fock")
    panel_rows = fock_matrix.shape[3]
    row_width = fock_matrix.shape[2]
    local_fock = fock_matrix.reshape(n_fock * row_width, panel_rows)
    gathered = lax.all_gather(geminal, "pair", axis=0, tiled=True)
    alive_mask = slot_live.astype(jnp.float32)
    products = jnp.einsum("kr,srb->skb", local_fock, gathered, preferred_element_type=jnp.float32)
    own_share = panel_total(products)
    fock_geminal = (own_share * alive_mask[:, None, None]).astype(jnp.bfloat16)
    own_rows = lax.dynamic_slice_in_dim(gathered, lax.axis_index("pair") * row_width, row_width, 1)
    intersections = jnp.einsum(
        "kwb,lwb->kl", own_rows, fock_geminal, preferred_element_type=jnp.float32
    )
    intersections = lax.psum(intersections, ("pair", "fock"))
    same_block = (slot_column_block[:, None] == slot_column_block[None, :]).astype(jnp.float32)
    matching = alive_mask[:, None] * alive_mask[None, :] * same_block
    onehot = (slot_occupied_pair[:, None] == jnp.arange(2, dtype=jnp.int32)[None, :]).astype(
        jnp.float32
    )
    inner = jnp.dot(onehot.T, matching * intersections, precision=HIGHEST)
    normalizer = 1.0 / (panel_rows * n_fock * gathered.shape[2])
    bmat = jnp.dot(inner, onehot, precision=HIGHEST) * normalizer
    return (fock_geminal, bmat)


def solution(mesh):
    return jax.shard_map(
        on_device,
        mesh=mesh,
        in_specs=(P("pair", "fock", None), P(None, "pair", None, "fock"), P(), P(), P()),
        out_specs=(P(None, ("fock", "pair"), None), P()),
        check_vma=False,
    )
```

profile of v0, /device:TPU:1, one launch (start us, length us, event | category | flops | bytes accessed | tf_op | source)
XLA Modules:
  0.0 321.3 jit_solution(16570011421115790931)
XLA Ops:
  7.2 0.0 copy-start
  7.2 0.0 all-gather.2.cloned.1.call-start
  7.2 0.7 all-gather.2.cloned.1.call-update
  7.9 0.0 all-reduce.2.cloned.1.call-start
  8.0 125.8 %all-gather.2.cloned.1.call-done = bf16[32,1536,128]{2,1,0:T(8,128)(2,1)} async-done(((bf16[1,1536,128]{2,1,0:T(8,128)(2,1)}), bf16[32,1536,128]{2,1,0:T(8,128)(2,1)}) %all-gather.2.cloned.1.call-update) | async-done | bytes 12582928 | tf_op jit(solution)/shard_map/all_gather | solution.py:20
  133.8 0.0 copy-done
  133.8 11.4 %convolution_bitcast_fusion = f32[32,384,128]{1,2,0:T(8,128)} fusion(bf16[32,1536,128]{2,1,0:T(8,128)(2,1)} %all-gather.2.cloned.1.call-done, bf16[384,1536,1]{1,0,2:T(8,128)(2,1)S(1)} %bitcast.11), kind=kOutput, calls=%fused_computation | convolution fusion | flops 4831838208 | bytes 20054016 | tf_op jit(solution)/shard_map/kr,srb->skb/dot_general | solution.py:22
  145.2 0.0 copy-start.1
  145.2 0.0 copy-start.2
  145.2 0.0 copy-start.3
  145.2 0.0 all-reduce.2.cloned.1.call-update
  145.2 0.6 copy-done.1
  145.8 1.0 constant_dynamic-slice_fusion
  146.9 84.9 %all-reduce.2.cloned.1.call-done = f32[32,384,128]{1,2,0:T(8,128)} async-done(((f32[32,384,128]{1,2,0:T(8,128)}), f32[32,384,128]{1,2,0:T(8,128)}) %all-reduce.2.cloned.1.call-update) | async-done | bytes 6291472 | tf_op jit(solution)/shard_map/psum | solution.py:11
  231.7 2.8 multiply_convert_fusion
  234.6 1.1 copy.10
  235.6 0.7 copy.13
  236.4 0.2 convolution_bitcast_fusion.1
  236.6 76.8 %psum.15 = f32[32,32]{1,0:T(8,128)S(1)} all-reduce(f32[32,32]{1,0:T(8,128)S(1)} %convolution_bitcast_fusion.1), channel_id=1, replica_groups=mesh['pair'=32,'fock'=8] {'pair','fock'}, use_global_device_ids=true, to_apply=%region_1.0 | all-reduce | flops 1024 | bytes 8192 | tf_op jit(solution)/shard_map/psum | solution.py:29
  313.4 0.0 copy-done.2
  313.4 0.0 copy-done.3
  313.4 0.3 fusion.1
  313.7 0.8 convolution_multiply_fusion
  (1 shorter events, 0.0 us)
Async XLA Ops:
  7.2 126.6 %copy-start = (bf16[8,1,48,1536]{3,2,1,0:T(8,128)(2,1)S(1)}, bf16[8,1,48,1536]{3,2,1,0:T(8,128)(2,1)}, u32[]{:S(2)}) copy-start(bf16[8,1,48,1536]{3,2,1,0:T(8,128)(2,1)} %param.6) | copy-start | bytes 3538948
  7.2 126.6 %all-gather.2.cloned.1.call-start = ((), (), s32[]{:S(2)}) async-start(), calls=%async_computation | async-start | bytes 12976128 | tf_op jit(solution)/shard_map/all_gather | solution.py:20
  7.9 223.8 %all-reduce.2.cloned.1.call-start = ((), (), s32[]{:S(2)}) async-start(), calls=%async_computation.1 | async-start | bytes 12582912 | tf_op jit(solution)/shard_map/psum | solution.py:11
  145.2 0.7 copy-start.1
  145.2 168.2 %copy-start.2 = (s32[32]{0:T(128)S(1)}, s32[32]{0:T(128)}, u32[]{:S(2)}) copy-start(s32[32]{0:T(128)} %param.8) | copy-start | bytes 388
  145.2 168.2 %copy-start.3 = (s32[32]{0:T(128)S(1)}, s32[32]{0:T(128)}, u32[]{:S(2)}) copy-start(s32[32]{0:T(128)} %param.7) | copy-start | bytes 388
Sparse Core Ops, SparseCore 0:
  10.6 123.1 all-gather.1
  145.3 86.3 all-reduce.1
where the time goes:
time: 321 us
  waiting for transfers between devices  211 us (66%)
  blocking collectives  76.8 us (24%)
  between operations  14.1 us (4%)
  matrix products  12.7 us (4%)
  local copies, waits for them, and re-layouts  3.44 us (1%)
    all_gather x1, waiting for transfers between devices, on_device(): gathered = lax.all_gather(geminal, 'pair', axis=0, tiled=True)  126 us
    psum x1, waiting for transfers between devices, panel_total(): summed = lax.psum(products, 'fock')  84.9 us
    psum x1, blocking collectives, on_device(): intersections = lax.psum(intersections, ('pair', 'fock'))  76.8 us
    dot_general x1, matrix products, on_device(): jnp.einsum('kr,srb->skb', local_fock, gathered, preferred_element_type=jn...  11.4 us
  transfers between devices with their start and end apart: 2, of which 2 were waited for; matrix products, arithmetic and copies ran while one was open for 0% of the time, Pallas kernels for 0%

commit v1 on v0

v1 whole, which is shorter than its diff:
```python
import functools

import jax
import jax.numpy as jnp
from jax import lax
from jax.experimental import pallas as pl
from jax.experimental.pallas import tpu as pltpu
from jax.sharding import PartitionSpec as P

HIGHEST = lax.Precision.HIGHEST
NZ, NY, NX, NC = 8, 4, 4, 2
SAME_CORE = [[x * NC + c for x in range(NX)] for c in range(NC)]

VMEM = pl.BlockSpec(memory_space=pltpu.VMEM)
SMEM = pl.BlockSpec(memory_space=pltpu.SMEM)
ANY = pl.BlockSpec(memory_space=pl.ANY)
CHEAP = pl.CostEstimate(flops=1, bytes_accessed=1, transcendentals=0)

NEAR, FAR = (0, 1, 7, 2, 6), (3, 5, 4)
ORDER = NEAR + FAR
FIRST = ((0, NEAR), (1, NEAR))
SECOND = ((0, FAR), (1, FAR), (2, ORDER), (3, ORDER))


def offset(j, x):
    return (0, -1, 1, 2)[j] if x < NX // 2 else (0, 1, -1, 2)[j]


def shift_z(v, s):
    return lax.ppermute(
        v, "pair", [(z * NY + y, (z + s) % NZ * NY + y) for z in range(NZ) for y in range(NY)]
    )


def shift_y(v, s):
    return lax.ppermute(
        v, "pair", [(z * NY + y, z * NY + (y + s) % NY) for z in range(NZ) for y in range(NY)]
    )


def to_owner(v, j):
    moves = []
    for z in range(NZ):
        for y in range(NY):
            for x in range(NX):
                for c in range(NC):
                    to = z * NY + (y + offset(j, x)) % NY
                    moves.append(((z * NY + y) * NX * NC + x * NC + c, to * NX * NC + x * NC + c))
    return lax.ppermute(v, ("pair", "fock"), moves) if j else v


def swap_core(v):
    return lax.ppermute(
        v, "fock", [(x * NC + c, x * NC + 1 - c) for x in range(NX) for c in range(NC)]
    )


def total_over(v, axis):
    n = lax.axis_size(axis)
    return lax.all_to_all(jnp.broadcast_to(v, (n,) + v.shape), axis, 0, 0).sum(0)


def split_kernel(own_ref, low_ref, high_ref):
    half = own_ref.shape[0] // 2
    low_ref[...] = own_ref[:half]
    high_ref[...] = own_ref[half:]


def split(own):
    half = jax.ShapeDtypeStruct((own.shape[0] // 2,) + own.shape[1:], own.dtype)
    return pl.pallas_call(
        split_kernel,
        out_shape=[half, half],
        in_specs=[VMEM],
        out_specs=[VMEM] * 2,
        compiler_params=pltpu.CompilerParams(vmem_limit_bytes=8 * 2**20),
        cost_estimate=CHEAP,
    )(own)


def join_kernel(low_ref, high_ref, left_ref, right_ref, to_right_ref, to_left_ref):
    half = low_ref.shape[0]
    to_right_ref[:half] = left_ref[...]
    to_right_ref[half:] = high_ref[...]
    to_left_ref[:half] = low_ref[...]
    to_left_ref[half:] = right_ref[...]


def join(low, high, left, right):
    whole = jax.ShapeDtypeStruct((2 * low.shape[0],) + low.shape[1:], low.dtype)
    return pl.pallas_call(
        join_kernel,
        out_shape=[whole, whole],
        in_specs=[VMEM] * 4,
        out_specs=[VMEM] * 2,
        compiler_params=pltpu.CompilerParams(vmem_limit_bytes=12 * 2**20),
        cost_estimate=CHEAP,
    )(low, high, left, right)


def pack_kernel(keep_ref, recv_ref, out_ref):
    _, width, total = keep_ref.shape
    columns = out_ref.shape[2] - total
    lane = lax.broadcasted_iota(jnp.int32, (width, columns), 1)
    exponents = jnp.zeros((width, columns), jnp.int32)
    for u in range(total // columns):
        span = slice(u * columns, (u + 1) * columns)
        value = keep_ref[0, :, span] + recv_ref[0, :, span]
        top = jnp.maximum(jnp.max(jnp.abs(value), axis=1, keepdims=True), 2.0**-100)
        power = jnp.ceil(jnp.log2(top)) - 15.0
        scaled = jnp.clip(jnp.round(value * jnp.exp2(-power)), -32767.0, 32767.0)
        out_ref[0, :, span] = scaled.astype(jnp.int32).astype(jnp.int16)
        exponents = jnp.where(lane == u, power.astype(jnp.int32), exponents)
    out_ref[0, :, total:] = exponents.astype(jnp.int16)


def pack(keep, recv, columns):
    n, width, total = keep.shape
    return pl.pallas_call(
        pack_kernel,
        out_shape=jax.ShapeDtypeStruct((n, width, total + columns), jnp.int16),
        grid=(n,),
        in_specs=[pl.BlockSpec((1, width, total), lambda t: (t, 0, 0))] * 2,
        out_specs=pl.BlockSpec((1, width, total + columns), lambda t: (t, 0, 0)),
        compiler_params=pltpu.CompilerParams(vmem_limit_bytes=16 * 2**20),
        cost_estimate=CHEAP,
    )(keep, recv)


def products_kernel(plan, n_f, g_rows, at_ref, *refs):
    n_g = sum(len(r) for r in g_rows)
    f_refs, g_refs = refs[:n_f], list(refs[n_f : n_f + n_g])
    away_ref, keep_ref, *rows_ref, joined = refs[n_f + n_g :]
    columns = g_refs[0].shape[1]
    first_core = at_ref[0] == 0
    for j, rows in enumerate(g_rows):
        at = 0
        for n in rows:
            joined[at : at + n, j * columns : (j + 1) * columns] = g_refs.pop(0)[...]
            at += n
    for ref in rows_ref:
        count = ref.shape[0]
        ref[...] = joined[pl.ds(pl.multiple_of(at_ref[1] * count, 64), count), :]
    at = 0
    for pieces, lo, hi in plan:
        span = (hi - lo) * columns
        parts = []
        for i, part in pieces:
            n, cores, width, depth = f_refs[i].shape
            value = f_refs[i][...] if part is None else f_refs[i][part * (n // 2) : (part + 1) * (n // 2)]
            parts.append(value.reshape(-1, depth))
        lhs = parts[0] if len(parts) == 1 else jnp.concatenate(parts, axis=0)
        out = jnp.dot(lhs, joined[:, lo * columns : hi * columns], preferred_element_type=jnp.float32)
        out = out.reshape(NX, NC, width, span)
        keep_ref[:, :, at : at + span] = jnp.where(first_core, out[:, 0], out[:, 1])
        away_ref[:, :, at : at + span] = jnp.where(first_core, out[:, 1], out[:, 0])
        at += span


def products(plan, at, f_arrays, g_pieces, with_rows):
    width, rows = f_arrays[0].shape[2:]
    g_rows = tuple(tuple(v.shape[0] for v in slot) for slot in g_pieces)
    g_flat = [v for slot in g_pieces for v in slot]
    columns = g_flat[0].shape[1]
    units = sum(hi - lo for _, lo, hi in plan)
    terms = jax.ShapeDtypeStruct((NX, width, units * columns), jnp.float32)
    own = jax.ShapeDtypeStruct((NY * width, len(g_pieces) * columns), jnp.bfloat16)
    return pl.pallas_call(
        functools.partial(products_kernel, plan, len(f_arrays), g_rows),
        out_shape=[terms, terms] + [own] * with_rows,
        in_specs=[SMEM] + [VMEM] * (len(f_arrays) + len(g_flat)),
        out_specs=[VMEM] * (2 + with_rows),
        scratch_shapes=[pltpu.VMEM((rows, len(g_pieces) * columns), jnp.bfloat16)],
        compiler_params=pltpu.CompilerParams(vmem_limit_bytes=28 * 2**20),
        cost_estimate=CHEAP,
    )(at, *f_arrays, *g_flat)


def unpack_into(total_ref, mask_ref, plan, done_refs, held, arrived):
    n, width, _ = total_ref.shape
    columns = mask_ref.shape[1] // NZ
    copies = [pltpu.make_async_copy(total_ref.at[t], held.at[t], arrived.at[t]) for t in range(n)]
    for copy in copies:
        copy.start()
    for copy in copies:
        copy.wait()
    units = held.shape[2] - columns
    scales = [jnp.exp2(held[t, :, units:].astype(jnp.int32).astype(jnp.float32)) for t in range(n)]
    made, u = [], 0
    for done_ref, (_, es) in zip(done_refs, plan):
        for i, e in enumerate(es):
            value = 0.0
            for t in range(n):
                term = held[t, :, u * columns : (u + 1) * columns].astype(jnp.int32).astype(jnp.float32)
                value = value + term * scales[t][:, u : u + 1]
            rounded = (value * mask_ref[:, e * columns : (e + 1) * columns]).astype(jnp.bfloat16)
            done_ref[:, i * columns : (i + 1) * columns] = rounded
            u += 1


def dots_into(plan, at_ref, done_refs, weight_ref, row_refs, bmat_ref, dots):
    width = done_refs[0].shape[0]
    columns = dots.shape[1]
    starts = [pl.multiple_of(at_ref[j] * width, 16) for j, _ in plan]
    count = {e for _, es in plan for e in es}
    if len(count) < NZ:
        dots[...] = jnp.zeros_like(dots)
    for k in range(NY):
        for f in range(NZ):
            sums = {}
            for (_, es), start, done_ref in zip(plan, starts, done_refs):
                row = row_refs[k][pl.ds(start, width), f * columns : (f + 1) * columns].astype(jnp.float32)
                for i, e in enumerate(es):
                    term = row * done_ref[:, i * columns : (i + 1) * columns].astype(jnp.float32)
                    term = term.reshape(width // 8, 8, columns).sum(0)
                    sums[e] = sums[e] + term if e in sums else term
            for e, term in sums.items():
                i = (k * NZ + f) * NZ + e
                dots[i : i + 1] = term.sum(0, keepdims=True)
    bmat_ref[...] = (dots[...].sum(1, keepdims=True) * weight_ref[...]).sum(0, keepdims=True)


def early_kernel(plan, total_ref, mask_ref, *refs):
    *done_refs, held, arrived = refs
    unpack_into(total_ref, mask_ref, plan, done_refs, held, arrived)


def early_dots_kernel(plan, at_ref, weight_ref, *refs):
    n = len(plan)
    dots_into(plan, at_ref, refs[:n], weight_ref, refs[n : n + NY], refs[n + NY], refs[n + NY + 1])


def late_kernel(plan, at_ref, total_ref, mask_ref, weight_ref, bmat_in_ref, *refs):
    row_refs, refs = refs[:NY], refs[NY:]
    *done_refs, bmat_ref, held, arrived, dots = refs
    unpack_into(total_ref, mask_ref, plan, done_refs, held, arrived)
    dots_into(plan, at_ref, done_refs, weight_ref, row_refs, bmat_ref, dots)
    bmat_ref[...] += bmat_in_ref[...]


def done_shapes(plan, width, columns):
    return [jax.ShapeDtypeStruct((width, len(es) * columns), jnp.bfloat16) for _, es in plan]


def early_finish(plan, total, mask):
    return pl.pallas_call(
        functools.partial(early_kernel, plan),
        out_shape=done_shapes(plan, total.shape[1], mask.shape[1] // NZ),
        in_specs=[ANY, VMEM],
        out_specs=[VMEM] * len(plan),
        scratch_shapes=[pltpu.VMEM(total.shape, total.dtype), pltpu.SemaphoreType.DMA((total.shape[0],))],
        compiler_params=pltpu.CompilerParams(vmem_limit_bytes=16 * 2**20),
        cost_estimate=CHEAP,
    )(total, mask)


def early_dots(plan, at, weight, done, rows):
    columns = rows[0].shape[1] // NZ
    return pl.pallas_call(
        functools.partial(early_dots_kernel, plan),
        out_shape=jax.ShapeDtypeStruct((1, weight.shape[1]), jnp.float32),
        in_specs=[SMEM] + [VMEM] * (1 + len(done) + NY),
        out_specs=VMEM,
        scratch_shapes=[pltpu.VMEM((NY * NZ * NZ, columns), jnp.float32)],
        compiler_params=pltpu.CompilerParams(vmem_limit_bytes=16 * 2**20),
        cost_estimate=CHEAP,
    )(at, weight, *done, *rows)


def late_finish(plan, at, total, mask, weight, bmat, rows):
    columns = rows[0].shape[1] // NZ
    return pl.pallas_call(
        functools.partial(late_kernel, plan),
        out_shape=done_shapes(plan, total.shape[1], columns)
        + [jax.ShapeDtypeStruct((1, weight.shape[1]), jnp.float32)],
        in_specs=[SMEM, ANY] + [VMEM] * (3 + NY),
        out_specs=[VMEM] * (len(plan) + 1),
        scratch_shapes=[
            pltpu.VMEM(total.shape, total.dtype),
            pltpu.SemaphoreType.DMA((total.shape[0],)),
            pltpu.VMEM((NY * NZ * NZ, columns), jnp.float32),
        ],
        compiler_params=pltpu.CompilerParams(vmem_limit_bytes=16 * 2**20),
        cost_estimate=CHEAP,
    )(at, total, mask, weight, bmat, *rows)


def place_kernel(plan, at_ref, *refs):
    *piece_refs, out_ref = refs
    columns = out_ref.shape[2]
    for piece_ref, (k, es) in zip(piece_refs, plan):
        for j, e in enumerate(es):
            slot = lax.rem(at_ref[0] + e, NZ) * NY + at_ref[1 + k]
            out_ref[slot] = piece_ref[:, j * columns : (j + 1) * columns]


def place(plan, at, pieces, columns):
    width = pieces[0].shape[0]
    return pl.pallas_call(
        functools.partial(place_kernel, plan),
        out_shape=jax.ShapeDtypeStruct((NZ * NY, width, columns), jnp.bfloat16),
        in_specs=[SMEM] + [VMEM] * len(pieces),
        out_specs=VMEM,
        compiler_params=pltpu.CompilerParams(vmem_limit_bytes=8 * 2**20),
        cost_estimate=CHEAP,
    )(at, *pieces)


def on_device(geminal, fock_matrix, slot_occupied_pair, slot_column_block, slot_live):
    n_fock, _, width, panel_rows = fock_matrix.shape
    columns = geminal.shape[2]
    n_slots = NZ * NY
    pair_at, fock_at = lax.axis_index("pair"), lax.axis_index("fock")
    z, y = pair_at // NY, pair_at % NY
    at = jnp.stack([fock_at % NC, z])

    own = fock_matrix.reshape(NX, NC, width, panel_rows)
    low, high = split(own)
    g, low, high = lax.optimization_barrier((geminal[0], low, high))
    from_left, from_right = shift_y(low, 1), shift_y(high, -1)
    to_right, to_left = join(low, high, from_left, from_right)
    after_left, after_right = shift_y(to_right, 1), shift_y(to_left, -1)
    f_arrays = [own, from_left, from_right, after_left, after_right]
    f_blocks = (((0, None),), ((1, None), (2, None)), ((4, 0), (3, 1)), ((3, 0), (4, 1)))

    half = panel_rows // 2
    slots = {0: g}
    slots[1], slots[7] = shift_z(slots[0], -1), shift_z(slots[0], 1)
    slots[2], slots[6] = shift_z(slots[1], -1), shift_z(slots[7], 1)
    slots[3], slots[5] = shift_z(slots[2], -1), shift_z(slots[6], 1)
    slots = {e: [v] for e, v in slots.items()}

    at_z = (z + jnp.array(ORDER, jnp.int32)) % NZ
    at_y = (y - jnp.arange(NY, dtype=jnp.int32)) % NY
    index = (at_z[None, :] * NY + at_y[:, None]).reshape(-1)
    chosen = (index[:, None] == jnp.arange(n_slots, dtype=jnp.int32)[None, :]).astype(jnp.float32)
    facts = jnp.stack([slot_live, slot_column_block, slot_occupied_pair], axis=1).astype(jnp.float32)
    facts = jnp.dot(chosen, facts, precision=HIGHEST)
    alive, block, occupied = facts[:, 0], facts[:, 1], facts[:, 2]
    matching = alive[:, None] * alive[None, :NZ] * (block[:, None] == block[None, :NZ])
    normalizer = 1.0 / (panel_rows * n_fock * columns)
    entry = 2 * occupied[:, None] + occupied[None, :NZ]
    entries = jnp.arange(128, dtype=jnp.float32)
    weight = (matching[:, :, None] * normalizer * (entry[:, :, None] == entries)).reshape(-1, 128)
    mask = jnp.repeat(alive[:NZ], columns).reshape(1, -1)

    x = fock_at // NC
    sign = jnp.where(x < NX // 2, -1, 1)
    steps = jnp.stack([0 * sign, sign, -sign, 0 * sign + 2])
    rows_at, classes = (y + steps) % NY, (y - steps) % NY

    def start(plan, order, arrays, with_rows):
        plan = tuple((f_blocks[j], order.index(es[0]), order.index(es[0]) + len(es)) for j, es in plan)
        away, *rest = products(plan, at, arrays, [slots[e] for e in order], with_rows)
        return swap_core(away), *rest

    def spread(total):
        return lax.all_to_all(total, "fock", 0, 0, axis_index_groups=SAME_CORE)

    def places(plan):
        return tuple((j, tuple(ORDER.index(e) for e in es)) for j, es in plan)

    def owned(plan, done):
        return [to_owner(v, j) for (j, _), v in zip(plan, done)]

    first = lax.optimization_barrier((*f_arrays[:3], to_right, to_left))[:3]
    recv, keep = start(FIRST, NEAR, list(first), 0)
    packed = pack(keep, recv, columns)
    slots[3], slots[5], packed = lax.optimization_barrier((slots[3], slots[5], packed))
    slots[4] = [shift_z(slots[3][0][:half], -1), shift_z(slots[5][0][half:], 1)]
    early = spread(packed)
    *f_arrays, early = lax.optimization_barrier((*f_arrays, early))
    done = early_finish(places(FIRST), early, mask)
    moved = owned(FIRST, done)
    recv, keep, joined = start(SECOND, ORDER, f_arrays, 1)
    rows = [joined, shift_y(joined, 1), shift_y(joined, 2), shift_y(joined, -1)]
    late = spread(pack(keep, recv, columns))
    bmat = early_dots(places(FIRST), rows_at, weight, done, rows)
    *done, bmat = late_finish(places(SECOND), rows_at, late, mask, weight, bmat, rows)
    more = owned(SECOND, done)
    bmat = total_over(bmat, "pair")

    at_place = jnp.concatenate([z.reshape(1), classes])
    *pieces, bmat = lax.optimization_barrier((*moved, *more, bmat))
    out = place(FIRST + SECOND, at_place, pieces, columns)
    return out, total_over(bmat, "fock")[0, :4].reshape(2, 2)


def solution(mesh):
    return jax.shard_map(
        on_device,
        mesh=mesh,
        in_specs=(P("pair", "fock", None), P(None, "pair", None, "fock"), P(), P(), P()),
        out_specs=(P(None, ("fock", "pair"), None), P()),
        check_vma=False,
    )
```

time: 321 us -> 151 us (0.47)
  waiting for transfers between devices: 211 us -> 56.8 us
  blocking collectives: 76.8 us -> 0 us
  starting transfers between devices: 0.08 us -> 52.5 us
  Pallas kernels: 0 us -> 27.3 us
  between operations: 14.1 us -> 0.83 us
  matrix products: 12.7 us -> 0.19 us
  local copies, waits for them, and re-layouts: 3.44 us -> 12.1 us
    all_gather x1 -> x0, waiting for transfers between devices: 126 us -> none  [on_device(): gathered = lax.all_gather(geminal, 'pair', axis=0, tiled=True)]
    psum x1 -> x0, waiting for transfers between devices: 84.9 us -> none  [panel_total(): summed = lax.psum(products, 'fock')]
    psum x1 -> x0, blocking collectives: 76.8 us -> none  [on_device(): intersections = lax.psum(intersections, ('pair', 'fock'))]
    ppermute x0 -> x21, waiting for transfers between devices: none -> 45.2 us  [the longest x7 25 us: shift_y(): lax.ppermute(v, 'pair', [(z * NY + y, z * NY + (y + s) % NY) for z in ran...]
    ppermute x0 -> x21, starting transfers between devices: none -> 31.5 us  [the longest x8 12.8 us: shift_z(): lax.ppermute(v, 'pair', [(z * NY + y, (z + s) % NZ * NY + y) for z in ran...]
    pallas_call x0 -> x10, Pallas kernels: none -> 27.3 us  [the longest x2 11.7 us: products(): pl.pallas_call(functools.partial(products_kernel, plan, len(f_arrays), g_...]
    all_to_all x0 -> x4, starting transfers between devices: none -> 21 us  [the longest x2 12.3 us: total_over(): lax.all_to_all(jnp.broadcast_to(v, (n,) + v.shape), axis, 0, 0).sum(0)]
    dot_general x4 -> x1, matrix products: 12.7 us -> 0.19 us  [on_device(): facts = jnp.dot(chosen, facts, precision=HIGHEST)]
  transfers between devices with their start and end apart: 2 -> 25, of which waited for: 2 -> 12; matrix products, arithmetic and copies ran while one was open for 0% -> 4% of each run, Pallas kernels for 0% -> 8%
where the time goes in v1:
time: 151 us; the launch traced here: 150 us
  waiting for transfers between devices  56.8 us (38%)
  starting transfers between devices  52.5 us (35%)
  Pallas kernels  27.3 us (18%)
  local copies, waits for them, and re-layouts  12.1 us (8%)
    ppermute x7, waiting for transfers between devices, shift_y(): lax.ppermute(v, 'pair', [(z * NY + y, z * NY + (y + s) % NY) for z in ran...  25 us
    ppermute x8, waiting for transfers between devices, shift_z(): lax.ppermute(v, 'pair', [(z * NY + y, (z + s) % NZ * NY + y) for z in ran...  16.5 us
    ppermute x8, starting transfers between devices, shift_z(): lax.ppermute(v, 'pair', [(z * NY + y, (z + s) % NZ * NY + y) for z in ran...  12.8 us
    all_to_all x2, starting transfers between devices, total_over(): lax.all_to_all(jnp.broadcast_to(v, (n,) + v.shape), axis, 0, 0).sum(0)  12.3 us
    pallas_call x2, Pallas kernels, products(): pl.pallas_call(functools.partial(products_kernel, plan, len(f_arrays), g_...  11.7 us
    all_to_all x2, waiting for transfers between devices, total_over(): lax.all_to_all(jnp.broadcast_to(v, (n,) + v.shape), axis, 0, 0).sum(0)  11.6 us
    ppermute x7, starting transfers between devices, shift_y(): lax.ppermute(v, 'pair', [(z * NY + y, z * NY + (y + s) % NY) for z in ran...  9.28 us
    all_to_all x2, starting transfers between devices, spread(): return lax.all_to_all(total, 'fock', 0, 0, axis_index_groups=SAME_CORE)  8.66 us
  transfers between devices with their start and end apart: 25, of which 12 were waited for; matrix products, arithmetic and copies ran while one was open for 4% of the time, Pallas kernels for 8%

profile of v1, /device:TPU:1, one launch (start us, length us, event | category | flops | bytes accessed | tf_op | source)
XLA Modules:
  0.0 150.2 jit_solution(5316936852112509763)
XLA Ops:
  0.6 1.3 copy-done
  1.9 1.1 shard_map.77
  3.0 6.4 %collective-permute-start.4 = (bf16[1536,128]{1,0:T(8,128)(2,1)S(1)}, bf16[1536,128]{1,0:T(8,128)(2,1)S(1)}, u32[]{:S(2)}, u32[]{:S(2)}) collective-permute-start(bf16[1536,128]{1,0:T(8,128)(2,1)S(1)} %bitcast.37), channel_id=1, source_target_pairs={{0,224},{8,232},{16,240},{24,248},{32,0},{40,8},{48,16},{56,24},{6... | collective-permute-start | bytes 1179656 | tf_op jit(solution)/shard_map/ppermute | solution.py:30
  9.4 1.3 collective-permute-start
  10.7 1.4 collective-permute-start.1
  12.2 5.0 %collective-permute-done.4.refs_4_.refs_6_ = bf16[1536,128]{1,0:T(8,128)(2,1)S(1)} collective-permute-done((bf16[1536,128]{1,0:T(8,128)(2,1)S(1)}, bf16[1536,128]{1,0:T(8,128)(2,1)S(1)}, u32[]{:S(2)}, u32[]{:S(2)}) %collective-permute-start.4) | collective-permute-done | bytes 393248 | tf_op jit(solution)/shard_map/ppermute | solution.py:30
  17.2 3.4 %collective-permute-start.5 = (bf16[1536,128]{1,0:T(8,128)(2,1)S(1)}, bf16[1536,128]{1,0:T(8,128)(2,1)}, u32[]{:S(2)}, u32[]{:S(2)}) collective-permute-start(bf16[1536,128]{1,0:T(8,128)(2,1)S(1)} %collective-permute-done.4.refs_4_.refs_6_), channel_id=1, source_target_pairs={{0,224},{8,232},{16,240},{24,248},{32,0},{40,8},{48,16},{56,24},{6... | collective-permute-start | bytes 1179656 | tf_op jit(solution)/shard_map/ppermute | solution.py:30
  20.7 4.1 %collective-permute-done.left_ref.refs_1_ = bf16[2,2,48,1536]{3,2,1,0:T(8,128)(2,1)S(1)} collective-permute-done((bf16[2,2,48,1536]{3,2,1,0:T(8,128)(2,1)}, bf16[2,2,48,1536]{3,2,1,0:T(8,128)(2,1)S(1)}, u32[]{:S(2)}, u32[]{:S(2)}) %collective-permute-start) | collective-permute-done | bytes 589856 | tf_op jit(solution)/shard_map/ppermute | solution.py:36
  24.8 2.8 %shard_map.78 = (bf16[4,2,48,1536]{3,2,1,0:T(8,128)(2,1)}, bf16[4,2,48,1536]{3,2,1,0:T(8,128)(2,1)}) custom-call(bf16[2,2,48,1536]{3,2,1,0:T(8,128)(2,1)} %get-tuple-element.42.low_ref, bf16[2,2,48,1536]{3,2,1,0:T(8,128)(2,1)} %get-tuple-element.43.high_ref, bf16[2,2,48,1536]{3,2,1,0:T(8,128)(2,1)S(1)} %collective-permute-done.left_ref.refs_1_, ...), custom_call_target="tpu_custom_call" | custom-call | flops 1 | bytes 1 | tf_op jit(solution)/shard_map/pallas_call | solution.py:91
  27.6 3.3 %collective-permute-done.8.refs_7_.refs_9_ = bf16[1536,128]{1,0:T(8,128)(2,1)} collective-permute-done((bf16[1536,128]{1,0:T(8,128)(2,1)}, bf16[1536,128]{1,0:T(8,128)(2,1)}, u32[]{:S(2)}, u32[]{:S(2)}) %collective-permute-start.8) | collective-permute-done | bytes 393248 | tf_op jit(solution)/shard_map/ppermute | solution.py:30
  30.9 3.3 %shard_map.79 = (f32[4,48,1280]{2,1,0:T(8,128)S(1)}, f32[4,48,1280]{2,1,0:T(8,128)S(1)}) custom-call(s32[2]{0:T(128)S(1)} %pad_add_fusion.2.at_ref, bf16[4,2,48,1536]{3,2,1,0:T(8,128)(2,1)S(1)} %bitcast.35, bf16[2,2,48,1536]{3,2,1,0:T(8,128)(2,1)S(1)} %collective-permute-done.left_ref.refs_1_, ...), custom_call_target="tpu_custom_call" | custom-call | flops 1 | bytes 1 | tf_op jit(solution)/shard_map/pallas_call | solution.py:168
  34.3 2.8 %collective-permute-start.10 = (f32[4,48,1280]{2,1,0:T(8,128)S(1)}, f32[4,48,1280]{2,1,0:T(8,128)S(1)}, u32[]{:S(2)}, u32[]{:S(2)}) collective-permute-start(f32[4,48,1280]{2,1,0:T(8,128)S(1)} %get-tuple-element.51), channel_id=1, source_target_pairs={{0,1},{1,0},{2,3},{3,2},{4,5},{5,4},{6,7},{7,6},{8,9},{9,8},{10,11... | collective-permute-start | bytes 2949128 | tf_op jit(solution)/shard_map/ppermute | solution.py:53
  37.1 1.3 collective-permute-start.2
  38.4 1.4 collective-permute-start.3
  39.8 1.5 collective-permute-start.9
  41.3 1.9 %shard_map.80 = s16[4,48,1408]{2,1,0:T(8,128)(2,1)} custom-call(f32[4,48,1280]{2,1,0:T(8,128)S(1)} %get-tuple-element.50.keep_ref, f32[4,48,1280]{2,1,0:T(8,128)S(1)} %collective-permute-done.10.recv_ref), custom_call_target="tpu_custom_call" | custom-call | flops 1 | bytes 1 | tf_op jit(solution)/shard_map/pallas_call | solution.py:119
  43.2 7.0 %collective-permute-done.6.refs_10_ = bf16[1536,128]{1,0:T(8,128)(2,1)} collective-permute-done((bf16[1536,128]{1,0:T(8,128)(2,1)}, bf16[1536,128]{1,0:T(8,128)(2,1)}, u32[]{:S(2)}, u32[]{:S(2)}) %collective-permute-start.6) | collective-permute-done | bytes 393248 | tf_op jit(solution)/shard_map/ppermute | solution.py:30
  50.2 1.1 collective-permute-done.9.refs_11_
  51.4 4.0 %all-to-all-start = ((s16[4,48,1408]{2,1,0:T(8,128)(2,1)}), s16[4,48,1408]{2,1,0:T(8,128)(2,1)S(1)}, u32[]{:S(2)}, u32[]{:S(2)}) async-start(s16[4,48,1408]{2,1,0:T(8,128)(2,1)} %shard_map.80), calls=%async_computation | async-start | bytes 1081344 | tf_op jit(solution)/shard_map/all_to_all | solution.py:358
  55.4 1.6 %slice.42 = bf16[768,128]{1,0:T(8,128)(2,1)} slice(bf16[1536,128]{1,0:T(8,128)(2,1)} %collective-permute-done.6.refs_10_), slice={[0:768], [0:128]} | slice | bytes 393216 | tf_op jit(solution)/shard_map/slice | solution.py:370
  57.3 1.7 %slice.43 = bf16[768,128]{1,0:T(8,128)(2,1)} slice(bf16[1536,128]{1,0:T(8,128)(2,1)} %collective-permute-done.9.refs_11_), slice={[768:1536], [0:128]} | slice | bytes 393216 | tf_op jit(solution)/shard_map/slice | solution.py:370
  59.0 1.1 collective-permute-start.13
  60.2 6.1 %collective-permute-done.2.refs_3_ = bf16[4,2,48,1536]{3,2,1,0:T(8,128)(2,1)} collective-permute-done((bf16[4,2,48,1536]{3,2,1,0:T(8,128)(2,1)}, bf16[4,2,48,1536]{3,2,1,0:T(8,128)(2,1)}, u32[]{:S(2)}, u32[]{:S(2)}) %collective-permute-start.2) | collective-permute-done | bytes 1179680 | tf_op jit(solution)/shard_map/ppermute | solution.py:36
  66.3 1.0 copy-done.6
  67.3 8.3 %shard_map.82 = (f32[4,48,2816]{2,1,0:T(8,128)}, f32[4,48,2816]{2,1,0:T(8,128)S(1)}, bf16[192,1024]{1,0:T(8,128)(2,1)S(1)}) custom-call(s32[2]{0:T(128)S(1)} %pad_add_fusion.2.at_ref, bf16[4,2,48,1536]{3,2,1,0:T(8,128)(2,1)S(1)} %bitcast.36, bf16[2,2,48,1536]{3,2,1,0:T(8,128)(2,1)S(1)} %collective-permute-done.left_ref.refs_1_, ...), custom_call_target="tpu_custom_call" | custom-call | flops 1 | bytes 1 | tf_op jit(solution)/shard_map/pallas_call | solution.py:168
  75.6 1.4 copy-done.2
  77.0 0.7 copy-done.7
  77.7 1.7 %collective-permute-start.14 = (f32[4,48,2816]{2,1,0:T(8,128)}, f32[4,48,2816]{2,1,0:T(8,128)S(1)}, u32[]{:S(2)}, u32[]{:S(2)}) collective-permute-start(f32[4,48,2816]{2,1,0:T(8,128)} %get-tuple-element.64), channel_id=1, source_target_pairs={{0,1},{1,0},{2,3},{3,2},{4,5},{5,4},{6,7},{7,6},{8,9},{9,8},{10,11... | collective-permute-start | bytes 6488072 | tf_op jit(solution)/shard_map/ppermute | solution.py:53
  79.8 3.7 %collective-permute-done.14.recv_ref = f32[4,48,2816]{2,1,0:T(8,128)S(1)} collective-permute-done((f32[4,48,2816]{2,1,0:T(8,128)}, f32[4,48,2816]{2,1,0:T(8,128)S(1)}, u32[]{:S(2)}, u32[]{:S(2)}) %collective-permute-start.14) | collective-permute-done | bytes 2162720 | tf_op jit(solution)/shard_map/ppermute | solution.py:53
  83.5 1.6 %copy-done.3 = f32[4,48,2816]{2,1,0:T(8,128)S(1)} copy-done((f32[4,48,2816]{2,1,0:T(8,128)S(1)}, f32[4,48,2816]{2,1,0:T(8,128)}, u32[]{:S(2)}) %copy-start.3) | copy-done | bytes 2162712
  85.1 2.5 %shard_map.83 = s16[4,48,2944]{2,1,0:T(8,128)(2,1)} custom-call(f32[4,48,2816]{2,1,0:T(8,128)S(1)} %copy-done.3, f32[4,48,2816]{2,1,0:T(8,128)S(1)} %collective-permute-done.14.recv_ref), custom_call_target="tpu_custom_call" | custom-call | flops 1 | bytes 1 | tf_op jit(solution)/shard_map/pallas_call | solution.py:119
  87.6 4.6 %all-to-all-start.1 = ((s16[4,48,2944]{2,1,0:T(8,128)(2,1)}), s16[4,48,2944]{2,1,0:T(8,128)(2,1)S(1)}, u32[]{:S(2)}, u32[]{:S(2)}) async-start(s16[4,48,2944]{2,1,0:T(8,128)(2,1)} %shard_map.83), calls=%async_computation.1 | async-start | bytes 2260992 | tf_op jit(solution)/shard_map/all_to_all | solution.py:358
  92.9 2.6 %collective-permute-start.16 = (bf16[192,1024]{1,0:T(8,128)(2,1)S(1)}, bf16[192,1024]{1,0:T(8,128)(2,1)S(1)}, u32[]{:S(2)}, u32[]{:S(2)}) collective-permute-start(bf16[192,1024]{1,0:T(8,128)(2,1)S(1)} %copy-done.8), channel_id=1, source_target_pairs={{0,16},{8,24},{16,0},{24,8},{32,48},{40,56},{48,32},{56,40},{64,80... | collective-permute-start | bytes 1179656 | tf_op jit(solution)/shard_map/ppermute | solution.py:36
  95.5 1.1 collective-permute-start.17
  97.2 1.0 shard_map.81
  98.3 5.8 %collective-permute-done.15.refs_3_.refs_1_ = bf16[192,1024]{1,0:T(8,128)(2,1)S(1)} collective-permute-done((bf16[192,1024]{1,0:T(8,128)(2,1)S(1)}, bf16[192,1024]{1,0:T(8,128)(2,1)S(1)}, u32[]{:S(2)}, u32[]{:S(2)}) %collective-permute-start.15) | collective-permute-done | bytes 393248 | tf_op jit(solution)/shard_map/ppermute | solution.py:36
  104.1 8.4 %collective-permute-done.16.refs_4_.refs_2_ = bf16[192,1024]{1,0:T(8,128)(2,1)S(1)} collective-permute-done((bf16[192,1024]{1,0:T(8,128)(2,1)S(1)}, bf16[192,1024]{1,0:T(8,128)(2,1)S(1)}, u32[]{:S(2)}, u32[]{:S(2)}) %collective-permute-start.16) | collective-permute-done | bytes 393248 | tf_op jit(solution)/shard_map/ppermute | solution.py:36
  113.1 1.6 %shard_map.84.bmat_in_ref = f32[1,128]{1,0:T(1,128)S(1)} custom-call(s32[4]{0:T(128)S(1)} %get-tuple-element.78.at_ref, f32[256,128]{1,0:T(8,128)S(1)} %fusion.weight_ref, bf16[48,640]{1,0:T(8,128)(2,1)S(1)} %get-tuple-element.71.refs_0_, bf16[48,640]{1,0:T(8,128)(2,1)S(1)} %get-tuple-element.55.refs_1_, bf16[192,1024]{1,0:T(8,128)(2,1)S(1)} %copy-done.8, ...), custom_call_target="tpu_custom_call" | custom-call | flops 1 | bytes 1 | tf_op jit(solution)/shard_map/pallas_call | solution.py:259
  114.7 3.3 %shard_map.85 = (bf16[48,384]{1,0:T(8,128)(2,1)S(1)}, bf16[48,384]{1,0:T(8,128)(2,1)S(1)}, bf16[48,1024]{1,0:T(8,128)(2,1)S(1)}, bf16[48,1024]{1,0:T(8,128)(2,1)S(1)}, f32[1,128]{1,0:T(1,128)S(1)}) custom-call(s32[4]{0:T(128)S(1)} %get-tuple-element.78.at_ref, s16[4,48,2944]{2,1,0:T(8,128)(2,1)S(1)} %all-to-all-done.1.total_ref, f32[1,1024]{1,0:T(1,128)S(1)} %bitcast.42, ...), custom_call_target="tpu_custom_call" | custom-call | flops 1 | bytes 1 | tf_op jit(solution)/shard_map/pallas_call | solution.py:272
  118.1 3.5 %collective-permute-start.18 = (bf16[48,384]{1,0:T(8,128)(2,1)S(1)}, bf16[48,384]{1,0:T(8,128)(2,1)S(1)}, u32[]{:S(2)}, u32[]{:S(2)}) collective-permute-start(bf16[48,384]{1,0:T(8,128)(2,1)S(1)} %get-tuple-element.67), channel_id=1, source_target_pairs={{0,24},{1,25},{2,26},{3,27},{4,12},{5,13},{6,14},{7,15},{8,0},{9,1... | collective-permute-start | bytes 110600 | tf_op jit(solution)/shard_map/ppermute | solution.py:49
  121.5 1.3 collective-permute-start.20
  122.8 0.6 broadcast_in_dim.7
  123.4 4.9 %all-to-all-start.2 = ((f32[32,1,128]{2,1,0:T(1,128)}), f32[32,1,128]{2,1,0:T(1,128)S(1)}, u32[]{:S(2)}, u32[]{:S(2)}) async-start(f32[32,1,128]{2,1,0:T(1,128)} %broadcast_in_dim.7), calls=%async_computation.2 | async-start | bytes 32768 | tf_op jit(solution)/shard_map/all_to_all | solution.py:60
  128.3 8.5 %all-to-all-done.2 = f32[32,1,128]{2,1,0:T(1,128)S(1)} async-done(((f32[32,1,128]{2,1,0:T(1,128)}), f32[32,1,128]{2,1,0:T(1,128)S(1)}, u32[]{:S(2)}, u32[]{:S(2)}) %all-to-all-start.2) | async-done | bytes 16416 | tf_op jit(solution)/shard_map/all_to_all | solution.py:60
  137.5 7.5 %all-to-all-start.3 = ((f32[8,1,128]{2,1,0:T(1,128)}), f32[8,1,128]{2,1,0:T(1,128)S(1)}, u32[]{:S(2)}, u32[]{:S(2)}) async-start(f32[8,1,128]{2,1,0:T(1,128)} %broadcast_in_dim.8), calls=%async_computation.3 | async-start | bytes 8192 | tf_op jit(solution)/shard_map/all_to_all | solution.py:60
  145.0 1.4 shard_map.86
  146.4 3.1 %all-to-all-done.3 = f32[8,1,128]{2,1,0:T(1,128)S(1)} async-done(((f32[8,1,128]{2,1,0:T(1,128)}), f32[8,1,128]{2,1,0:T(1,128)S(1)}, u32[]{:S(2)}, u32[]{:S(2)}) %all-to-all-start.3) | async-done | bytes 4128 | tf_op jit(solution)/shard_map/all_to_all | solution.py:60
  149.6 0.6 reshape_squeeze.3
  (73 shorter events, 3.5 us)
Async XLA Ops:
  0.6 1.3 copy-start
  1.9 1.1 copy-start.4
  3.0 14.2 %collective-permute-start.4 = (bf16[1536,128]{1,0:T(8,128)(2,1)S(1)}, bf16[1536,128]{1,0:T(8,128)(2,1)S(1)}, u32[]{:S(2)}, u32[]{:S(2)}) collective-permute-start(bf16[1536,128]{1,0:T(8,128)(2,1)S(1)} %bitcast.37), channel_id=1, source_target_pairs={{0,224},{8,232},{16,240},{24,248},{32,0},{40,8},{48,16},{56,24},{6... | collective-permute-start | bytes 1179656 | tf_op jit(solution)/shard_map/ppermute | solution.py:30
  9.4 11.2 %collective-permute-start.7 = (bf16[1536,128]{1,0:T(8,128)(2,1)S(1)}, bf16[1536,128]{1,0:T(8,128)(2,1)}, u32[]{:S(2)}, u32[]{:S(2)}) collective-permute-start(bf16[1536,128]{1,0:T(8,128)(2,1)S(1)} %bitcast.38), channel_id=1, source_target_pairs={{0,32},{8,40},{16,48},{24,56},{32,64},{40,72},{48,80},{56,88},{64,... | collective-permute-start | bytes 1179656 | tf_op jit(solution)/shard_map/ppermute | solution.py:30
  9.4 15.4 %collective-permute-start = (bf16[2,2,48,1536]{3,2,1,0:T(8,128)(2,1)}, bf16[2,2,48,1536]{3,2,1,0:T(8,128)(2,1)S(1)}, u32[]{:S(2)}, u32[]{:S(2)}) collective-permute-start(bf16[2,2,48,1536]{3,2,1,0:T(8,128)(2,1)} %get-tuple-element.42.low_ref), channel_id=1, source_target_pairs={{0,8},{8,16},{16,24},{24,0},{32,40},{40,48},{48,56},{56,32},{64,72... | collective-permute-start | bytes 1769480 | tf_op jit(solution)/shard_map/ppermute | solution.py:36
  10.7 14.1 %collective-permute-start.1 = (bf16[2,2,48,1536]{3,2,1,0:T(8,128)(2,1)}, bf16[2,2,48,1536]{3,2,1,0:T(8,128)(2,1)S(1)}, u32[]{:S(2)}, u32[]{:S(2)}) collective-permute-start(bf16[2,2,48,1536]{3,2,1,0:T(8,128)(2,1)} %get-tuple-element.43.high_ref), channel_id=1, source_target_pairs={{0,24},{8,0},{16,8},{24,16},{32,56},{40,32},{48,40},{56,48},{64,88... | collective-permute-start | bytes 1769480 | tf_op jit(solution)/shard_map/ppermute | solution.py:36
  17.2 13.7 %copy-start.5 = (bf16[1536,128]{1,0:T(8,128)(2,1)}, bf16[1536,128]{1,0:T(8,128)(2,1)S(1)}, u32[]{:S(2)}) copy-start(bf16[1536,128]{1,0:T(8,128)(2,1)S(1)} %collective-permute-done.4.refs_4_.refs_6_) | copy-start | bytes 1179652
  17.2 10.4 %collective-permute-start.5 = (bf16[1536,128]{1,0:T(8,128)(2,1)S(1)}, bf16[1536,128]{1,0:T(8,128)(2,1)}, u32[]{:S(2)}, u32[]{:S(2)}) collective-permute-start(bf16[1536,128]{1,0:T(8,128)(2,1)S(1)} %collective-permute-done.4.refs_4_.refs_6_), channel_id=1, source_target_pairs={{0,224},{8,232},{16,240},{24,248},{32,0},{40,8},{48,16},{56,24},{6... | collective-permute-start | bytes 1179656 | tf_op jit(solution)/shard_map/ppermute | solution.py:30
  20.6 10.3 %collective-permute-start.8 = (bf16[1536,128]{1,0:T(8,128)(2,1)}, bf16[1536,128]{1,0:T(8,128)(2,1)}, u32[]{:S(2)}, u32[]{:S(2)}) collective-permute-start(bf16[1536,128]{1,0:T(8,128)(2,1)} %collective-permute-done.7.refs_5_.refs_7_), channel_id=1, source_target_pairs={{0,32},{8,40},{16,48},{24,56},{32,64},{40,72},{48,80},{56,88},{64,... | collective-permute-start | bytes 1179656 | tf_op jit(solution)/shard_map/ppermute | solution.py:30
  20.7 10.2 %copy-start.1 = (bf16[8,1,48,1536]{3,2,1,0:T(8,128)(2,1)S(1)}, bf16[8,1,48,1536]{3,2,1,0:T(8,128)(2,1)}, u32[]{:S(2)}) copy-start(bf16[8,1,48,1536]{3,2,1,0:T(8,128)(2,1)} %param.7) | copy-start | bytes 3538948
  34.3 7.0 %collective-permute-start.10 = (f32[4,48,1280]{2,1,0:T(8,128)S(1)}, f32[4,48,1280]{2,1,0:T(8,128)S(1)}, u32[]{:S(2)}, u32[]{:S(2)}) collective-permute-start(f32[4,48,1280]{2,1,0:T(8,128)S(1)} %get-tuple-element.51), channel_id=1, source_target_pairs={{0,1},{1,0},{2,3},{3,2},{4,5},{5,4},{6,7},{7,6},{8,9},{9,8},{10,11... | collective-permute-start | bytes 2949128 | tf_op jit(solution)/shard_map/ppermute | solution.py:53
  37.1 29.2 %collective-permute-start.2 = (bf16[4,2,48,1536]{3,2,1,0:T(8,128)(2,1)}, bf16[4,2,48,1536]{3,2,1,0:T(8,128)(2,1)}, u32[]{:S(2)}, u32[]{:S(2)}) collective-permute-start(bf16[4,2,48,1536]{3,2,1,0:T(8,128)(2,1)} %get-tuple-element.44), channel_id=1, source_target_pairs={{0,8},{8,16},{16,24},{24,0},{32,40},{40,48},{48,56},{56,32},{64,72... | collective-permute-start | bytes 3538952 | tf_op jit(solution)/shard_map/ppermute | solution.py:36
  38.4 27.8 %collective-permute-start.3 = (bf16[4,2,48,1536]{3,2,1,0:T(8,128)(2,1)}, bf16[4,2,48,1536]{3,2,1,0:T(8,128)(2,1)}, u32[]{:S(2)}, u32[]{:S(2)}) collective-permute-start(bf16[4,2,48,1536]{3,2,1,0:T(8,128)(2,1)} %get-tuple-element.45), channel_id=1, source_target_pairs={{0,24},{8,0},{16,8},{24,16},{32,56},{40,32},{48,40},{56,48},{64,88... | collective-permute-start | bytes 3538952 | tf_op jit(solution)/shard_map/ppermute | solution.py:36
  39.8 10.4 %collective-permute-start.6 = (bf16[1536,128]{1,0:T(8,128)(2,1)}, bf16[1536,128]{1,0:T(8,128)(2,1)}, u32[]{:S(2)}, u32[]{:S(2)}) collective-permute-start(bf16[1536,128]{1,0:T(8,128)(2,1)} %collective-permute-done.5.refs_6_.refs_8_), channel_id=1, source_target_pairs={{0,224},{8,232},{16,240},{24,248},{32,0},{40,8},{48,16},{56,24},{6... | collective-permute-start | bytes 1179656 | tf_op jit(solution)/shard_map/ppermute | solution.py:30
  39.8 11.5 %collective-permute-start.9 = (bf16[1536,128]{1,0:T(8,128)(2,1)}, bf16[1536,128]{1,0:T(8,128)(2,1)}, u32[]{:S(2)}, u32[]{:S(2)}) collective-permute-start(bf16[1536,128]{1,0:T(8,128)(2,1)} %collective-permute-done.8.refs_7_.refs_9_), channel_id=1, source_target_pairs={{0,32},{8,40},{16,48},{24,56},{32,64},{40,72},{48,80},{56,88},{64,... | collective-permute-start | bytes 1179656 | tf_op jit(solution)/shard_map/ppermute | solution.py:30
  51.4 14.9 %all-to-all-start = ((s16[4,48,1408]{2,1,0:T(8,128)(2,1)}), s16[4,48,1408]{2,1,0:T(8,128)(2,1)S(1)}, u32[]{:S(2)}, u32[]{:S(2)}) async-start(s16[4,48,1408]{2,1,0:T(8,128)(2,1)} %shard_map.80), calls=%async_computation | async-start | bytes 1081344 | tf_op jit(solution)/shard_map/all_to_all | solution.py:358
  57.0 9.3 %collective-permute-start.12 = (bf16[768,128]{1,0:T(8,128)(2,1)}, bf16[768,128]{1,0:T(8,128)(2,1)S(1)}, u32[]{:S(2)}, u32[]{:S(2)}) collective-permute-start(bf16[768,128]{1,0:T(8,128)(2,1)} %slice.42), channel_id=1, source_target_pairs={{0,224},{8,232},{16,240},{24,248},{32,0},{40,8},{48,16},{56,24},{6... | collective-permute-start | bytes 589832 | tf_op jit(solution)/shard_map/ppermute | solution.py:30
  57.3 22.1 %copy-start.12 = (s32[8]{0:T(128)S(1)}, s32[8]{0:T(128)}, u32[]{:S(2)}) copy-start(s32[8]{0:T(128)} %constant.100.clone) | copy-start | bytes 100
  57.3 22.3 %copy-start.9 = (s32[32]{0:T(128)S(1)}, s32[32]{0:T(128)}, u32[]{:S(2)}) copy-start(s32[32]{0:T(128)} %param.8) | copy-start | bytes 388
  57.3 22.3 %copy-start.10 = (s32[32]{0:T(128)S(1)}, s32[32]{0:T(128)}, u32[]{:S(2)}) copy-start(s32[32]{0:T(128)} %param.9) | copy-start | bytes 388
  57.3 22.3 %copy-start.11 = (s32[32]{0:T(128)S(1)}, s32[32]{0:T(128)}, u32[]{:S(2)}) copy-start(s32[32]{0:T(128)} %param.10) | copy-start | bytes 388
  59.0 7.2 %collective-permute-start.13 = (bf16[768,128]{1,0:T(8,128)(2,1)}, bf16[768,128]{1,0:T(8,128)(2,1)}, u32[]{:S(2)}, u32[]{:S(2)}) collective-permute-start(bf16[768,128]{1,0:T(8,128)(2,1)} %slice.43), channel_id=1, source_target_pairs={{0,32},{8,40},{16,48},{24,56},{32,64},{40,72},{48,80},{56,88},{64,... | collective-permute-start | bytes 589832 | tf_op jit(solution)/shard_map/ppermute | solution.py:30
  66.3 1.0 copy-start.6
  75.6 1.4 copy-start.2
  77.0 0.7 copy-start.7
  77.7 5.8 %collective-permute-start.14 = (f32[4,48,2816]{2,1,0:T(8,128)}, f32[4,48,2816]{2,1,0:T(8,128)S(1)}, u32[]{:S(2)}, u32[]{:S(2)}) collective-permute-start(f32[4,48,2816]{2,1,0:T(8,128)} %get-tuple-element.64), channel_id=1, source_target_pairs={{0,1},{1,0},{2,3},{3,2},{4,5},{5,4},{6,7},{7,6},{8,9},{9,8},{10,11... | collective-permute-start | bytes 6488072 | tf_op jit(solution)/shard_map/ppermute | solution.py:53
  83.5 1.6 %copy-start.3 = (f32[4,48,2816]{2,1,0:T(8,128)S(1)}, f32[4,48,2816]{2,1,0:T(8,128)}, u32[]{:S(2)}) copy-start(f32[4,48,2816]{2,1,0:T(8,128)} %copy-done.2) | copy-start | bytes 6488068
  87.6 5.2 %copy-start.8 = (bf16[192,1024]{1,0:T(8,128)(2,1)S(1)}, bf16[192,1024]{1,0:T(8,128)(2,1)}, u32[]{:S(2)}) copy-start(bf16[192,1024]{1,0:T(8,128)(2,1)} %copy-done.7) | copy-start | bytes 1179652
  87.6 27.1 %all-to-all-start.1 = ((s16[4,48,2944]{2,1,0:T(8,128)(2,1)}), s16[4,48,2944]{2,1,0:T(8,128)(2,1)S(1)}, u32[]{:S(2)}, u32[]{:S(2)}) async-start(s16[4,48,2944]{2,1,0:T(8,128)(2,1)} %shard_map.83), calls=%async_computation.1 | async-start | bytes 2260992 | tf_op jit(solution)/shard_map/all_to_all | solution.py:358
  92.8 11.3 %collective-permute-start.15 = (bf16[192,1024]{1,0:T(8,128)(2,1)S(1)}, bf16[192,1024]{1,0:T(8,128)(2,1)S(1)}, u32[]{:S(2)}, u32[]{:S(2)}) collective-permute-start(bf16[192,1024]{1,0:T(8,128)(2,1)S(1)} %copy-done.8), channel_id=1, source_target_pairs={{0,8},{8,16},{16,24},{24,0},{32,40},{40,48},{48,56},{56,32},{64,72... | collective-permute-start | bytes 1179656 | tf_op jit(solution)/shard_map/ppermute | solution.py:36
  92.9 19.6 %collective-permute-start.16 = (bf16[192,1024]{1,0:T(8,128)(2,1)S(1)}, bf16[192,1024]{1,0:T(8,128)(2,1)S(1)}, u32[]{:S(2)}, u32[]{:S(2)}) collective-permute-start(bf16[192,1024]{1,0:T(8,128)(2,1)S(1)} %copy-done.8), channel_id=1, source_target_pairs={{0,16},{8,24},{16,0},{24,8},{32,48},{40,56},{48,32},{56,40},{64,80... | collective-permute-start | bytes 1179656 | tf_op jit(solution)/shard_map/ppermute | solution.py:36
  95.5 17.6 %collective-permute-start.17 = (bf16[192,1024]{1,0:T(8,128)(2,1)S(1)}, bf16[192,1024]{1,0:T(8,128)(2,1)S(1)}, u32[]{:S(2)}, u32[]{:S(2)}) collective-permute-start(bf16[192,1024]{1,0:T(8,128)(2,1)S(1)} %copy-done.8), channel_id=1, source_target_pairs={{0,24},{8,0},{16,8},{24,16},{32,56},{40,32},{48,40},{56,48},{64,88... | collective-permute-start | bytes 1179656 | tf_op jit(solution)/shard_map/ppermute | solution.py:36
  98.2 38.6 %collective-permute-start.11 = (bf16[48,640]{1,0:T(8,128)(2,1)S(1)}, bf16[48,640]{1,0:T(8,128)(2,1)S(1)}, u32[]{:S(2)}, u32[]{:S(2)}) collective-permute-start(bf16[48,640]{1,0:T(8,128)(2,1)S(1)} %get-tuple-element.55.refs_1_), channel_id=1, source_target_pairs={{0,24},{1,25},{2,26},{3,27},{4,12},{5,13},{6,14},{7,15},{8,0},{9,1... | collective-permute-start | bytes 184328 | tf_op jit(solution)/shard_map/ppermute | solution.py:49
  118.1 18.8 %collective-permute-start.18 = (bf16[48,384]{1,0:T(8,128)(2,1)S(1)}, bf16[48,384]{1,0:T(8,128)(2,1)S(1)}, u32[]{:S(2)}, u32[]{:S(2)}) collective-permute-start(bf16[48,384]{1,0:T(8,128)(2,1)S(1)} %get-tuple-element.67), channel_id=1, source_target_pairs={{0,24},{1,25},{2,26},{3,27},{4,12},{5,13},{6,14},{7,15},{8,0},{9,1... | collective-permute-start | bytes 110600 | tf_op jit(solution)/shard_map/ppermute | solution.py:49
  121.5 15.3 %collective-permute-start.19 = (bf16[48,1024]{1,0:T(8,128)(2,1)S(1)}, bf16[48,1024]{1,0:T(8,128)(2,1)S(1)}, u32[]{:S(2)}, u32[]{:S(2)}) collective-permute-start(bf16[48,1024]{1,0:T(8,128)(2,1)S(1)} %get-tuple-element.68), channel_id=1, source_target_pairs={{0,8},{1,9},{2,10},{3,11},{4,28},{5,29},{6,30},{7,31},{8,16},{9,17... | collective-permute-start | bytes 294920 | tf_op jit(solution)/shard_map/ppermute | solution.py:49
  121.5 15.3 %collective-permute-start.20 = (bf16[48,1024]{1,0:T(8,128)(2,1)S(1)}, bf16[48,1024]{1,0:T(8,128)(2,1)S(1)}, u32[]{:S(2)}, u32[]{:S(2)}) collective-permute-start(bf16[48,1024]{1,0:T(8,128)(2,1)S(1)} %get-tuple-element.69), channel_id=1, source_target_pairs={{0,16},{1,17},{2,18},{3,19},{4,20},{5,21},{6,22},{7,23},{8,24},{9,... | collective-permute-start | bytes 294920 | tf_op jit(solution)/shard_map/ppermute | solution.py:49
  123.4 13.4 %all-to-all-start.2 = ((f32[32,1,128]{2,1,0:T(1,128)}), f32[32,1,128]{2,1,0:T(1,128)S(1)}, u32[]{:S(2)}, u32[]{:S(2)}) async-start(f32[32,1,128]{2,1,0:T(1,128)} %broadcast_in_dim.7), calls=%async_computation.2 | async-start | bytes 32768 | tf_op jit(solution)/shard_map/all_to_all | solution.py:60
  137.5 12.0 %all-to-all-start.3 = ((f32[8,1,128]{2,1,0:T(1,128)}), f32[8,1,128]{2,1,0:T(1,128)S(1)}, u32[]{:S(2)}, u32[]{:S(2)}) async-start(f32[8,1,128]{2,1,0:T(1,128)} %broadcast_in_dim.8), calls=%async_computation.3 | async-start | bytes 8192 | tf_op jit(solution)/shard_map/all_to_all | solution.py:60

commit v2 on v0

v2 whole, which is shorter than its diff:
```python
import functools

import jax
import jax.numpy as jnp
from jax import lax
from jax.experimental import pallas as pl
from jax.experimental.pallas import tpu as pltpu
from jax.sharding import Mesh
from jax.sharding import PartitionSpec as P

HIGHEST = lax.Precision.HIGHEST
NZ, NY, NX, NC = 8, 4, 4, 2
VMEM = pl.BlockSpec(memory_space=pltpu.VMEM)
SMEM = pl.BlockSpec(memory_space=pltpu.SMEM)
ANY = pl.BlockSpec(memory_space=pl.ANY)
CHEAP = pl.CostEstimate(flops=1, bytes_accessed=1, transcendentals=0)

NEAR, FAR = (0, 1, 7), (2, 6, 3, 5, 4)
ORDER = NEAR + FAR
FIRST = ((0, NEAR), (1, NEAR))
SECOND = ((0, FAR), (1, FAR), (2, ORDER), (3, ORDER))


def offset(j, x):
    return (0, -1, 1, 2)[j] if x < NX // 2 else (0, 1, -1, 2)[j]


def offset_at(j, x):
    near, far = jnp.where(x < NX // 2, NY - 1, 1), jnp.where(x < NX // 2, 1, NY - 1)
    return (0, near, far, 2)[j]


def shift_z(v, s):
    return lax.ppermute(v, "z", [(z, (z + s) % NZ) for z in range(NZ)])


def shift_y(v, s):
    return lax.ppermute(v, "y", [(y, (y + s) % NY) for y in range(NY)])


def to_owner(v, j):
    moves = []
    for y in range(NY):
        for x in range(NX):
            moves.append((y * NX + x, (y + offset(j, x)) % NY * NX + x))
    return lax.ppermute(v, ("y", "x"), moves) if j else v


def swap_core(v):
    return lax.ppermute(v, "c", [(0, 1), (1, 0)])


def total_over(v, axis, n):
    return lax.all_to_all(jnp.broadcast_to(v, (n,) + v.shape), axis, 0, 0).sum(0)


def split_kernel(own_ref, low_ref, high_ref):
    half = own_ref.shape[0] // 2
    low_ref[...] = own_ref[:half]
    high_ref[...] = own_ref[half:]


def split(own):
    half = jax.ShapeDtypeStruct((own.shape[0] // 2,) + own.shape[1:], own.dtype)
    return pl.pallas_call(
        split_kernel,
        out_shape=[half, half],
        in_specs=[VMEM],
        out_specs=[VMEM] * 2,
        compiler_params=pltpu.CompilerParams(vmem_limit_bytes=8 * 2**20),
        cost_estimate=CHEAP,
    )(own)


def join_kernel(low_ref, high_ref, left_ref, right_ref, to_right_ref, to_left_ref):
    half = low_ref.shape[0]
    to_right_ref[:half] = left_ref[...]
    to_right_ref[half:] = high_ref[...]
    to_left_ref[:half] = low_ref[...]
    to_left_ref[half:] = right_ref[...]


def join(low, high, left, right):
    whole = jax.ShapeDtypeStruct((2 * low.shape[0],) + low.shape[1:], low.dtype)
    return pl.pallas_call(
        join_kernel,
        out_shape=[whole, whole],
        in_specs=[VMEM] * 4,
        out_specs=[VMEM] * 2,
        compiler_params=pltpu.CompilerParams(vmem_limit_bytes=12 * 2**20),
        cost_estimate=CHEAP,
    )(low, high, left, right)


def pack_kernel(keep_ref, recv_ref, *refs):
    *before_ref, out_ref = refs
    _, width, total = keep_ref.shape
    columns = 128
    lane = lax.broadcasted_iota(jnp.int32, (width, columns), 1)
    at = 0
    exponents = jnp.zeros((width, columns), jnp.int32)
    for ref in before_ref:
        at = ref.shape[2] - columns
        out_ref[0, :, :at] = ref[0, :, :at]
        exponents = ref[0, :, at:].astype(jnp.int32)
    for u in range(total // columns):
        span = slice(u * columns, (u + 1) * columns)
        value = keep_ref[0, :, span] + recv_ref[0, :, span]
        top = jnp.maximum(jnp.max(jnp.abs(value), axis=1, keepdims=True), 2.0**-100)
        power = jnp.ceil(jnp.log2(top)) - 15.0
        scaled = jnp.clip(jnp.round(value * jnp.exp2(-power)), -32767.0, 32767.0)
        out_ref[0, :, at + u * columns : at + (u + 1) * columns] = scaled.astype(jnp.int32).astype(jnp.int16)
        exponents = jnp.where(lane == at // columns + u, power.astype(jnp.int32), exponents)
    out_ref[0, :, at + total :] = exponents.astype(jnp.int16)


def pack(keep, recv, before=()):
    n, width, total = keep.shape
    columns = total + (before[0].shape[2] if before else 128)

    def spec(v):
        return pl.BlockSpec((1,) + v.shape[1:], lambda t: (t, 0, 0))

    out = jax.ShapeDtypeStruct((n, width, columns), jnp.int16)
    return pl.pallas_call(
        pack_kernel,
        out_shape=out,
        grid=(n,),
        in_specs=[spec(v) for v in (keep, recv, *before)],
        out_specs=spec(out),
        compiler_params=pltpu.CompilerParams(vmem_limit_bytes=8 * 2**20),
        cost_estimate=CHEAP,
    )(keep, recv, *before)


def products_kernel(plan, n_f, n_g, at_ref, *refs):
    f_refs, g_refs = refs[:n_f], refs[n_f : n_f + n_g]
    away_ref, keep_ref, joined = refs[n_f + n_g :]
    columns = g_refs[0].shape[1]
    first_core = at_ref[0] == 0
    for j, ref in enumerate(g_refs):
        joined[:, j * columns : (j + 1) * columns] = ref[...]
    at = 0
    for pieces, lo, hi in plan:
        span = (hi - lo) * columns
        parts = []
        for i, part in pieces:
            n, cores, width, depth = f_refs[i].shape
            value = f_refs[i][...] if part is None else f_refs[i][part * (n // 2) : (part + 1) * (n // 2)]
            parts.append(value.reshape(-1, depth))
        lhs = parts[0] if len(parts) == 1 else jnp.concatenate(parts, axis=0)
        out = jnp.dot(lhs, joined[:, lo * columns : hi * columns], preferred_element_type=jnp.float32)
        out = out.reshape(NX, NC, width, span)
        keep_ref[:, :, at : at + span] = jnp.where(first_core, out[:, 0], out[:, 1])
        away_ref[:, :, at : at + span] = jnp.where(first_core, out[:, 1], out[:, 0])
        at += span


def products(plan, at, f_arrays, g_pieces):
    width, rows = f_arrays[0].shape[2:]
    columns = g_pieces[0].shape[1]
    units = sum(hi - lo for _, lo, hi in plan)
    terms = jax.ShapeDtypeStruct((NX, width, units * columns), jnp.float32)
    return pl.pallas_call(
        functools.partial(products_kernel, plan, len(f_arrays), len(g_pieces)),
        out_shape=[terms, terms],
        in_specs=[SMEM] + [VMEM] * (len(f_arrays) + len(g_pieces)),
        out_specs=[VMEM] * 2,
        scratch_shapes=[pltpu.VMEM((rows, len(g_pieces) * columns), jnp.bfloat16)],
        compiler_params=pltpu.CompilerParams(vmem_limit_bytes=26 * 2**20),
        cost_estimate=CHEAP,
    )(at, *f_arrays, *g_pieces)


def facts_kernel(normalizer, at_ref, pair_ref, block_ref, live_ref, weight_ref, mask_ref):
    columns = mask_ref.shape[1] // NZ
    lane = lax.broadcasted_iota(jnp.int32, (1, weight_ref.shape[1]), 1)
    z, y = at_ref[1], at_ref[2]
    own = [lax.rem(z + e, NZ) * NY + y for e in range(NZ)]
    own = [own[e] for e in ORDER]
    for i, slot in enumerate(own):
        live = jnp.full((1, columns), live_ref[slot].astype(jnp.float32))
        mask_ref[:, i * columns : (i + 1) * columns] = live
    for k in range(NY - 1):
        for i, f in enumerate(ORDER):
            other = lax.rem(z + f, NZ) * NY + lax.rem(y + k, NY)
            for j, slot in enumerate(own):
                alike = (block_ref[other] == block_ref[slot]).astype(jnp.int32)
                value = (alike * live_ref[other] * live_ref[slot]).astype(jnp.float32) * normalizer
                row = jnp.where(lane == 2 * pair_ref[other] + pair_ref[slot], value, 0.0)
                if k == 1:
                    row = row + jnp.where(lane == 2 * pair_ref[slot] + pair_ref[other], value, 0.0)
                n = (k * NZ + i) * NZ + j
                weight_ref[n : n + 1] = row


def facts(at, pair, block, live, normalizer, columns):
    return pl.pallas_call(
        functools.partial(facts_kernel, normalizer),
        out_shape=[
            jax.ShapeDtypeStruct(((NY - 1) * NZ * NZ, 128), jnp.float32),
            jax.ShapeDtypeStruct((1, NZ * columns), jnp.float32),
        ],
        in_specs=[SMEM] * 4,
        out_specs=[VMEM] * 2,
        compiler_params=pltpu.CompilerParams(vmem_limit_bytes=4 * 2**20),
        cost_estimate=CHEAP,
    )(at, pair, block, live)


def finish_kernel(plan, n_rows, at_ref, total_ref, mask_ref, weight_ref, *refs):
    row_refs, done_refs = refs[:n_rows], refs[n_rows : n_rows + NY]
    bmat_ref, held, arrived, dots = refs[n_rows + NY :]
    n, width, _ = held.shape
    columns = dots.shape[1]
    copies = [pltpu.make_async_copy(total_ref.at[t], held.at[t], arrived.at[t]) for t in range(n)]
    for copy in copies:
        copy.start()
    for copy in copies:
        copy.wait()
    units = held.shape[2] - columns
    scales = [jnp.exp2(held[t, :, units:].astype(jnp.int32).astype(jnp.float32)) for t in range(n)]
    u = 0
    for j, es in plan:
        for e in es:
            value = 0.0
            for t in range(n):
                term = held[t, :, u * columns : (u + 1) * columns].astype(jnp.int32).astype(jnp.float32)
                value = value + term * scales[t][:, u : u + 1]
            value = value * mask_ref[:, e * columns : (e + 1) * columns]
            done_refs[j][:, e * columns : (e + 1) * columns] = value.astype(jnp.bfloat16)
            u += 1
    starts = [pl.multiple_of(lax.rem(at_ref[2] + offset_at(j, at_ref[3]), NY) * width, 16) for j in range(NY)]
    for k in range(n_rows):
        for f in range(NZ):
            sums = [0.0] * NZ
            for start, done_ref in zip(starts, done_refs):
                row = row_refs[k][pl.ds(start, width), f * columns : (f + 1) * columns].astype(jnp.float32)
                for e in range(NZ):
                    term = row * done_ref[:, e * columns : (e + 1) * columns].astype(jnp.float32)
                    sums[e] = sums[e] + term.reshape(width // 8, 8, columns).sum(0)
            for e in range(NZ):
                i = (k * NZ + f) * NZ + e
                dots[i : i + 1] = sums[e].sum(0, keepdims=True)
    bmat_ref[...] = (dots[...].sum(1, keepdims=True) * weight_ref[...]).sum(0, keepdims=True)


def finish(plan, at, total, mask, weight, rows):
    columns = rows[0].shape[1] // NZ
    done = jax.ShapeDtypeStruct((total.shape[1], NZ * columns), jnp.bfloat16)
    return pl.pallas_call(
        functools.partial(finish_kernel, plan, len(rows)),
        out_shape=[done] * NY + [jax.ShapeDtypeStruct((1, weight.shape[1]), jnp.float32)],
        in_specs=[SMEM, ANY] + [VMEM] * (2 + len(rows)),
        out_specs=[VMEM] * (NY + 1),
        scratch_shapes=[
            pltpu.VMEM(total.shape, total.dtype),
            pltpu.SemaphoreType.DMA((total.shape[0],)),
            pltpu.VMEM((weight.shape[0], columns), jnp.float32),
        ],
        compiler_params=pltpu.CompilerParams(vmem_limit_bytes=16 * 2**20),
        cost_estimate=CHEAP,
    )(at, total, mask, weight, *rows)


def rows_kernel(n, at_ref, *refs):
    g_refs, (out_ref, arrived) = refs[:n], refs[n:]
    count, columns = out_ref.shape[0], g_refs[0].shape[1]
    start = pl.multiple_of(at_ref[1] * count, 64)
    copies = [
        pltpu.make_async_copy(
            ref.at[pl.ds(start, count)], out_ref.at[:, j * columns : (j + 1) * columns], arrived.at[j]
        )
        for j, ref in enumerate(g_refs)
    ]
    for copy in copies:
        copy.start()
    for copy in copies:
        copy.wait()


def rows_of(at, g, count):
    return pl.pallas_call(
        functools.partial(rows_kernel, len(g)),
        out_shape=jax.ShapeDtypeStruct((count, len(g) * g[0].shape[1]), g[0].dtype),
        in_specs=[SMEM] + [ANY] * len(g),
        out_specs=VMEM,
        scratch_shapes=[pltpu.SemaphoreType.DMA((len(g),))],
        compiler_params=pltpu.CompilerParams(vmem_limit_bytes=4 * 2**20),
        cost_estimate=CHEAP,
    )(at, *g)


def place_kernel(at_ref, *refs):
    *piece_refs, out_ref = refs
    columns = out_ref.shape[2]
    for k, piece_ref in enumerate(piece_refs):
        owner = lax.rem(at_ref[2] + NY - offset_at(k, at_ref[3]), NY)
        for j, e in enumerate(ORDER):
            slot = lax.rem(at_ref[1] + e, NZ) * NY + owner
            out_ref[slot] = piece_ref[:, j * columns : (j + 1) * columns]


def place(at, pieces, columns):
    width = pieces[0].shape[0]
    return pl.pallas_call(
        place_kernel,
        out_shape=jax.ShapeDtypeStruct((NZ * NY, width, columns), jnp.bfloat16),
        in_specs=[SMEM] + [VMEM] * len(pieces),
        out_specs=VMEM,
        compiler_params=pltpu.CompilerParams(vmem_limit_bytes=8 * 2**20),
        cost_estimate=CHEAP,
    )(at, *pieces)


def on_device(geminal, fock_matrix, slot_occupied_pair, slot_column_block, slot_live):
    n_fock, _, width, panel_rows = fock_matrix.shape
    columns = geminal.shape[2]
    n_slots = NZ * NY
    z, y, x = lax.axis_index("z"), lax.axis_index("y"), lax.axis_index("x")
    at = jnp.stack([lax.axis_index("c"), z, y, x])
    normalizer = 1.0 / (panel_rows * n_fock * columns)

    own = fock_matrix.reshape(NX, NC, width, panel_rows)
    low, high = split(own)
    g, low, high = lax.optimization_barrier((geminal[0], low, high))
    from_left, from_right = shift_y(low, 1), shift_y(high, -1)
    to_right, to_left = join(low, high, from_left, from_right)
    after_left, after_right = shift_y(to_right, 1), shift_y(to_left, -1)
    f_arrays = [own, from_left, from_right, after_left, after_right]
    f_blocks = (((0, None),), ((1, None), (2, None)), ((4, 0), (3, 1)), ((3, 0), (4, 1)))

    slots = {0: g}
    slots[1], slots[7] = shift_z(slots[0], -1), shift_z(slots[0], 1)
    slots[2], slots[6] = shift_z(slots[1], -1), shift_z(slots[7], 1)
    slots[3], slots[5] = shift_z(slots[2], -1), shift_z(slots[6], 1)

    weight, mask = facts(at, slot_occupied_pair, slot_column_block, slot_live, normalizer, columns)

    def start(plan, order, arrays):
        plan = tuple((f_blocks[j], order.index(es[0]), order.index(es[0]) + len(es)) for j, es in plan)
        away, keep = products(plan, at, arrays, [slots[e] for e in order])
        return swap_core(away), keep

    def spread(total):
        return lax.all_to_all(total, "x", 0, 0)

    def places(plan):
        return tuple((j, tuple(ORDER.index(e) for e in es)) for j, es in plan)

    first = lax.optimization_barrier((*f_arrays[:3], to_right, to_left))[:3]
    recv, keep = start(FIRST, NEAR, list(first))
    packed = pack(keep, recv)
    slots[4] = shift_z(slots[5], 1)

    rows = [rows_of(at, [slots[e] for e in ORDER], NY * width)]
    rows.append(shift_y(rows[0], -1))
    rows.append(shift_y(rows[1], -1))

    recv, keep = start(SECOND, ORDER, f_arrays)
    total = spread(pack(keep, recv, (packed,)))
    *done, bmat = finish(places(FIRST + SECOND), at, total, mask, weight, rows)
    bmat = total_over(bmat, "z", NZ)
    pieces = [to_owner(v, j) for j, v in enumerate(done)]
    *pieces, bmat = lax.optimization_barrier((*pieces, bmat))

    out = place(at, pieces, columns)
    return out, total_over(bmat, ("y", "x", "c"), NY * NX * NC)[0, :4].reshape(2, 2)


def solution(mesh):
    mesh = Mesh(mesh.devices.reshape(NZ, NY, NX, NC), ("z", "y", "x", "c"))
    pair, fock = ("z", "y"), ("x", "c")
    return jax.shard_map(
        on_device,
        mesh=mesh,
        in_specs=(P(pair, fock, None), P(None, pair, None, fock), P(), P(), P()),
        out_specs=(P(None, fock + pair, None), P()),
        check_vma=False,
    )
```

time: 321 us -> 136 us (0.42)
  waiting for transfers between devices: 211 us -> 46.6 us
  blocking collectives: 76.8 us -> 13.1 us
  starting transfers between devices: 0.08 us -> 47.3 us
  Pallas kernels: 0 us -> 22 us
  between operations: 14.1 us -> 0.77 us
  matrix products: 12.7 us -> 0 us
    all_gather x1 -> x0, waiting for transfers between devices: 126 us -> none  [on_device(): gathered = lax.all_gather(geminal, 'pair', axis=0, tiled=True)]
    psum x1 -> x0, waiting for transfers between devices: 84.9 us -> none  [panel_total(): summed = lax.psum(products, 'fock')]
    psum x1 -> x0, blocking collectives: 76.8 us -> none  [on_device(): intersections = lax.psum(intersections, ('pair', 'fock'))]
    ppermute x0 -> x18, waiting for transfers between devices: none -> 41.1 us  [the longest x7 24.1 us: shift_z(): return lax.ppermute(v, 'z', [(z, (z + s) % NZ) for z in range(NZ)])]
    ppermute x0 -> x18, starting transfers between devices: none -> 32.8 us  [the longest x7 13.2 us: shift_z(): return lax.ppermute(v, 'z', [(z, (z + s) % NZ) for z in range(NZ)])]
    pallas_call x0 -> x10, Pallas kernels: none -> 22 us  [the longest x2 8.66 us: products(): pl.pallas_call(functools.partial(products_kernel, plan, len(f_arrays), le...]
    all_to_all x0 -> x2, starting transfers between devices: none -> 14.4 us  [the longest x1 10.3 us: total_over(): lax.all_to_all(jnp.broadcast_to(v, (n,) + v.shape), axis, 0, 0).sum(0)]
    all_to_all x0 -> x1, blocking collectives: none -> 13.1 us  [total_over(): lax.all_to_all(jnp.broadcast_to(v, (n,) + v.shape), axis, 0, 0).sum(0)]
  transfers between devices with their start and end apart: 2 -> 20, of which waited for: 2 -> 11; matrix products, arithmetic and copies ran while one was open for 0% -> 0% of each run, Pallas kernels for 0% -> 6%
where the time goes in v2:
time: 136 us
  starting transfers between devices  47.3 us (35%)
  waiting for transfers between devices  46.6 us (34%)
  Pallas kernels  22 us (16%)
  blocking collectives  13.1 us (10%)
  local copies, waits for them, and re-layouts  6.05 us (4%)
    ppermute x7, waiting for transfers between devices, shift_z(): return lax.ppermute(v, 'z', [(z, (z + s) % NZ) for z in range(NZ)])  24.1 us
    ppermute x6, waiting for transfers between devices, shift_y(): return lax.ppermute(v, 'y', [(y, (y + s) % NY) for y in range(NY)])  13.7 us
    ppermute x7, starting transfers between devices, shift_z(): return lax.ppermute(v, 'z', [(z, (z + s) % NZ) for z in range(NZ)])  13.2 us
    all_to_all x1, blocking collectives, total_over(): lax.all_to_all(jnp.broadcast_to(v, (n,) + v.shape), axis, 0, 0).sum(0)  13.1 us
    ppermute x6, starting transfers between devices, shift_y(): return lax.ppermute(v, 'y', [(y, (y + s) % NY) for y in range(NY)])  10.6 us
    all_to_all x1, starting transfers between devices, total_over(): lax.all_to_all(jnp.broadcast_to(v, (n,) + v.shape), axis, 0, 0).sum(0)  10.3 us
    pallas_call x2, Pallas kernels, products(): pl.pallas_call(functools.partial(products_kernel, plan, len(f_arrays), le...  8.66 us
    all_to_all x1, waiting for transfers between devices, total_over(): lax.all_to_all(jnp.broadcast_to(v, (n,) + v.shape), axis, 0, 0).sum(0)  5.55 us
  transfers between devices with their start and end apart: 20, of which 11 were waited for; matrix products, arithmetic and copies ran while one was open for 0% of the time, Pallas kernels for 6%

profile of v2, /device:TPU:1, one launch (start us, length us, event | category | flops | bytes accessed | tf_op | source)
XLA Modules:
  0.0 135.9 jit_solution(11027216931138273054)
XLA Ops:
  0.6 1.3 copy-done
  1.9 0.1 shard_map.68
  2.0 2.2 %collective-permute-start = (bf16[2,2,48,1536]{3,2,1,0:T(8,128)(2,1)S(1)}, bf16[2,2,48,1536]{3,2,1,0:T(8,128)(2,1)S(1)}, u32[]{:S(2)}, u32[]{:S(2)}) collective-permute-start(bf16[2,2,48,1536]{3,2,1,0:T(8,128)(2,1)S(1)} %get-tuple-element.30.low_ref), channel_id=1, source_target_pairs={{0,8},{8,16},{16,24},{24,0},{1,9},{9,17},{17,25},{25,1},{2,10},{10... | collective-permute-start | bytes 1769480 | tf_op jit(solution)/shard_map/ppermute | solution.py:38
  4.2 1.5 %collective-permute-start.1 = (bf16[2,2,48,1536]{3,2,1,0:T(8,128)(2,1)S(1)}, bf16[2,2,48,1536]{3,2,1,0:T(8,128)(2,1)S(1)}, u32[]{:S(2)}, u32[]{:S(2)}) collective-permute-start(bf16[2,2,48,1536]{3,2,1,0:T(8,128)(2,1)S(1)} %get-tuple-element.31.high_ref), channel_id=1, source_target_pairs={{0,24},{8,0},{16,8},{24,16},{1,25},{9,1},{17,9},{25,17},{2,26},{10... | collective-permute-start | bytes 1769480 | tf_op jit(solution)/shard_map/ppermute | solution.py:38
  5.7 1.6 %collective-permute-start.5 = (bf16[1536,128]{1,0:T(8,128)(2,1)}, bf16[1536,128]{1,0:T(8,128)(2,1)S(1)}, u32[]{:S(2)}, u32[]{:S(2)}) collective-permute-start(bf16[1536,128]{1,0:T(8,128)(2,1)} %bitcast.15), channel_id=1, source_target_pairs={{0,32},{32,64},{64,96},{96,128},{128,160},{160,192},{192,224},{224... | collective-permute-start | bytes 1179656 | tf_op jit(solution)/shard_map/ppermute | solution.py:34
  7.4 3.9 %collective-permute-start.4 = (bf16[1536,128]{1,0:T(8,128)(2,1)}, bf16[1536,128]{1,0:T(8,128)(2,1)S(1)}, u32[]{:S(2)}, u32[]{:S(2)}) collective-permute-start(bf16[1536,128]{1,0:T(8,128)(2,1)} %bitcast.16), channel_id=1, source_target_pairs={{0,224},{32,0},{64,32},{96,64},{128,96},{160,128},{192,160},{224,1... | collective-permute-start | bytes 1179656 | tf_op jit(solution)/shard_map/ppermute | solution.py:34
  11.3 8.6 %collective-permute-done.5.refs_7_.refs_5_.refs_2_ = bf16[1536,128]{1,0:T(8,128)(2,1)S(1)} collective-permute-done((bf16[1536,128]{1,0:T(8,128)(2,1)}, bf16[1536,128]{1,0:T(8,128)(2,1)S(1)}, u32[]{:S(2)}, u32[]{:S(2)}) %collective-permute-start.5) | collective-permute-done | bytes 393248 | tf_op jit(solution)/shard_map/ppermute | solution.py:34
  19.9 0.0 collective-permute-start.7
  19.9 1.6 %shard_map.69 = (bf16[4,2,48,1536]{3,2,1,0:T(8,128)(2,1)}, bf16[4,2,48,1536]{3,2,1,0:T(8,128)(2,1)}) custom-call(bf16[2,2,48,1536]{3,2,1,0:T(8,128)(2,1)S(1)} %get-tuple-element.30.low_ref, bf16[2,2,48,1536]{3,2,1,0:T(8,128)(2,1)S(1)} %get-tuple-element.31.high_ref, bf16[2,2,48,1536]{3,2,1,0:T(8,128)(2,1)S(1)} %collective-permute-done.left_ref.refs_1_, ...), custom_call_target="tpu_custom_call" | custom-call | flops 1 | bytes 1 | tf_op jit(solution)/shard_map/pallas_call | solution.py:85
  21.5 2.7 %collective-permute-start.3 = (bf16[4,2,48,1536]{3,2,1,0:T(8,128)(2,1)}, bf16[4,2,48,1536]{3,2,1,0:T(8,128)(2,1)}, u32[]{:S(2)}, u32[]{:S(2)}) collective-permute-start(bf16[4,2,48,1536]{3,2,1,0:T(8,128)(2,1)} %get-tuple-element.33), channel_id=1, source_target_pairs={{0,24},{8,0},{16,8},{24,16},{1,25},{9,1},{17,9},{25,17},{2,26},{10... | collective-permute-start | bytes 3538952 | tf_op jit(solution)/shard_map/ppermute | solution.py:38
  24.1 4.1 %collective-permute-start.6 = (bf16[1536,128]{1,0:T(8,128)(2,1)S(1)}, bf16[1536,128]{1,0:T(8,128)(2,1)}, u32[]{:S(2)}, u32[]{:S(2)}) collective-permute-start(bf16[1536,128]{1,0:T(8,128)(2,1)S(1)} %collective-permute-done.4.refs_6_.refs_4_.refs_1_), channel_id=1, source_target_pairs={{0,224},{32,0},{64,32},{96,64},{128,96},{160,128},{192,160},{224,1... | collective-permute-start | bytes 1179656 | tf_op jit(solution)/shard_map/ppermute | solution.py:34
  28.3 1.8 %collective-permute-done.7.refs_9_.refs_4_ = bf16[1536,128]{1,0:T(8,128)(2,1)S(1)} collective-permute-done((bf16[1536,128]{1,0:T(8,128)(2,1)S(1)}, bf16[1536,128]{1,0:T(8,128)(2,1)S(1)}, u32[]{:S(2)}, u32[]{:S(2)}) %collective-permute-start.7) | collective-permute-done | bytes 393248 | tf_op jit(solution)/shard_map/ppermute | solution.py:34
  30.1 0.7 copy-done.3
  30.8 3.8 %collective-permute-done.6.refs_8_.refs_3_ = bf16[1536,128]{1,0:T(8,128)(2,1)} collective-permute-done((bf16[1536,128]{1,0:T(8,128)(2,1)S(1)}, bf16[1536,128]{1,0:T(8,128)(2,1)}, u32[]{:S(2)}, u32[]{:S(2)}) %collective-permute-start.6) | collective-permute-done | bytes 393248 | tf_op jit(solution)/shard_map/ppermute | solution.py:34
  34.6 3.5 %collective-permute-start.8 = (bf16[1536,128]{1,0:T(8,128)(2,1)}, bf16[1536,128]{1,0:T(8,128)(2,1)}, u32[]{:S(2)}, u32[]{:S(2)}) collective-permute-start(bf16[1536,128]{1,0:T(8,128)(2,1)} %collective-permute-done.6.refs_8_.refs_3_), channel_id=1, source_target_pairs={{0,224},{32,0},{64,32},{96,64},{128,96},{160,128},{192,160},{224,1... | collective-permute-start | bytes 1179656 | tf_op jit(solution)/shard_map/ppermute | solution.py:34
  38.1 1.4 collective-permute-done.9.refs_11_.refs_6_
  39.5 0.1 pad_add_fusion.at_ref
  39.6 4.3 %collective-permute-done.8.refs_10_.refs_5_ = bf16[1536,128]{1,0:T(8,128)(2,1)} collective-permute-done((bf16[1536,128]{1,0:T(8,128)(2,1)}, bf16[1536,128]{1,0:T(8,128)(2,1)}, u32[]{:S(2)}, u32[]{:S(2)}) %collective-permute-start.8) | collective-permute-done | bytes 393248 | tf_op jit(solution)/shard_map/ppermute | solution.py:34
  43.9 4.3 %collective-permute-done.10.refs_12_.refs_7_ = bf16[1536,128]{1,0:T(8,128)(2,1)} collective-permute-done((bf16[1536,128]{1,0:T(8,128)(2,1)}, bf16[1536,128]{1,0:T(8,128)(2,1)}, u32[]{:S(2)}, u32[]{:S(2)}) %collective-permute-start.10) | collective-permute-done | bytes 393248 | tf_op jit(solution)/shard_map/ppermute | solution.py:34
  48.2 0.6 collective-permute-done.2.refs_3_
  48.8 0.0 copy-start.4
  48.8 1.0 copy-done.4
  49.8 6.7 %shard_map.70 = (f32[4,48,3328]{2,1,0:T(8,128)S(1)}, f32[4,48,3328]{2,1,0:T(8,128)S(1)}) custom-call(s32[4]{0:T(128)S(1)} %pad_add_fusion.at_ref, bf16[4,2,48,1536]{3,2,1,0:T(8,128)(2,1)S(1)} %bitcast.13, bf16[2,2,48,1536]{3,2,1,0:T(8,128)(2,1)S(1)} %collective-permute-done.left_ref.refs_1_, ...), custom_call_target="tpu_custom_call" | custom-call | flops 1 | bytes 1 | tf_op jit(solution)/shard_map/pallas_call | solution.py:164
  56.4 4.1 %collective-permute-start.11 = (f32[4,48,3328]{2,1,0:T(8,128)S(1)}, f32[4,48,3328]{2,1,0:T(8,128)S(1)}, u32[]{:S(2)}, u32[]{:S(2)}) collective-permute-start(f32[4,48,3328]{2,1,0:T(8,128)S(1)} %get-tuple-element.36), channel_id=1, source_target_pairs={{0,1},{1,0},{2,3},{3,2},{4,5},{5,4},{6,7},{7,6},{8,9},{9,8},{10,11... | collective-permute-start | bytes 7667720 | tf_op jit(solution)/shard_map/ppermute | solution.py:50
  60.5 2.0 %shard_map.71 = (f32[4,48,768]{2,1,0:T(8,128)S(1)}, f32[4,48,768]{2,1,0:T(8,128)S(1)}) custom-call(s32[4]{0:T(128)S(1)} %pad_add_fusion.at_ref, bf16[4,2,48,1536]{3,2,1,0:T(8,128)(2,1)S(1)} %bitcast.14, bf16[2,2,48,1536]{3,2,1,0:T(8,128)(2,1)S(1)} %collective-permute-done.left_ref.refs_1_, ...), custom_call_target="tpu_custom_call" | custom-call | flops 1 | bytes 1 | tf_op jit(solution)/shard_map/pallas_call | solution.py:164
  62.5 0.1 collective-permute-start.12
  62.6 3.2 %collective-permute-done.12.recv_ref = f32[4,48,768]{2,1,0:T(8,128)S(1)} collective-permute-done((f32[4,48,768]{2,1,0:T(8,128)S(1)}, f32[4,48,768]{2,1,0:T(8,128)S(1)}, u32[]{:S(2)}, u32[]{:S(2)}) %collective-permute-start.12) | collective-permute-done | bytes 589856 | tf_op jit(solution)/shard_map/ppermute | solution.py:50
  65.8 0.7 shard_map.72.refs_0_
  66.5 2.7 %shard_map.73 = s16[4,48,4224]{2,1,0:T(8,128)(2,1)} custom-call(f32[4,48,3328]{2,1,0:T(8,128)S(1)} %get-tuple-element.35.keep_ref, f32[4,48,3328]{2,1,0:T(8,128)S(1)} %collective-permute-done.11.recv_ref, s16[4,48,896]{2,1,0:T(8,128)(2,1)S(1)} %shard_map.72.refs_0_), custom_call_target="tpu_custom_call" | custom-call | flops 1 | bytes 1 | tf_op jit(solution)/shard_map/pallas_call | solution.py:125
  69.2 4.1 %all-to-all-start = ((s16[4,48,4224]{2,1,0:T(8,128)(2,1)}), s16[4,48,4224]{2,1,0:T(8,128)(2,1)S(1)}, u32[]{:S(2)}, u32[]{:S(2)}) async-start(s16[4,48,4224]{2,1,0:T(8,128)(2,1)} %shard_map.73), calls=%async_computation | async-start | bytes 3244032 | tf_op jit(solution)/shard_map/all_to_all | solution.py:346
  73.4 0.0 copy-start.10
  73.4 1.5 %shard_map.75.refs_0_ = bf16[192,1024]{1,0:T(8,128)(2,1)S(1)} custom-call(s32[4]{0:T(128)S(1)} %pad_add_fusion.at_ref, bf16[1536,128]{1,0:T(8,128)(2,1)S(1)} %bitcast.19, bf16[1536,128]{1,0:T(8,128)(2,1)S(1)} %collective-permute-done.4.refs_6_.refs_4_.refs_1_, bf16[1536,128]{1,0:T(8,128)(2,1)S(1)} %collective-permute-done.5.refs_7_.refs_5_.refs_2_, ...), custom_call_target="tpu_custom_call" | custom-call | flops 1 | bytes 1 | tf_op jit(solution)/shard_map/pallas_call | solution.py:283
  74.9 1.6 %collective-permute-start.13 = (bf16[192,1024]{1,0:T(8,128)(2,1)S(1)}, bf16[192,1024]{1,0:T(8,128)(2,1)S(1)}, u32[]{:S(2)}, u32[]{:S(2)}) collective-permute-start(bf16[192,1024]{1,0:T(8,128)(2,1)S(1)} %shard_map.75.refs_0_), channel_id=1, source_target_pairs={{0,24},{8,0},{16,8},{24,16},{1,25},{9,1},{17,9},{25,17},{2,26},{10... | collective-permute-start | bytes 1179656 | tf_op jit(solution)/shard_map/ppermute | solution.py:38
  76.5 0.7 copy-done.6
  77.2 7.8 %collective-permute-done.13.refs_1_ = bf16[192,1024]{1,0:T(8,128)(2,1)S(1)} collective-permute-done((bf16[192,1024]{1,0:T(8,128)(2,1)S(1)}, bf16[192,1024]{1,0:T(8,128)(2,1)S(1)}, u32[]{:S(2)}, u32[]{:S(2)}) %collective-permute-start.13) | collective-permute-done | bytes 393248 | tf_op jit(solution)/shard_map/ppermute | solution.py:38
  85.0 2.7 %collective-permute-start.14 = (bf16[192,1024]{1,0:T(8,128)(2,1)S(1)}, bf16[192,1024]{1,0:T(8,128)(2,1)S(1)}, u32[]{:S(2)}, u32[]{:S(2)}) collective-permute-start(bf16[192,1024]{1,0:T(8,128)(2,1)S(1)} %collective-permute-done.13.refs_1_), channel_id=1, source_target_pairs={{0,24},{8,0},{16,8},{24,16},{1,25},{9,1},{17,9},{25,17},{2,26},{10... | collective-permute-start | bytes 1179656 | tf_op jit(solution)/shard_map/ppermute | solution.py:38
  87.7 1.5 %shard_map.74 = (f32[192,128]{1,0:T(8,128)S(1)}, f32[1,1024]{1,0:T(1,128)S(1)}) custom-call(s32[4]{0:T(128)S(1)} %pad_add_fusion.at_ref, s32[32]{0:T(128)S(1)} %copy-done.8, s32[32]{0:T(128)S(1)} %copy-done.9, s32[32]{0:T(128)S(1)} %copy-done.10), custom_call_target="tpu_custom_call" | custom-call | flops 1 | bytes 1 | tf_op jit(solution)/shard_map/pallas_call | solution.py:198
  89.2 5.4 %collective-permute-done.14.refs_2_ = bf16[192,1024]{1,0:T(8,128)(2,1)S(1)} collective-permute-done((bf16[192,1024]{1,0:T(8,128)(2,1)S(1)}, bf16[192,1024]{1,0:T(8,128)(2,1)S(1)}, u32[]{:S(2)}, u32[]{:S(2)}) %collective-permute-start.14) | collective-permute-done | bytes 393248 | tf_op jit(solution)/shard_map/ppermute | solution.py:38
  94.6 1.0 copy-done.7
  95.6 3.9 %shard_map.76 = (bf16[48,1024]{1,0:T(8,128)(2,1)S(1)}, bf16[48,1024]{1,0:T(8,128)(2,1)S(1)}, bf16[48,1024]{1,0:T(8,128)(2,1)S(1)}, bf16[48,1024]{1,0:T(8,128)(2,1)S(1)}, f32[1,128]{1,0:T(1,128)S(1)}) custom-call(s32[4]{0:T(128)S(1)} %pad_add_fusion.at_ref, s16[4,48,4224]{2,1,0:T(8,128)(2,1)S(1)} %all-to-all-done.total_ref, ...), custom_call_target="tpu_custom_call" | custom-call | flops 1 | bytes 1 | tf_op jit(solution)/shard_map/pallas_call | solution.py:251
  99.5 3.5 %collective-permute-start.15 = (bf16[48,1024]{1,0:T(8,128)(2,1)S(1)}, bf16[48,1024]{1,0:T(8,128)(2,1)S(1)}, u32[]{:S(2)}, u32[]{:S(2)}) collective-permute-start(bf16[48,1024]{1,0:T(8,128)(2,1)S(1)} %get-tuple-element.45), channel_id=1, source_target_pairs={{0,24},{2,26},{4,12},{6,14},{8,0},{10,2},{12,20},{14,22},{16,8},{1... | collective-permute-start | bytes 294920 | tf_op jit(solution)/shard_map/ppermute | solution.py:46
  103.0 1.3 collective-permute-start.17
  104.3 13.1 %all_to_all.15 = f32[8,1,128]{2,1,0:T(1,128)S(1)} all-to-all(f32[8,1,128]{2,1,0:T(1,128)S(1)} %broadcast_in_dim.6), channel_id=1, replica_groups=mesh['z'=8,'y'=4,'x'=4,'c'=2] {'z'}, dimensions={0} | all-to-all | bytes 8192 | tf_op jit(solution)/shard_map/all_to_all | solution.py:54
  117.4 0.6 broadcast_in_dim.7
  118.0 10.3 %all-to-all-start.2 = ((f32[32,1,128]{2,1,0:T(1,128)}), f32[32,1,128]{2,1,0:T(1,128)S(1)}, u32[]{:S(2)}, u32[]{:S(2)}) async-start(f32[32,1,128]{2,1,0:T(1,128)} %broadcast_in_dim.7), calls=%async_computation.2 | async-start | bytes 32768 | tf_op jit(solution)/shard_map/all_to_all | solution.py:54
  128.3 1.4 %shard_map.77 = bf16[32,48,128]{2,1,0:T(8,128)(2,1)} custom-call(s32[4]{0:T(128)S(1)} %pad_add_fusion.at_ref, bf16[48,1024]{1,0:T(8,128)(2,1)S(1)} %get-tuple-element.49.refs_0_, bf16[48,1024]{1,0:T(8,128)(2,1)S(1)} %collective-permute-done.15.refs_1_, bf16[48,1024]{1,0:T(8,128)(2,1)S(1)} %collective-permute-done.16.refs_2_, ...), custom_call_target="tpu_custom_call" | custom-call | flops 1 | bytes 1 | tf_op jit(solution)/shard_map/pallas_call | solution.py:306
  129.7 5.6 %all-to-all-done.2 = f32[32,1,128]{2,1,0:T(1,128)S(1)} async-done(((f32[32,1,128]{2,1,0:T(1,128)}), f32[32,1,128]{2,1,0:T(1,128)S(1)}, u32[]{:S(2)}, u32[]{:S(2)}) %all-to-all-start.2) | async-done | bytes 16416 | tf_op jit(solution)/shard_map/all_to_all | solution.py:54
  135.3 0.6 reshape_squeeze.3
  (32 shorter events, 0.1 us)
Async XLA Ops:
  0.6 1.3 copy-start
  1.9 46.9 %copy-start.1 = (bf16[8,1,48,1536]{3,2,1,0:T(8,128)(2,1)S(1)}, bf16[8,1,48,1536]{3,2,1,0:T(8,128)(2,1)}, u32[]{:S(2)}) copy-start(bf16[8,1,48,1536]{3,2,1,0:T(8,128)(2,1)} %param.6) | copy-start | bytes 3538948
  1.9 46.9 %copy-start.2 = (bf16[1,1536,128]{2,1,0:T(8,128)(2,1)S(1)}, bf16[1,1536,128]{2,1,0:T(8,128)(2,1)}, u32[]{:S(2)}) copy-start(bf16[1,1536,128]{2,1,0:T(8,128)(2,1)} %param.5) | copy-start | bytes 1179652
  2.0 17.9 %collective-permute-start = (bf16[2,2,48,1536]{3,2,1,0:T(8,128)(2,1)S(1)}, bf16[2,2,48,1536]{3,2,1,0:T(8,128)(2,1)S(1)}, u32[]{:S(2)}, u32[]{:S(2)}) collective-permute-start(bf16[2,2,48,1536]{3,2,1,0:T(8,128)(2,1)S(1)} %get-tuple-element.30.low_ref), channel_id=1, source_target_pairs={{0,8},{8,16},{16,24},{24,0},{1,9},{9,17},{17,25},{25,1},{2,10},{10... | collective-permute-start | bytes 1769480 | tf_op jit(solution)/shard_map/ppermute | solution.py:38
  4.2 15.7 %collective-permute-start.1 = (bf16[2,2,48,1536]{3,2,1,0:T(8,128)(2,1)S(1)}, bf16[2,2,48,1536]{3,2,1,0:T(8,128)(2,1)S(1)}, u32[]{:S(2)}, u32[]{:S(2)}) collective-permute-start(bf16[2,2,48,1536]{3,2,1,0:T(8,128)(2,1)S(1)} %get-tuple-element.31.high_ref), channel_id=1, source_target_pairs={{0,24},{8,0},{16,8},{24,16},{1,25},{9,1},{17,9},{25,17},{2,26},{10... | collective-permute-start | bytes 1769480 | tf_op jit(solution)/shard_map/ppermute | solution.py:38
  5.7 14.2 %collective-permute-start.5 = (bf16[1536,128]{1,0:T(8,128)(2,1)}, bf16[1536,128]{1,0:T(8,128)(2,1)S(1)}, u32[]{:S(2)}, u32[]{:S(2)}) collective-permute-start(bf16[1536,128]{1,0:T(8,128)(2,1)} %bitcast.15), channel_id=1, source_target_pairs={{0,32},{32,64},{64,96},{96,128},{128,160},{160,192},{192,224},{224... | collective-permute-start | bytes 1179656 | tf_op jit(solution)/shard_map/ppermute | solution.py:34
  7.4 16.8 %collective-permute-start.4 = (bf16[1536,128]{1,0:T(8,128)(2,1)}, bf16[1536,128]{1,0:T(8,128)(2,1)S(1)}, u32[]{:S(2)}, u32[]{:S(2)}) collective-permute-start(bf16[1536,128]{1,0:T(8,128)(2,1)} %bitcast.16), channel_id=1, source_target_pairs={{0,224},{32,0},{64,32},{96,64},{128,96},{160,128},{192,160},{224,1... | collective-permute-start | bytes 1179656 | tf_op jit(solution)/shard_map/ppermute | solution.py:34
  19.9 10.2 %collective-permute-start.7 = (bf16[1536,128]{1,0:T(8,128)(2,1)S(1)}, bf16[1536,128]{1,0:T(8,128)(2,1)S(1)}, u32[]{:S(2)}, u32[]{:S(2)}) collective-permute-start(bf16[1536,128]{1,0:T(8,128)(2,1)S(1)} %collective-permute-done.5.refs_7_.refs_5_.refs_2_), channel_id=1, source_target_pairs={{0,32},{32,64},{64,96},{96,128},{128,160},{160,192},{192,224},{224... | collective-permute-start | bytes 1179656 | tf_op jit(solution)/shard_map/ppermute | solution.py:34
  21.5 27.3 %collective-permute-start.2 = (bf16[4,2,48,1536]{3,2,1,0:T(8,128)(2,1)}, bf16[4,2,48,1536]{3,2,1,0:T(8,128)(2,1)}, u32[]{:S(2)}, u32[]{:S(2)}) collective-permute-start(bf16[4,2,48,1536]{3,2,1,0:T(8,128)(2,1)} %get-tuple-element.32), channel_id=1, source_target_pairs={{0,8},{8,16},{16,24},{24,0},{1,9},{9,17},{17,25},{25,1},{2,10},{10... | collective-permute-start | bytes 3538952 | tf_op jit(solution)/shard_map/ppermute | solution.py:38
  21.5 27.3 %collective-permute-start.3 = (bf16[4,2,48,1536]{3,2,1,0:T(8,128)(2,1)}, bf16[4,2,48,1536]{3,2,1,0:T(8,128)(2,1)}, u32[]{:S(2)}, u32[]{:S(2)}) collective-permute-start(bf16[4,2,48,1536]{3,2,1,0:T(8,128)(2,1)} %get-tuple-element.33), channel_id=1, source_target_pairs={{0,24},{8,0},{16,8},{24,16},{1,25},{9,1},{17,9},{25,17},{2,26},{10... | collective-permute-start | bytes 3538952 | tf_op jit(solution)/shard_map/ppermute | solution.py:38
  24.1 10.5 %collective-permute-start.6 = (bf16[1536,128]{1,0:T(8,128)(2,1)S(1)}, bf16[1536,128]{1,0:T(8,128)(2,1)}, u32[]{:S(2)}, u32[]{:S(2)}) collective-permute-start(bf16[1536,128]{1,0:T(8,128)(2,1)S(1)} %collective-permute-done.4.refs_6_.refs_4_.refs_1_), channel_id=1, source_target_pairs={{0,224},{32,0},{64,32},{96,64},{128,96},{160,128},{192,160},{224,1... | collective-permute-start | bytes 1179656 | tf_op jit(solution)/shard_map/ppermute | solution.py:34
  30.1 9.4 %collective-permute-start.9 = (bf16[1536,128]{1,0:T(8,128)(2,1)S(1)}, bf16[1536,128]{1,0:T(8,128)(2,1)}, u32[]{:S(2)}, u32[]{:S(2)}) collective-permute-start(bf16[1536,128]{1,0:T(8,128)(2,1)S(1)} %collective-permute-done.7.refs_9_.refs_4_), channel_id=1, source_target_pairs={{0,32},{32,64},{64,96},{96,128},{128,160},{160,192},{192,224},{224... | collective-permute-start | bytes 1179656 | tf_op jit(solution)/shard_map/ppermute | solution.py:34
  30.1 0.7 copy-start.3
  34.6 9.3 %collective-permute-start.8 = (bf16[1536,128]{1,0:T(8,128)(2,1)}, bf16[1536,128]{1,0:T(8,128)(2,1)}, u32[]{:S(2)}, u32[]{:S(2)}) collective-permute-start(bf16[1536,128]{1,0:T(8,128)(2,1)} %collective-permute-done.6.refs_8_.refs_3_), channel_id=1, source_target_pairs={{0,224},{32,0},{64,32},{96,64},{128,96},{160,128},{192,160},{224,1... | collective-permute-start | bytes 1179656 | tf_op jit(solution)/shard_map/ppermute | solution.py:34
  39.5 8.7 %collective-permute-start.10 = (bf16[1536,128]{1,0:T(8,128)(2,1)}, bf16[1536,128]{1,0:T(8,128)(2,1)}, u32[]{:S(2)}, u32[]{:S(2)}) collective-permute-start(bf16[1536,128]{1,0:T(8,128)(2,1)} %collective-permute-done.9.refs_11_.refs_6_), channel_id=1, source_target_pairs={{0,32},{32,64},{64,96},{96,128},{128,160},{160,192},{192,224},{224... | collective-permute-start | bytes 1179656 | tf_op jit(solution)/shard_map/ppermute | solution.py:34
  48.8 1.0 copy-start.4
  56.4 10.0 %collective-permute-start.11 = (f32[4,48,3328]{2,1,0:T(8,128)S(1)}, f32[4,48,3328]{2,1,0:T(8,128)S(1)}, u32[]{:S(2)}, u32[]{:S(2)}) collective-permute-start(f32[4,48,3328]{2,1,0:T(8,128)S(1)} %get-tuple-element.36), channel_id=1, source_target_pairs={{0,1},{1,0},{2,3},{3,2},{4,5},{5,4},{6,7},{7,6},{8,9},{9,8},{10,11... | collective-permute-start | bytes 7667720 | tf_op jit(solution)/shard_map/ppermute | solution.py:50
  62.5 3.3 %collective-permute-start.12 = (f32[4,48,768]{2,1,0:T(8,128)S(1)}, f32[4,48,768]{2,1,0:T(8,128)S(1)}, u32[]{:S(2)}, u32[]{:S(2)}) collective-permute-start(f32[4,48,768]{2,1,0:T(8,128)S(1)} %get-tuple-element.41), channel_id=1, source_target_pairs={{0,1},{1,0},{2,3},{3,2},{4,5},{5,4},{6,7},{7,6},{8,9},{9,8},{10,11... | collective-permute-start | bytes 1769480 | tf_op jit(solution)/shard_map/ppermute | solution.py:50
  69.2 4.1 %copy-start.5 = (bf16[1536,128]{1,0:T(8,128)(2,1)S(1)}, bf16[1536,128]{1,0:T(8,128)(2,1)}, u32[]{:S(2)}) copy-start(bf16[1536,128]{1,0:T(8,128)(2,1)} %copy-done.3) | copy-start | bytes 1179652
  69.2 25.4 %all-to-all-start = ((s16[4,48,4224]{2,1,0:T(8,128)(2,1)}), s16[4,48,4224]{2,1,0:T(8,128)(2,1)S(1)}, u32[]{:S(2)}, u32[]{:S(2)}) async-start(s16[4,48,4224]{2,1,0:T(8,128)(2,1)} %shard_map.73), calls=%async_computation | async-start | bytes 3244032 | tf_op jit(solution)/shard_map/all_to_all | solution.py:346
  73.4 14.3 %copy-start.8 = (s32[32]{0:T(128)S(1)}, s32[32]{0:T(128)}, u32[]{:S(2)}) copy-start(s32[32]{0:T(128)} %pair_ref.1) | copy-start | bytes 388
  73.4 14.3 %copy-start.9 = (s32[32]{0:T(128)S(1)}, s32[32]{0:T(128)}, u32[]{:S(2)}) copy-start(s32[32]{0:T(128)} %block_ref.1) | copy-start | bytes 388
  73.4 14.3 %copy-start.10 = (s32[32]{0:T(128)S(1)}, s32[32]{0:T(128)}, u32[]{:S(2)}) copy-start(s32[32]{0:T(128)} %live_ref.1) | copy-start | bytes 388
  74.9 10.1 %collective-permute-start.13 = (bf16[192,1024]{1,0:T(8,128)(2,1)S(1)}, bf16[192,1024]{1,0:T(8,128)(2,1)S(1)}, u32[]{:S(2)}, u32[]{:S(2)}) collective-permute-start(bf16[192,1024]{1,0:T(8,128)(2,1)S(1)} %shard_map.75.refs_0_), channel_id=1, source_target_pairs={{0,24},{8,0},{16,8},{24,16},{1,25},{9,1},{17,9},{25,17},{2,26},{10... | collective-permute-start | bytes 1179656 | tf_op jit(solution)/shard_map/ppermute | solution.py:38
  76.5 0.7 copy-start.6
  85.0 9.6 %collective-permute-start.14 = (bf16[192,1024]{1,0:T(8,128)(2,1)S(1)}, bf16[192,1024]{1,0:T(8,128)(2,1)S(1)}, u32[]{:S(2)}, u32[]{:S(2)}) collective-permute-start(bf16[192,1024]{1,0:T(8,128)(2,1)S(1)} %collective-permute-done.13.refs_1_), channel_id=1, source_target_pairs={{0,24},{8,0},{16,8},{24,16},{1,25},{9,1},{17,9},{25,17},{2,26},{10... | collective-permute-start | bytes 1179656 | tf_op jit(solution)/shard_map/ppermute | solution.py:38
  94.6 1.0 copy-start.7
  99.5 17.8 %collective-permute-start.15 = (bf16[48,1024]{1,0:T(8,128)(2,1)S(1)}, bf16[48,1024]{1,0:T(8,128)(2,1)S(1)}, u32[]{:S(2)}, u32[]{:S(2)}) collective-permute-start(bf16[48,1024]{1,0:T(8,128)(2,1)S(1)} %get-tuple-element.45), channel_id=1, source_target_pairs={{0,24},{2,26},{4,12},{6,14},{8,0},{10,2},{12,20},{14,22},{16,8},{1... | collective-permute-start | bytes 294920 | tf_op jit(solution)/shard_map/ppermute | solution.py:46
  103.0 14.4 %collective-permute-start.16 = (bf16[48,1024]{1,0:T(8,128)(2,1)S(1)}, bf16[48,1024]{1,0:T(8,128)(2,1)S(1)}, u32[]{:S(2)}, u32[]{:S(2)}) collective-permute-start(bf16[48,1024]{1,0:T(8,128)(2,1)S(1)} %get-tuple-element.46), channel_id=1, source_target_pairs={{0,8},{2,10},{4,28},{6,30},{8,16},{10,18},{12,4},{14,6},{16,24},{1... | collective-permute-start | bytes 294920 | tf_op jit(solution)/shard_map/ppermute | solution.py:46
  103.0 14.4 %collective-permute-start.17 = (bf16[48,1024]{1,0:T(8,128)(2,1)S(1)}, bf16[48,1024]{1,0:T(8,128)(2,1)S(1)}, u32[]{:S(2)}, u32[]{:S(2)}) collective-permute-start(bf16[48,1024]{1,0:T(8,128)(2,1)S(1)} %get-tuple-element.47), channel_id=1, source_target_pairs={{0,16},{2,18},{4,20},{6,22},{8,24},{10,26},{12,28},{14,30},{16,0},... | collective-permute-start | bytes 294920 | tf_op jit(solution)/shard_map/ppermute | solution.py:46
  118.0 17.2 %all-to-all-start.2 = ((f32[32,1,128]{2,1,0:T(1,128)}), f32[32,1,128]{2,1,0:T(1,128)S(1)}, u32[]{:S(2)}, u32[]{:S(2)}) async-start(f32[32,1,128]{2,1,0:T(1,128)} %broadcast_in_dim.7), calls=%async_computation.2 | async-start | bytes 32768 | tf_op jit(solution)/shard_map/all_to_all | solution.py:54

commit v3 on v2

--- a/solution.py
+++ b/solution.py
@@ -13,9 +13,10 @@
 VMEM = pl.BlockSpec(memory_space=pltpu.VMEM)
 SMEM = pl.BlockSpec(memory_space=pltpu.SMEM)
 ANY = pl.BlockSpec(memory_space=pl.ANY)
+TAIL = 16
 CHEAP = pl.CostEstimate(flops=1, bytes_accessed=1, transcendentals=0)
 
-NEAR, FAR = (0, 1, 7), (2, 6, 3, 5, 4)
+NEAR, FAR = (0, 1, 7, 2, 6), (3, 5, 4)
 ORDER = NEAR + FAR
 FIRST = ((0, NEAR), (1, NEAR))
 SECOND = ((0, FAR), (1, FAR), (2, ORDER), (3, ORDER))
@@ -48,10 +49,6 @@
 
 def swap_core(v):
     return lax.ppermute(v, "c", [(0, 1), (1, 0)])
-
-
-def total_over(v, axis, n):
-    return lax.all_to_all(jnp.broadcast_to(v, (n,) + v.shape), axis, 0, 0).sum(0)
 
 
 def split_kernel(own_ref, low_ref, high_ref):
@@ -210,7 +207,7 @@
 
 def finish_kernel(plan, n_rows, at_ref, total_ref, mask_ref, weight_ref, *refs):
     row_refs, done_refs = refs[:n_rows], refs[n_rows : n_rows + NY]
-    bmat_ref, held, arrived, dots = refs[n_rows + NY :]
+    held, arrived, dots, made = refs[n_rows + NY :]
     n, width, _ = held.shape
     columns = dots.shape[1]
     copies = [pltpu.make_async_copy(total_ref.at[t], held.at[t], arrived.at[t]) for t in range(n)]
@@ -228,35 +225,47 @@
                 term = held[t, :, u * columns : (u + 1) * columns].astype(jnp.int32).astype(jnp.float32)
                 value = value + term * scales[t][:, u : u + 1]
             value = value * mask_ref[:, e * columns : (e + 1) * columns]
-            done_refs[j][:, e * columns : (e + 1) * columns] = value.astype(jnp.bfloat16)
+            value = value.astype(jnp.bfloat16)
+            done_refs[j][:width, e * columns : (e + 1) * columns] = value
+            made[j, :, e * columns : (e + 1) * columns] = value.astype(jnp.float32)
             u += 1
     starts = [pl.multiple_of(lax.rem(at_ref[2] + offset_at(j, at_ref[3]), NY) * width, 16) for j in range(NY)]
     for k in range(n_rows):
         for f in range(NZ):
             sums = [0.0] * NZ
-            for start, done_ref in zip(starts, done_refs):
+            for j, start in enumerate(starts):
                 row = row_refs[k][pl.ds(start, width), f * columns : (f + 1) * columns].astype(jnp.float32)
                 for e in range(NZ):
-                    term = row * done_ref[:, e * columns : (e + 1) * columns].astype(jnp.float32)
+                    term = row * made[j, :, e * columns : (e + 1) * columns]
                     sums[e] = sums[e] + term.reshape(width // 8, 8, columns).sum(0)
             for e in range(NZ):
                 i = (k * NZ + f) * NZ + e
                 dots[i : i + 1] = sums[e].sum(0, keepdims=True)
-    bmat_ref[...] = (dots[...].sum(1, keepdims=True) * weight_ref[...]).sum(0, keepdims=True)
+    bmat = (dots[...].sum(1, keepdims=True) * weight_ref[...]).sum(0, keepdims=True)
+    row = lax.broadcasted_iota(jnp.int32, (TAIL, columns), 0)
+    tail = jnp.zeros((TAIL, columns), jnp.float32)
+    for i in range(3):
+        part = bmat.astype(jnp.bfloat16).astype(jnp.float32)
+        tail = jnp.where(row == i, part, tail)
+        bmat = bmat - part
+    for done_ref in done_refs:
+        done_ref[width:, :columns] = tail.astype(jnp.bfloat16)
+        done_ref[width:, columns:] = jnp.zeros((TAIL, (NZ - 1) * columns), jnp.bfloat16)
 
 
 def finish(plan, at, total, mask, weight, rows):
     columns = rows[0].shape[1] // NZ
-    done = jax.ShapeDtypeStruct((total.shape[1], NZ * columns), jnp.bfloat16)
+    done = jax.ShapeDtypeStruct((total.shape[1] + TAIL, NZ * columns), jnp.bfloat16)
     return pl.pallas_call(
         functools.partial(finish_kernel, plan, len(rows)),
-        out_shape=[done] * NY + [jax.ShapeDtypeStruct((1, weight.shape[1]), jnp.float32)],
+        out_shape=[done] * NY,
         in_specs=[SMEM, ANY] + [VMEM] * (2 + len(rows)),
-        out_specs=[VMEM] * (NY + 1),
+        out_specs=[VMEM] * NY,
         scratch_shapes=[
             pltpu.VMEM(total.shape, total.dtype),
             pltpu.SemaphoreType.DMA((total.shape[0],)),
             pltpu.VMEM((weight.shape[0], columns), jnp.float32),
+            pltpu.VMEM((NY, total.shape[1], NZ * columns), jnp.float32),
         ],
         compiler_params=pltpu.CompilerParams(vmem_limit_bytes=16 * 2**20),
         cost_estimate=CHEAP,
@@ -292,22 +301,29 @@
 
 
 def place_kernel(at_ref, *refs):
-    *piece_refs, out_ref = refs
-    columns = out_ref.shape[2]
+    *piece_refs, out_ref, bmat_ref = refs
+    _, width, columns = out_ref.shape
+    bmat = 0.0
     for k, piece_ref in enumerate(piece_refs):
         owner = lax.rem(at_ref[2] + NY - offset_at(k, at_ref[3]), NY)
         for j, e in enumerate(ORDER):
             slot = lax.rem(at_ref[1] + e, NZ) * NY + owner
-            out_ref[slot] = piece_ref[:, j * columns : (j + 1) * columns]
+            out_ref[slot] = piece_ref[:width, j * columns : (j + 1) * columns]
+        tail = piece_ref[width:, :columns].astype(jnp.float32)
+        bmat = bmat + tail.sum(0, keepdims=True)
+    bmat_ref[...] = jnp.broadcast_to(bmat, bmat_ref.shape)
 
 
 def place(at, pieces, columns):
-    width = pieces[0].shape[0]
+    width = pieces[0].shape[0] - TAIL
     return pl.pallas_call(
         place_kernel,
-        out_shape=jax.ShapeDtypeStruct((NZ * NY, width, columns), jnp.bfloat16),
+        out_shape=[
+            jax.ShapeDtypeStruct((NZ * NY, width, columns), jnp.bfloat16),
+            jax.ShapeDtypeStruct((NZ * NX * NC, columns), jnp.float32),
+        ],
         in_specs=[SMEM] + [VMEM] * len(pieces),
-        out_specs=VMEM,
+        out_specs=[VMEM] * 2,
         compiler_params=pltpu.CompilerParams(vmem_limit_bytes=8 * 2**20),
         cost_estimate=CHEAP,
     )(at, *pieces)
@@ -357,15 +373,13 @@
     rows.append(shift_y(rows[0], -1))
     rows.append(shift_y(rows[1], -1))
 
+    rows[0], *f_arrays = lax.optimization_barrier((rows[0], *f_arrays))
     recv, keep = start(SECOND, ORDER, f_arrays)
     total = spread(pack(keep, recv, (packed,)))
-    *done, bmat = finish(places(FIRST + SECOND), at, total, mask, weight, rows)
-    bmat = total_over(bmat, "z", NZ)
-    pieces = [to_owner(v, j) for j, v in enumerate(done)]
-    *pieces, bmat = lax.optimization_barrier((*pieces, bmat))
-
-    out = place(at, pieces, columns)
-    return out, total_over(bmat, ("y", "x", "c"), NY * NX * NC)[0, :4].reshape(2, 2)
+    done = finish(places(FIRST + SECOND), at, total, mask, weight, rows)
+    out, bmat = place(at, [to_owner(v, j) for j, v in enumerate(done)], columns)
+    bmat = lax.all_to_all(bmat, ("z", "x", "c"), 0, 0, tiled=True)
+    return out, bmat[:, :4].sum(0).reshape(2, 2)
 
 
 def solution(mesh):

time: 136 us -> 129 us (0.949)
  starting transfers between devices: 47.3 us -> 34.6 us
  blocking collectives: 13.1 us -> 20.6 us
  local copies, waits for them, and re-layouts: 6.05 us -> 2.67 us
  waiting for transfers between devices: 46.6 us -> 48.7 us
    all_to_all x1 -> x0, starting transfers between devices: 10.3 us -> none  [total_over(): lax.all_to_all(jnp.broadcast_to(v, (n,) + v.shape), axis, 0, 0).sum(0)]
    all_to_all x1, blocking collectives: 13.1 us -> 20.6 us  [on_device(): bmat = lax.all_to_all(bmat, ('z', 'x', 'c'), 0, 0, tiled=True)]
    all_to_all x1 -> x0, waiting for transfers between devices: 5.55 us -> none  [total_over(): lax.all_to_all(jnp.broadcast_to(v, (n,) + v.shape), axis, 0, 0).sum(0)]
    ppermute x3, waiting for transfers between devices: 0.01 us -> 5.16 us  [to_owner(): return lax.ppermute(v, ('y', 'x'), moves) if j else v]
    unnamed x22 -> x16, local copies, waits for them, and re-layouts: 4.77 us -> 2.03 us
    ppermute x6, starting transfers between devices: 10.6 us -> 8.33 us  [shift_y(): return lax.ppermute(v, 'y', [(y, (y + s) % NY) for y in range(NY)])]
    ppermute x3, starting transfers between devices: 4.76 us -> 3.21 us  [to_owner(): return lax.ppermute(v, ('y', 'x'), moves) if j else v]
    all_to_all x1, waiting for transfers between devices: 0.01 us -> 1.53 us  [spread(): return lax.all_to_all(total, 'x', 0, 0)]
  transfers between devices with their start and end apart: 20 -> 19, of which waited for: 11 -> 12; matrix products, arithmetic and copies ran while one was open for 0% -> 0% of each run, Pallas kernels for 6% -> 6%
where the time goes in v3:
time: 129 us
  waiting for transfers between devices  48.7 us (38%)
  starting transfers between devices  34.6 us (27%)
  Pallas kernels  21.5 us (17%)
  blocking collectives  20.6 us (16%)
  local copies, waits for them, and re-layouts  2.67 us (2%)
    ppermute x7, waiting for transfers between devices, shift_z(): return lax.ppermute(v, 'z', [(z, (z + s) % NZ) for z in range(NZ)])  24.9 us
    all_to_all x1, blocking collectives, on_device(): bmat = lax.all_to_all(bmat, ('z', 'x', 'c'), 0, 0, tiled=True)  20.6 us
    ppermute x6, waiting for transfers between devices, shift_y(): return lax.ppermute(v, 'y', [(y, (y + s) % NY) for y in range(NY)])  14.6 us
    ppermute x7, starting transfers between devices, shift_z(): return lax.ppermute(v, 'z', [(z, (z + s) % NZ) for z in range(NZ)])  14.3 us
    pallas_call x2, Pallas kernels, products(): pl.pallas_call(functools.partial(products_kernel, plan, len(f_arrays), le...  8.5 us
    ppermute x6, starting transfers between devices, shift_y(): return lax.ppermute(v, 'y', [(y, (y + s) % NY) for y in range(NY)])  8.33 us
    ppermute x3, waiting for transfers between devices, to_owner(): return lax.ppermute(v, ('y', 'x'), moves) if j else v  5.16 us
    ppermute x2, starting transfers between devices, swap_core(): return lax.ppermute(v, 'c', [(0, 1), (1, 0)])  4.63 us
  transfers between devices with their start and end apart: 19, of which 12 were waited for; matrix products, arithmetic and copies ran while one was open for 0% of the time, Pallas kernels for 6%

profile of v3, /device:TPU:1, one launch (start us, length us, event | category | flops | bytes accessed | tf_op | source)
XLA Modules:
  0.0 129.0 jit_solution(14261873447978441604)
XLA Ops:
  0.6 0.0 copy-start
  0.6 1.3 copy-done
  1.9 0.1 shard_map.68
  2.0 2.2 %collective-permute-start.7 = (bf16[2,2,48,1536]{3,2,1,0:T(8,128)(2,1)S(1)}, bf16[2,2,48,1536]{3,2,1,0:T(8,128)(2,1)S(1)}, u32[]{:S(2)}, u32[]{:S(2)}) collective-permute-start(bf16[2,2,48,1536]{3,2,1,0:T(8,128)(2,1)S(1)} %get-tuple-element.33.low_ref), channel_id=1, source_target_pairs={{0,8},{8,16},{16,24},{24,0},{1,9},{9,17},{17,25},{25,1},{2,10},{10... | collective-permute-start | bytes 1769480 | tf_op jit(solution)/shard_map/ppermute | solution.py:39
  4.2 1.5 %collective-permute-start.8 = (bf16[2,2,48,1536]{3,2,1,0:T(8,128)(2,1)S(1)}, bf16[2,2,48,1536]{3,2,1,0:T(8,128)(2,1)S(1)}, u32[]{:S(2)}, u32[]{:S(2)}) collective-permute-start(bf16[2,2,48,1536]{3,2,1,0:T(8,128)(2,1)S(1)} %get-tuple-element.34.high_ref), channel_id=1, source_target_pairs={{0,24},{8,0},{16,8},{24,16},{1,25},{9,1},{17,9},{25,17},{2,26},{10... | collective-permute-start | bytes 1769480 | tf_op jit(solution)/shard_map/ppermute | solution.py:39
  5.7 1.6 %collective-permute-start.1 = (bf16[1536,128]{1,0:T(8,128)(2,1)}, bf16[1536,128]{1,0:T(8,128)(2,1)S(1)}, u32[]{:S(2)}, u32[]{:S(2)}) collective-permute-start(bf16[1536,128]{1,0:T(8,128)(2,1)} %bitcast.13), channel_id=1, source_target_pairs={{0,32},{32,64},{64,96},{96,128},{128,160},{160,192},{192,224},{224... | collective-permute-start | bytes 1179656 | tf_op jit(solution)/shard_map/ppermute | solution.py:35
  7.4 3.9 %collective-permute-start = (bf16[1536,128]{1,0:T(8,128)(2,1)}, bf16[1536,128]{1,0:T(8,128)(2,1)S(1)}, u32[]{:S(2)}, u32[]{:S(2)}) collective-permute-start(bf16[1536,128]{1,0:T(8,128)(2,1)} %bitcast.14), channel_id=1, source_target_pairs={{0,224},{32,0},{64,32},{96,64},{128,96},{160,128},{192,160},{224,1... | collective-permute-start | bytes 1179656 | tf_op jit(solution)/shard_map/ppermute | solution.py:35
  11.3 8.6 %collective-permute-done.1.refs_2_.refs_7_.refs_5_ = bf16[1536,128]{1,0:T(8,128)(2,1)S(1)} collective-permute-done((bf16[1536,128]{1,0:T(8,128)(2,1)}, bf16[1536,128]{1,0:T(8,128)(2,1)S(1)}, u32[]{:S(2)}, u32[]{:S(2)}) %collective-permute-start.1) | collective-permute-done | bytes 393248 | tf_op jit(solution)/shard_map/ppermute | solution.py:35
  19.9 0.0 collective-permute-start.3
  19.9 1.6 %shard_map.70 = (bf16[4,2,48,1536]{3,2,1,0:T(8,128)(2,1)}, bf16[4,2,48,1536]{3,2,1,0:T(8,128)(2,1)}) custom-call(bf16[2,2,48,1536]{3,2,1,0:T(8,128)(2,1)S(1)} %get-tuple-element.33.low_ref, bf16[2,2,48,1536]{3,2,1,0:T(8,128)(2,1)S(1)} %get-tuple-element.34.high_ref, bf16[2,2,48,1536]{3,2,1,0:T(8,128)(2,1)S(1)} %collective-permute-done.7.left_ref.refs_1_, ...), custom_call_target="tpu_custom_call" | custom-call | flops 1 | bytes 1 | tf_op jit(solution)/shard_map/pallas_call | solution.py:82
  21.5 1.2 collective-permute-start.10
  22.7 0.3 collective-permute-start.9
  22.9 0.0 collective-permute-done.refs_1_.refs_6_.refs_4_
  22.9 5.2 %collective-permute-start.2 = (bf16[1536,128]{1,0:T(8,128)(2,1)S(1)}, bf16[1536,128]{1,0:T(8,128)(2,1)S(1)}, u32[]{:S(2)}, u32[]{:S(2)}) collective-permute-start(bf16[1536,128]{1,0:T(8,128)(2,1)S(1)} %collective-permute-done.refs_1_.refs_6_.refs_4_), channel_id=1, source_target_pairs={{0,224},{32,0},{64,32},{96,64},{128,96},{160,128},{192,160},{224,1... | collective-permute-start | bytes 1179656 | tf_op jit(solution)/shard_map/ppermute | solution.py:35
  28.1 2.0 %collective-permute-done.3.refs_4_.refs_9_.refs_7_ = bf16[1536,128]{1,0:T(8,128)(2,1)S(1)} collective-permute-done((bf16[1536,128]{1,0:T(8,128)(2,1)S(1)}, bf16[1536,128]{1,0:T(8,128)(2,1)S(1)}, u32[]{:S(2)}, u32[]{:S(2)}) %collective-permute-start.3) | collective-permute-done | bytes 393248 | tf_op jit(solution)/shard_map/ppermute | solution.py:35
  30.1 0.0 collective-permute-start.5
  30.1 4.5 %collective-permute-done.2.refs_3_.refs_8_.refs_6_ = bf16[1536,128]{1,0:T(8,128)(2,1)S(1)} collective-permute-done((bf16[1536,128]{1,0:T(8,128)(2,1)S(1)}, bf16[1536,128]{1,0:T(8,128)(2,1)S(1)}, u32[]{:S(2)}, u32[]{:S(2)}) %collective-permute-start.2) | collective-permute-done | bytes 393248 | tf_op jit(solution)/shard_map/ppermute | solution.py:35
  34.5 3.5 %collective-permute-start.4 = (bf16[1536,128]{1,0:T(8,128)(2,1)S(1)}, bf16[1536,128]{1,0:T(8,128)(2,1)}, u32[]{:S(2)}, u32[]{:S(2)}) collective-permute-start(bf16[1536,128]{1,0:T(8,128)(2,1)S(1)} %collective-permute-done.2.refs_3_.refs_8_.refs_6_), channel_id=1, source_target_pairs={{0,224},{32,0},{64,32},{96,64},{128,96},{160,128},{192,160},{224,1... | collective-permute-start | bytes 1179656 | tf_op jit(solution)/shard_map/ppermute | solution.py:35
  38.1 1.4 %collective-permute-done.5.refs_6_.refs_11_ = bf16[1536,128]{1,0:T(8,128)(2,1)S(1)} collective-permute-done((bf16[1536,128]{1,0:T(8,128)(2,1)S(1)}, bf16[1536,128]{1,0:T(8,128)(2,1)S(1)}, u32[]{:S(2)}, u32[]{:S(2)}) %collective-permute-start.5) | collective-permute-done | bytes 393248 | tf_op jit(solution)/shard_map/ppermute | solution.py:35
  39.5 0.1 pad_add_fusion.at_ref
  39.6 4.1 %collective-permute-done.4.refs_5_.refs_10_ = bf16[1536,128]{1,0:T(8,128)(2,1)} collective-permute-done((bf16[1536,128]{1,0:T(8,128)(2,1)S(1)}, bf16[1536,128]{1,0:T(8,128)(2,1)}, u32[]{:S(2)}, u32[]{:S(2)}) %collective-permute-start.4) | collective-permute-done | bytes 393248 | tf_op jit(solution)/shard_map/ppermute | solution.py:35
  43.7 4.4 %collective-permute-done.6.refs_7_.refs_12_ = bf16[1536,128]{1,0:T(8,128)(2,1)} collective-permute-done((bf16[1536,128]{1,0:T(8,128)(2,1)S(1)}, bf16[1536,128]{1,0:T(8,128)(2,1)}, u32[]{:S(2)}, u32[]{:S(2)}) %collective-permute-start.6) | collective-permute-done | bytes 393248 | tf_op jit(solution)/shard_map/ppermute | solution.py:35
  48.1 1.5 %shard_map.69.refs_0_ = bf16[192,1024]{1,0:T(8,128)(2,1)S(1)} custom-call(s32[4]{0:T(128)S(1)} %pad_add_fusion.at_ref, bf16[1536,128]{1,0:T(8,128)(2,1)S(1)} %bitcast.15, bf16[1536,128]{1,0:T(8,128)(2,1)S(1)} %collective-permute-done.refs_1_.refs_6_.refs_4_, bf16[1536,128]{1,0:T(8,128)(2,1)S(1)} %collective-permute-done.1.refs_2_.refs_7_.refs_5_, ...), custom_call_target="tpu_custom_call" | custom-call | flops 1 | bytes 1 | tf_op jit(solution)/shard_map/pallas_call | solution.py:292
  49.6 0.0 copy-start.3
  49.6 0.7 copy-done.3
  50.4 0.0 collective-permute-done.10.refs_4_
  50.4 5.8 %shard_map.71 = (f32[4,48,2816]{2,1,0:T(8,128)S(1)}, f32[4,48,2816]{2,1,0:T(8,128)S(1)}) custom-call(s32[4]{0:T(128)S(1)} %pad_add_fusion.at_ref, bf16[4,2,48,1536]{3,2,1,0:T(8,128)(2,1)S(1)} %bitcast.11, bf16[2,2,48,1536]{3,2,1,0:T(8,128)(2,1)S(1)} %collective-permute-done.7.left_ref.refs_1_, ...), custom_call_target="tpu_custom_call" | custom-call | flops 1 | bytes 1 | tf_op jit(solution)/shard_map/pallas_call | solution.py:161
  56.2 4.5 %collective-permute-start.11 = (f32[4,48,2816]{2,1,0:T(8,128)S(1)}, f32[4,48,2816]{2,1,0:T(8,128)S(1)}, u32[]{:S(2)}, u32[]{:S(2)}) collective-permute-start(f32[4,48,2816]{2,1,0:T(8,128)S(1)} %get-tuple-element.43), channel_id=1, source_target_pairs={{0,1},{1,0},{2,3},{3,2},{4,5},{5,4},{6,7},{7,6},{8,9},{9,8},{10,11... | collective-permute-start | bytes 6488072 | tf_op jit(solution)/shard_map/ppermute | solution.py:51
  60.7 2.7 %shard_map.72 = (f32[4,48,1280]{2,1,0:T(8,128)S(1)}, f32[4,48,1280]{2,1,0:T(8,128)S(1)}) custom-call(s32[4]{0:T(128)S(1)} %pad_add_fusion.at_ref, bf16[4,2,48,1536]{3,2,1,0:T(8,128)(2,1)S(1)} %bitcast.12, bf16[2,2,48,1536]{3,2,1,0:T(8,128)(2,1)S(1)} %collective-permute-done.7.left_ref.refs_1_, ...), custom_call_target="tpu_custom_call" | custom-call | flops 1 | bytes 1 | tf_op jit(solution)/shard_map/pallas_call | solution.py:161
  63.4 0.1 collective-permute-start.12
  63.5 2.5 %collective-permute-done.12.recv_ref = f32[4,48,1280]{2,1,0:T(8,128)S(1)} collective-permute-done((f32[4,48,1280]{2,1,0:T(8,128)S(1)}, f32[4,48,1280]{2,1,0:T(8,128)S(1)}, u32[]{:S(2)}, u32[]{:S(2)}) %collective-permute-start.12) | collective-permute-done | bytes 983072 | tf_op jit(solution)/shard_map/ppermute | solution.py:51
  66.1 0.9 shard_map.73.refs_0_
  66.9 2.6 %shard_map.74 = s16[4,48,4224]{2,1,0:T(8,128)(2,1)} custom-call(f32[4,48,2816]{2,1,0:T(8,128)S(1)} %get-tuple-element.42.keep_ref, f32[4,48,2816]{2,1,0:T(8,128)S(1)} %collective-permute-done.11.recv_ref, s16[4,48,1408]{2,1,0:T(8,128)(2,1)S(1)} %shard_map.73.refs_0_), custom_call_target="tpu_custom_call" | custom-call | flops 1 | bytes 1 | tf_op jit(solution)/shard_map/pallas_call | solution.py:122
  69.5 4.2 %all-to-all-start = ((s16[4,48,4224]{2,1,0:T(8,128)(2,1)}), s16[4,48,4224]{2,1,0:T(8,128)(2,1)S(1)}, u32[]{:S(2)}, u32[]{:S(2)}) async-start(s16[4,48,4224]{2,1,0:T(8,128)(2,1)} %shard_map.74), calls=%async_computation | async-start | bytes 3244032 | tf_op jit(solution)/shard_map/all_to_all | solution.py:362
  73.7 1.0 collective-permute-start.13
  74.7 9.1 %collective-permute-done.13.refs_1_ = bf16[192,1024]{1,0:T(8,128)(2,1)S(1)} collective-permute-done((bf16[192,1024]{1,0:T(8,128)(2,1)S(1)}, bf16[192,1024]{1,0:T(8,128)(2,1)S(1)}, u32[]{:S(2)}, u32[]{:S(2)}) %collective-permute-start.13) | collective-permute-done | bytes 393248 | tf_op jit(solution)/shard_map/ppermute | solution.py:39
  83.8 2.2 %collective-permute-start.14 = (bf16[192,1024]{1,0:T(8,128)(2,1)S(1)}, bf16[192,1024]{1,0:T(8,128)(2,1)S(1)}, u32[]{:S(2)}, u32[]{:S(2)}) collective-permute-start(bf16[192,1024]{1,0:T(8,128)(2,1)S(1)} %collective-permute-done.13.refs_1_), channel_id=1, source_target_pairs={{0,24},{8,0},{16,8},{24,16},{1,25},{9,1},{17,9},{25,17},{2,26},{10... | collective-permute-start | bytes 1179656 | tf_op jit(solution)/shard_map/ppermute | solution.py:39
  85.9 1.5 %shard_map.75 = (f32[192,128]{1,0:T(8,128)S(1)}, f32[1,1024]{1,0:T(1,128)S(1)}) custom-call(s32[4]{0:T(128)S(1)} %pad_add_fusion.at_ref, s32[32]{0:T(128)S(1)} %copy-done.5, s32[32]{0:T(128)S(1)} %copy-done.6, s32[32]{0:T(128)S(1)} %copy-done.7), custom_call_target="tpu_custom_call" | custom-call | flops 1 | bytes 1 | tf_op jit(solution)/shard_map/pallas_call | solution.py:195
  87.4 5.4 %collective-permute-done.14.refs_2_ = bf16[192,1024]{1,0:T(8,128)(2,1)S(1)} collective-permute-done((bf16[192,1024]{1,0:T(8,128)(2,1)S(1)}, bf16[192,1024]{1,0:T(8,128)(2,1)S(1)}, u32[]{:S(2)}, u32[]{:S(2)}) %collective-permute-start.14) | collective-permute-done | bytes 393248 | tf_op jit(solution)/shard_map/ppermute | solution.py:39
  92.9 1.5 %all-to-all-done.total_ref = s16[4,48,4224]{2,1,0:T(8,128)(2,1)S(1)} async-done(((s16[4,48,4224]{2,1,0:T(8,128)(2,1)}), s16[4,48,4224]{2,1,0:T(8,128)(2,1)S(1)}, u32[]{:S(2)}, u32[]{:S(2)}) %all-to-all-start) | async-done | bytes 1622048 | tf_op jit(solution)/shard_map/all_to_all | solution.py:362
  94.4 3.5 %shard_map.76 = (bf16[64,1024]{1,0:T(8,128)(2,1)S(1)}, bf16[64,1024]{1,0:T(8,128)(2,1)S(1)}, bf16[64,1024]{1,0:T(8,128)(2,1)S(1)}, bf16[64,1024]{1,0:T(8,128)(2,1)S(1)}) custom-call(s32[4]{0:T(128)S(1)} %pad_add_fusion.at_ref, s16[4,48,4224]{2,1,0:T(8,128)(2,1)S(1)} %all-to-all-done.total_ref, f32[1,1024]{1,0:T(1,128)S(1)} %get-tuple-element.49.mask_ref, ...), custom_call_target="tpu_custom_call" | custom-call | flops 1 | bytes 1 | tf_op jit(solution)/shard_map/pallas_call | solution.py:259
  98.0 1.9 %collective-permute-start.15 = (bf16[64,1024]{1,0:T(8,128)(2,1)S(1)}, bf16[64,1024]{1,0:T(8,128)(2,1)S(1)}, u32[]{:S(2)}, u32[]{:S(2)}) collective-permute-start(bf16[64,1024]{1,0:T(8,128)(2,1)S(1)} %get-tuple-element.53), channel_id=1, source_target_pairs={{0,24},{2,26},{4,12},{6,14},{8,0},{10,2},{12,20},{14,22},{16,8},{1... | collective-permute-start | bytes 393224 | tf_op jit(solution)/shard_map/ppermute | solution.py:47
  99.9 1.3 collective-permute-start.17
  101.2 0.7 collective-permute-done.15.refs_1_
  101.9 4.5 %collective-permute-done.16.refs_2_ = bf16[64,1024]{1,0:T(8,128)(2,1)S(1)} collective-permute-done((bf16[64,1024]{1,0:T(8,128)(2,1)S(1)}, bf16[64,1024]{1,0:T(8,128)(2,1)S(1)}, u32[]{:S(2)}, u32[]{:S(2)}) %collective-permute-start.16) | collective-permute-done | bytes 131104 | tf_op jit(solution)/shard_map/ppermute | solution.py:47
  106.3 1.4 %shard_map.77 = (bf16[32,48,128]{2,1,0:T(8,128)(2,1)}, f32[64,128]{1,0:T(8,128)S(1)}) custom-call(s32[4]{0:T(128)S(1)} %pad_add_fusion.at_ref, bf16[64,1024]{1,0:T(8,128)(2,1)S(1)} %get-tuple-element.52.refs_0_, bf16[64,1024]{1,0:T(8,128)(2,1)S(1)} %collective-permute-done.15.refs_1_, bf16[64,1024]{1,0:T(8,128)(2,1)S(1)} %collective-permute-done.16.refs_2_, ...), custom_call_target="tpu_custom_call" | custom-call | flops 1 | bytes 1 | tf_op jit(solution)/shard_map/pallas_call | solution.py:319
  107.7 20.6 %all_to_all.17 = f32[64,1,128]{2,1,0:T(1,128)S(1)} all-to-all(f32[64,1,128]{2,1,0:T(1,128)S(1)} %bitcast.18), channel_id=1, replica_groups=mesh['z'=8,'y'=4,'x'=4,'c'=2] {'z','x','c'}, dimensions={0} | all-to-all | bytes 65536 | tf_op jit(solution)/shard_map/all_to_all | solution.py:381
  128.4 0.6 reshape.13
  (20 shorter events, 0.1 us)
Async XLA Ops:
  0.6 1.3 copy-start
  1.9 46.2 %copy-start.2 = (bf16[1,1536,128]{2,1,0:T(8,128)(2,1)S(1)}, bf16[1,1536,128]{2,1,0:T(8,128)(2,1)}, u32[]{:S(2)}) copy-start(bf16[1,1536,128]{2,1,0:T(8,128)(2,1)} %param.5) | copy-start | bytes 1179652
  2.0 17.9 %collective-permute-start.7 = (bf16[2,2,48,1536]{3,2,1,0:T(8,128)(2,1)S(1)}, bf16[2,2,48,1536]{3,2,1,0:T(8,128)(2,1)S(1)}, u32[]{:S(2)}, u32[]{:S(2)}) collective-permute-start(bf16[2,2,48,1536]{3,2,1,0:T(8,128)(2,1)S(1)} %get-tuple-element.33.low_ref), channel_id=1, source_target_pairs={{0,8},{8,16},{16,24},{24,0},{1,9},{9,17},{17,25},{25,1},{2,10},{10... | collective-permute-start | bytes 1769480 | tf_op jit(solution)/shard_map/ppermute | solution.py:39
  4.2 15.7 %collective-permute-start.8 = (bf16[2,2,48,1536]{3,2,1,0:T(8,128)(2,1)S(1)}, bf16[2,2,48,1536]{3,2,1,0:T(8,128)(2,1)S(1)}, u32[]{:S(2)}, u32[]{:S(2)}) collective-permute-start(bf16[2,2,48,1536]{3,2,1,0:T(8,128)(2,1)S(1)} %get-tuple-element.34.high_ref), channel_id=1, source_target_pairs={{0,24},{8,0},{16,8},{24,16},{1,25},{9,1},{17,9},{25,17},{2,26},{10... | collective-permute-start | bytes 1769480 | tf_op jit(solution)/shard_map/ppermute | solution.py:39
  5.7 14.2 %collective-permute-start.1 = (bf16[1536,128]{1,0:T(8,128)(2,1)}, bf16[1536,128]{1,0:T(8,128)(2,1)S(1)}, u32[]{:S(2)}, u32[]{:S(2)}) collective-permute-start(bf16[1536,128]{1,0:T(8,128)(2,1)} %bitcast.13), channel_id=1, source_target_pairs={{0,32},{32,64},{64,96},{96,128},{128,160},{160,192},{192,224},{224... | collective-permute-start | bytes 1179656 | tf_op jit(solution)/shard_map/ppermute | solution.py:35
  7.4 15.6 %collective-permute-start = (bf16[1536,128]{1,0:T(8,128)(2,1)}, bf16[1536,128]{1,0:T(8,128)(2,1)S(1)}, u32[]{:S(2)}, u32[]{:S(2)}) collective-permute-start(bf16[1536,128]{1,0:T(8,128)(2,1)} %bitcast.14), channel_id=1, source_target_pairs={{0,224},{32,0},{64,32},{96,64},{128,96},{160,128},{192,160},{224,1... | collective-permute-start | bytes 1179656 | tf_op jit(solution)/shard_map/ppermute | solution.py:35
  19.9 10.2 %collective-permute-start.3 = (bf16[1536,128]{1,0:T(8,128)(2,1)S(1)}, bf16[1536,128]{1,0:T(8,128)(2,1)S(1)}, u32[]{:S(2)}, u32[]{:S(2)}) collective-permute-start(bf16[1536,128]{1,0:T(8,128)(2,1)S(1)} %collective-permute-done.1.refs_2_.refs_7_.refs_5_), channel_id=1, source_target_pairs={{0,32},{32,64},{64,96},{96,128},{128,160},{160,192},{192,224},{224... | collective-permute-start | bytes 1179656 | tf_op jit(solution)/shard_map/ppermute | solution.py:35
  21.5 28.9 %collective-permute-start.10 = (bf16[4,2,48,1536]{3,2,1,0:T(8,128)(2,1)}, bf16[4,2,48,1536]{3,2,1,0:T(8,128)(2,1)}, u32[]{:S(2)}, u32[]{:S(2)}) collective-permute-start(bf16[4,2,48,1536]{3,2,1,0:T(8,128)(2,1)} %get-tuple-element.36), channel_id=1, source_target_pairs={{0,24},{8,0},{16,8},{24,16},{1,25},{9,1},{17,9},{25,17},{2,26},{10... | collective-permute-start | bytes 3538952 | tf_op jit(solution)/shard_map/ppermute | solution.py:39
  22.7 27.7 %collective-permute-start.9 = (bf16[4,2,48,1536]{3,2,1,0:T(8,128)(2,1)}, bf16[4,2,48,1536]{3,2,1,0:T(8,128)(2,1)}, u32[]{:S(2)}, u32[]{:S(2)}) collective-permute-start(bf16[4,2,48,1536]{3,2,1,0:T(8,128)(2,1)} %get-tuple-element.35), channel_id=1, source_target_pairs={{0,8},{8,16},{16,24},{24,0},{1,9},{9,17},{17,25},{25,1},{2,10},{10... | collective-permute-start | bytes 3538952 | tf_op jit(solution)/shard_map/ppermute | solution.py:39
  22.9 11.6 %collective-permute-start.2 = (bf16[1536,128]{1,0:T(8,128)(2,1)S(1)}, bf16[1536,128]{1,0:T(8,128)(2,1)S(1)}, u32[]{:S(2)}, u32[]{:S(2)}) collective-permute-start(bf16[1536,128]{1,0:T(8,128)(2,1)S(1)} %collective-permute-done.refs_1_.refs_6_.refs_4_), channel_id=1, source_target_pairs={{0,224},{32,0},{64,32},{96,64},{128,96},{160,128},{192,160},{224,1... | collective-permute-start | bytes 1179656 | tf_op jit(solution)/shard_map/ppermute | solution.py:35
  30.1 9.4 %collective-permute-start.5 = (bf16[1536,128]{1,0:T(8,128)(2,1)S(1)}, bf16[1536,128]{1,0:T(8,128)(2,1)S(1)}, u32[]{:S(2)}, u32[]{:S(2)}) collective-permute-start(bf16[1536,128]{1,0:T(8,128)(2,1)S(1)} %collective-permute-done.3.refs_4_.refs_9_.refs_7_), channel_id=1, source_target_pairs={{0,32},{32,64},{64,96},{96,128},{128,160},{160,192},{192,224},{224... | collective-permute-start | bytes 1179656 | tf_op jit(solution)/shard_map/ppermute | solution.py:35
  34.5 9.1 %collective-permute-start.4 = (bf16[1536,128]{1,0:T(8,128)(2,1)S(1)}, bf16[1536,128]{1,0:T(8,128)(2,1)}, u32[]{:S(2)}, u32[]{:S(2)}) collective-permute-start(bf16[1536,128]{1,0:T(8,128)(2,1)S(1)} %collective-permute-done.2.refs_3_.refs_8_.refs_6_), channel_id=1, source_target_pairs={{0,224},{32,0},{64,32},{96,64},{128,96},{160,128},{192,160},{224,1... | collective-permute-start | bytes 1179656 | tf_op jit(solution)/shard_map/ppermute | solution.py:35
  39.5 8.6 %collective-permute-start.6 = (bf16[1536,128]{1,0:T(8,128)(2,1)S(1)}, bf16[1536,128]{1,0:T(8,128)(2,1)}, u32[]{:S(2)}, u32[]{:S(2)}) collective-permute-start(bf16[1536,128]{1,0:T(8,128)(2,1)S(1)} %collective-permute-done.5.refs_6_.refs_11_), channel_id=1, source_target_pairs={{0,32},{32,64},{64,96},{96,128},{128,160},{160,192},{192,224},{224... | collective-permute-start | bytes 1179656 | tf_op jit(solution)/shard_map/ppermute | solution.py:35
  39.6 10.8 %copy-start.1 = (bf16[8,1,48,1536]{3,2,1,0:T(8,128)(2,1)S(1)}, bf16[8,1,48,1536]{3,2,1,0:T(8,128)(2,1)}, u32[]{:S(2)}) copy-start(bf16[8,1,48,1536]{3,2,1,0:T(8,128)(2,1)} %param.6) | copy-start | bytes 3538948
  49.6 0.7 copy-start.3
  56.2 10.7 %collective-permute-start.11 = (f32[4,48,2816]{2,1,0:T(8,128)S(1)}, f32[4,48,2816]{2,1,0:T(8,128)S(1)}, u32[]{:S(2)}, u32[]{:S(2)}) collective-permute-start(f32[4,48,2816]{2,1,0:T(8,128)S(1)} %get-tuple-element.43), channel_id=1, source_target_pairs={{0,1},{1,0},{2,3},{3,2},{4,5},{5,4},{6,7},{7,6},{8,9},{9,8},{10,11... | collective-permute-start | bytes 6488072 | tf_op jit(solution)/shard_map/ppermute | solution.py:51
  63.4 2.7 %collective-permute-start.12 = (f32[4,48,1280]{2,1,0:T(8,128)S(1)}, f32[4,48,1280]{2,1,0:T(8,128)S(1)}, u32[]{:S(2)}, u32[]{:S(2)}) collective-permute-start(f32[4,48,1280]{2,1,0:T(8,128)S(1)} %get-tuple-element.48), channel_id=1, source_target_pairs={{0,1},{1,0},{2,3},{3,2},{4,5},{5,4},{6,7},{7,6},{8,9},{9,8},{10,11... | collective-permute-start | bytes 2949128 | tf_op jit(solution)/shard_map/ppermute | solution.py:51
  69.5 4.2 %copy-start.4 = (bf16[192,1024]{1,0:T(8,128)(2,1)S(1)}, bf16[192,1024]{1,0:T(8,128)(2,1)}, u32[]{:S(2)}) copy-start(bf16[192,1024]{1,0:T(8,128)(2,1)} %copy-done.3) | copy-start | bytes 1179652
  69.5 16.4 %copy-start.5 = (s32[32]{0:T(128)S(1)}, s32[32]{0:T(128)}, u32[]{:S(2)}) copy-start(s32[32]{0:T(128)} %pair_ref.1) | copy-start | bytes 388
  69.5 16.4 %copy-start.6 = (s32[32]{0:T(128)S(1)}, s32[32]{0:T(128)}, u32[]{:S(2)}) copy-start(s32[32]{0:T(128)} %block_ref.1) | copy-start | bytes 388
  69.5 16.4 %copy-start.7 = (s32[32]{0:T(128)S(1)}, s32[32]{0:T(128)}, u32[]{:S(2)}) copy-start(s32[32]{0:T(128)} %live_ref.1) | copy-start | bytes 388
  69.5 24.9 %all-to-all-start = ((s16[4,48,4224]{2,1,0:T(8,128)(2,1)}), s16[4,48,4224]{2,1,0:T(8,128)(2,1)S(1)}, u32[]{:S(2)}, u32[]{:S(2)}) async-start(s16[4,48,4224]{2,1,0:T(8,128)(2,1)} %shard_map.74), calls=%async_computation | async-start | bytes 3244032 | tf_op jit(solution)/shard_map/all_to_all | solution.py:362
  73.7 10.1 %collective-permute-start.13 = (bf16[192,1024]{1,0:T(8,128)(2,1)S(1)}, bf16[192,1024]{1,0:T(8,128)(2,1)S(1)}, u32[]{:S(2)}, u32[]{:S(2)}) collective-permute-start(bf16[192,1024]{1,0:T(8,128)(2,1)S(1)} %copy-done.4), channel_id=1, source_target_pairs={{0,24},{8,0},{16,8},{24,16},{1,25},{9,1},{17,9},{25,17},{2,26},{10... | collective-permute-start | bytes 1179656 | tf_op jit(solution)/shard_map/ppermute | solution.py:39
  83.8 9.1 %collective-permute-start.14 = (bf16[192,1024]{1,0:T(8,128)(2,1)S(1)}, bf16[192,1024]{1,0:T(8,128)(2,1)S(1)}, u32[]{:S(2)}, u32[]{:S(2)}) collective-permute-start(bf16[192,1024]{1,0:T(8,128)(2,1)S(1)} %collective-permute-done.13.refs_1_), channel_id=1, source_target_pairs={{0,24},{8,0},{16,8},{24,16},{1,25},{9,1},{17,9},{25,17},{2,26},{10... | collective-permute-start | bytes 1179656 | tf_op jit(solution)/shard_map/ppermute | solution.py:39
  98.0 3.9 %collective-permute-start.15 = (bf16[64,1024]{1,0:T(8,128)(2,1)S(1)}, bf16[64,1024]{1,0:T(8,128)(2,1)S(1)}, u32[]{:S(2)}, u32[]{:S(2)}) collective-permute-start(bf16[64,1024]{1,0:T(8,128)(2,1)S(1)} %get-tuple-element.53), channel_id=1, source_target_pairs={{0,24},{2,26},{4,12},{6,14},{8,0},{10,2},{12,20},{14,22},{16,8},{1... | collective-permute-start | bytes 393224 | tf_op jit(solution)/shard_map/ppermute | solution.py:47
  99.9 6.4 %collective-permute-start.16 = (bf16[64,1024]{1,0:T(8,128)(2,1)S(1)}, bf16[64,1024]{1,0:T(8,128)(2,1)S(1)}, u32[]{:S(2)}, u32[]{:S(2)}) collective-permute-start(bf16[64,1024]{1,0:T(8,128)(2,1)S(1)} %get-tuple-element.54), channel_id=1, source_target_pairs={{0,8},{2,10},{4,28},{6,30},{8,16},{10,18},{12,4},{14,6},{16,24},{1... | collective-permute-start | bytes 393224 | tf_op jit(solution)/shard_map/ppermute | solution.py:47
  99.9 6.4 %collective-permute-start.17 = (bf16[64,1024]{1,0:T(8,128)(2,1)S(1)}, bf16[64,1024]{1,0:T(8,128)(2,1)S(1)}, u32[]{:S(2)}, u32[]{:S(2)}) collective-permute-start(bf16[64,1024]{1,0:T(8,128)(2,1)S(1)} %get-tuple-element.55), channel_id=1, source_target_pairs={{0,16},{2,18},{4,20},{6,22},{8,24},{10,26},{12,28},{14,30},{16,0},... | collective-permute-start | bytes 393224 | tf_op jit(solution)/shard_map/ppermute | solution.py:47

commit v4 on v3

--- a/solution.py
+++ b/solution.py
@@ -69,12 +69,19 @@
     )(own)
 
 
-def join_kernel(low_ref, high_ref, left_ref, right_ref, to_right_ref, to_left_ref):
+def join_kernel(low_ref, high_ref, left_ref, right_ref, to_right_ref, to_left_ref, arrived):
     half = low_ref.shape[0]
-    to_right_ref[:half] = left_ref[...]
-    to_right_ref[half:] = high_ref[...]
-    to_left_ref[:half] = low_ref[...]
-    to_left_ref[half:] = right_ref[...]
+    moves = [
+        (left_ref, to_right_ref.at[:half]),
+        (right_ref, to_left_ref.at[half:]),
+        (high_ref, to_right_ref.at[half:]),
+        (low_ref, to_left_ref.at[:half]),
+    ]
+    copies = [pltpu.make_async_copy(a, b, arrived.at[i]) for i, (a, b) in enumerate(moves)]
+    for copy in copies:
+        copy.start()
+    for copy in copies:
+        copy.wait()
 
 
 def join(low, high, left, right):
@@ -82,9 +89,10 @@
     return pl.pallas_call(
         join_kernel,
         out_shape=[whole, whole],
-        in_specs=[VMEM] * 4,
-        out_specs=[VMEM] * 2,
-        compiler_params=pltpu.CompilerParams(vmem_limit_bytes=12 * 2**20),
+        in_specs=[ANY] * 4,
+        out_specs=[ANY] * 2,
+        scratch_shapes=[pltpu.SemaphoreType.DMA((4,))],
+        compiler_params=pltpu.CompilerParams(vmem_limit_bytes=4 * 2**20),
         cost_estimate=CHEAP,
     )(low, high, left, right)
 
@@ -103,7 +111,7 @@
     for u in range(total // columns):
         span = slice(u * columns, (u + 1) * columns)
         value = keep_ref[0, :, span] + recv_ref[0, :, span]
-        top = jnp.maximum(jnp.max(jnp.abs(value), axis=1, keepdims=True), 2.0**-100)
+        top = jnp.maximum(jnp.max(jnp.abs(value), axis=1, keepdims=True), 2.0**-110)
         power = jnp.ceil(jnp.log2(top)) - 15.0
         scaled = jnp.clip(jnp.round(value * jnp.exp2(-power)), -32767.0, 32767.0)
         out_ref[0, :, at + u * columns : at + (u + 1) * columns] = scaled.astype(jnp.int32).astype(jnp.int16)
@@ -207,22 +215,17 @@
 
 def finish_kernel(plan, n_rows, at_ref, total_ref, mask_ref, weight_ref, *refs):
     row_refs, done_refs = refs[:n_rows], refs[n_rows : n_rows + NY]
-    held, arrived, dots, made = refs[n_rows + NY :]
-    n, width, _ = held.shape
+    dots, made = refs[n_rows + NY :]
+    n, width, _ = total_ref.shape
     columns = dots.shape[1]
-    copies = [pltpu.make_async_copy(total_ref.at[t], held.at[t], arrived.at[t]) for t in range(n)]
-    for copy in copies:
-        copy.start()
-    for copy in copies:
-        copy.wait()
-    units = held.shape[2] - columns
-    scales = [jnp.exp2(held[t, :, units:].astype(jnp.int32).astype(jnp.float32)) for t in range(n)]
+    units = total_ref.shape[2] - columns
+    scales = [jnp.exp2(total_ref[t, :, units:].astype(jnp.int32).astype(jnp.float32)) for t in range(n)]
     u = 0
     for j, es in plan:
         for e in es:
             value = 0.0
             for t in range(n):
-                term = held[t, :, u * columns : (u + 1) * columns].astype(jnp.int32).astype(jnp.float32)
+                term = total_ref[t, :, u * columns : (u + 1) * columns].astype(jnp.int32).astype(jnp.float32)
                 value = value + term * scales[t][:, u : u + 1]
             value = value * mask_ref[:, e * columns : (e + 1) * columns]
             value = value.astype(jnp.bfloat16)
@@ -259,11 +262,9 @@
     return pl.pallas_call(
         functools.partial(finish_kernel, plan, len(rows)),
         out_shape=[done] * NY,
-        in_specs=[SMEM, ANY] + [VMEM] * (2 + len(rows)),
+        in_specs=[SMEM] + [VMEM] * (3 + len(rows)),
         out_specs=[VMEM] * NY,
         scratch_shapes=[
-            pltpu.VMEM(total.shape, total.dtype),
-            pltpu.SemaphoreType.DMA((total.shape[0],)),
             pltpu.VMEM((weight.shape[0], columns), jnp.float32),
             pltpu.VMEM((NY, total.shape[1], NZ * columns), jnp.float32),
         ],

time: 129 us -> 128 us (level)
  no operation moved by 1% of the time
where the time goes in v4:
time: 128 us
  waiting for transfers between devices  48.8 us (38%)
  starting transfers between devices  34.6 us (27%)
  blocking collectives  20.6 us (16%)
  Pallas kernels  20.5 us (16%)
  local copies, waits for them, and re-layouts  2.67 us (2%)
    ppermute x7, waiting for transfers between devices, shift_z(): return lax.ppermute(v, 'z', [(z, (z + s) % NZ) for z in range(NZ)])  25 us
    all_to_all x1, blocking collectives, on_device(): bmat = lax.all_to_all(bmat, ('z', 'x', 'c'), 0, 0, tiled=True)  20.6 us
    ppermute x6, waiting for transfers between devices, shift_y(): return lax.ppermute(v, 'y', [(y, (y + s) % NY) for y in range(NY)])  14.6 us
    ppermute x7, starting transfers between devices, shift_z(): return lax.ppermute(v, 'z', [(z, (z + s) % NZ) for z in range(NZ)])  14.3 us
    pallas_call x2, Pallas kernels, products(): pl.pallas_call(functools.partial(products_kernel, plan, len(f_arrays), le...  8.5 us
    ppermute x6, starting transfers between devices, shift_y(): return lax.ppermute(v, 'y', [(y, (y + s) % NY) for y in range(NY)])  8.36 us
    ppermute x3, waiting for transfers between devices, to_owner(): return lax.ppermute(v, ('y', 'x'), moves) if j else v  5.16 us
    ppermute x2, starting transfers between devices, swap_core(): return lax.ppermute(v, 'c', [(0, 1), (1, 0)])  4.63 us
  transfers between devices with their start and end apart: 19, of which 12 were waited for; matrix products, arithmetic and copies ran while one was open for 0% of the time, Pallas kernels for 6%

profile of v4, /device:TPU:1, one launch (start us, length us, event | category | flops | bytes accessed | tf_op | source)
XLA Modules:
  0.0 128.1 jit_solution(438048114995279211)
XLA Ops:
  0.6 0.0 copy-start
  0.6 1.3 copy-done
  1.9 0.1 shard_map.68
  2.0 2.2 %collective-permute-start.7 = (bf16[2,2,48,1536]{3,2,1,0:T(8,128)(2,1)S(1)}, bf16[2,2,48,1536]{3,2,1,0:T(8,128)(2,1)S(1)}, u32[]{:S(2)}, u32[]{:S(2)}) collective-permute-start(bf16[2,2,48,1536]{3,2,1,0:T(8,128)(2,1)S(1)} %get-tuple-element.33.low_ref), channel_id=1, source_target_pairs={{0,8},{8,16},{16,24},{24,0},{1,9},{9,17},{17,25},{25,1},{2,10},{10... | collective-permute-start | bytes 1769480 | tf_op jit(solution)/shard_map/ppermute | solution.py:39
  4.2 1.5 %collective-permute-start.8 = (bf16[2,2,48,1536]{3,2,1,0:T(8,128)(2,1)S(1)}, bf16[2,2,48,1536]{3,2,1,0:T(8,128)(2,1)S(1)}, u32[]{:S(2)}, u32[]{:S(2)}) collective-permute-start(bf16[2,2,48,1536]{3,2,1,0:T(8,128)(2,1)S(1)} %get-tuple-element.34.high_ref), channel_id=1, source_target_pairs={{0,24},{8,0},{16,8},{24,16},{1,25},{9,1},{17,9},{25,17},{2,26},{10... | collective-permute-start | bytes 1769480 | tf_op jit(solution)/shard_map/ppermute | solution.py:39
  5.7 1.6 %collective-permute-start.1 = (bf16[1536,128]{1,0:T(8,128)(2,1)}, bf16[1536,128]{1,0:T(8,128)(2,1)S(1)}, u32[]{:S(2)}, u32[]{:S(2)}) collective-permute-start(bf16[1536,128]{1,0:T(8,128)(2,1)} %bitcast.13), channel_id=1, source_target_pairs={{0,32},{32,64},{64,96},{96,128},{128,160},{160,192},{192,224},{224... | collective-permute-start | bytes 1179656 | tf_op jit(solution)/shard_map/ppermute | solution.py:35
  7.4 3.9 %collective-permute-start = (bf16[1536,128]{1,0:T(8,128)(2,1)}, bf16[1536,128]{1,0:T(8,128)(2,1)S(1)}, u32[]{:S(2)}, u32[]{:S(2)}) collective-permute-start(bf16[1536,128]{1,0:T(8,128)(2,1)} %bitcast.14), channel_id=1, source_target_pairs={{0,224},{32,0},{64,32},{96,64},{128,96},{160,128},{192,160},{224,1... | collective-permute-start | bytes 1179656 | tf_op jit(solution)/shard_map/ppermute | solution.py:35
  11.3 8.6 %collective-permute-done.1.refs_2_.refs_7_.refs_5_ = bf16[1536,128]{1,0:T(8,128)(2,1)S(1)} collective-permute-done((bf16[1536,128]{1,0:T(8,128)(2,1)}, bf16[1536,128]{1,0:T(8,128)(2,1)S(1)}, u32[]{:S(2)}, u32[]{:S(2)}) %collective-permute-start.1) | collective-permute-done | bytes 393248 | tf_op jit(solution)/shard_map/ppermute | solution.py:35
  19.9 0.0 collective-permute-start.3
  19.9 1.5 %shard_map.70 = (bf16[4,2,48,1536]{3,2,1,0:T(8,128)(2,1)}, bf16[4,2,48,1536]{3,2,1,0:T(8,128)(2,1)}) custom-call(bf16[2,2,48,1536]{3,2,1,0:T(8,128)(2,1)S(1)} %get-tuple-element.33.low_ref, bf16[2,2,48,1536]{3,2,1,0:T(8,128)(2,1)S(1)} %get-tuple-element.34.high_ref, bf16[2,2,48,1536]{3,2,1,0:T(8,128)(2,1)S(1)} %collective-permute-done.7.left_ref.refs_1_, ...), custom_call_target="tpu_custom_call" | custom-call | flops 1 | bytes 1 | tf_op jit(solution)/shard_map/pallas_call | solution.py:89
  21.4 1.3 %collective-permute-start.10 = (bf16[4,2,48,1536]{3,2,1,0:T(8,128)(2,1)}, bf16[4,2,48,1536]{3,2,1,0:T(8,128)(2,1)}, u32[]{:S(2)}, u32[]{:S(2)}) collective-permute-start(bf16[4,2,48,1536]{3,2,1,0:T(8,128)(2,1)} %get-tuple-element.36), channel_id=1, source_target_pairs={{0,24},{8,0},{16,8},{24,16},{1,25},{9,1},{17,9},{25,17},{2,26},{10... | collective-permute-start | bytes 3538952 | tf_op jit(solution)/shard_map/ppermute | solution.py:39
  22.6 0.3 collective-permute-start.9
  22.9 0.0 collective-permute-done.refs_1_.refs_6_.refs_4_
  22.9 5.2 %collective-permute-start.2 = (bf16[1536,128]{1,0:T(8,128)(2,1)S(1)}, bf16[1536,128]{1,0:T(8,128)(2,1)S(1)}, u32[]{:S(2)}, u32[]{:S(2)}) collective-permute-start(bf16[1536,128]{1,0:T(8,128)(2,1)S(1)} %collective-permute-done.refs_1_.refs_6_.refs_4_), channel_id=1, source_target_pairs={{0,224},{32,0},{64,32},{96,64},{128,96},{160,128},{192,160},{224,1... | collective-permute-start | bytes 1179656 | tf_op jit(solution)/shard_map/ppermute | solution.py:35
  28.1 2.0 %collective-permute-done.3.refs_4_.refs_9_.refs_7_ = bf16[1536,128]{1,0:T(8,128)(2,1)S(1)} collective-permute-done((bf16[1536,128]{1,0:T(8,128)(2,1)S(1)}, bf16[1536,128]{1,0:T(8,128)(2,1)S(1)}, u32[]{:S(2)}, u32[]{:S(2)}) %collective-permute-start.3) | collective-permute-done | bytes 393248 | tf_op jit(solution)/shard_map/ppermute | solution.py:35
  30.1 0.0 collective-permute-start.5
  30.1 4.4 %collective-permute-done.2.refs_3_.refs_8_.refs_6_ = bf16[1536,128]{1,0:T(8,128)(2,1)S(1)} collective-permute-done((bf16[1536,128]{1,0:T(8,128)(2,1)S(1)}, bf16[1536,128]{1,0:T(8,128)(2,1)S(1)}, u32[]{:S(2)}, u32[]{:S(2)}) %collective-permute-start.2) | collective-permute-done | bytes 393248 | tf_op jit(solution)/shard_map/ppermute | solution.py:35
  34.5 3.5 %collective-permute-start.4 = (bf16[1536,128]{1,0:T(8,128)(2,1)S(1)}, bf16[1536,128]{1,0:T(8,128)(2,1)}, u32[]{:S(2)}, u32[]{:S(2)}) collective-permute-start(bf16[1536,128]{1,0:T(8,128)(2,1)S(1)} %collective-permute-done.2.refs_3_.refs_8_.refs_6_), channel_id=1, source_target_pairs={{0,224},{32,0},{64,32},{96,64},{128,96},{160,128},{192,160},{224,1... | collective-permute-start | bytes 1179656 | tf_op jit(solution)/shard_map/ppermute | solution.py:35
  38.0 1.5 %collective-permute-done.5.refs_6_.refs_11_ = bf16[1536,128]{1,0:T(8,128)(2,1)S(1)} collective-permute-done((bf16[1536,128]{1,0:T(8,128)(2,1)S(1)}, bf16[1536,128]{1,0:T(8,128)(2,1)S(1)}, u32[]{:S(2)}, u32[]{:S(2)}) %collective-permute-start.5) | collective-permute-done | bytes 393248 | tf_op jit(solution)/shard_map/ppermute | solution.py:35
  39.5 0.1 pad_add_fusion.at_ref
  39.6 4.1 %collective-permute-done.4.refs_5_.refs_10_ = bf16[1536,128]{1,0:T(8,128)(2,1)} collective-permute-done((bf16[1536,128]{1,0:T(8,128)(2,1)S(1)}, bf16[1536,128]{1,0:T(8,128)(2,1)}, u32[]{:S(2)}, u32[]{:S(2)}) %collective-permute-start.4) | collective-permute-done | bytes 393248 | tf_op jit(solution)/shard_map/ppermute | solution.py:35
  43.6 4.4 %collective-permute-done.6.refs_7_.refs_12_ = bf16[1536,128]{1,0:T(8,128)(2,1)} collective-permute-done((bf16[1536,128]{1,0:T(8,128)(2,1)S(1)}, bf16[1536,128]{1,0:T(8,128)(2,1)}, u32[]{:S(2)}, u32[]{:S(2)}) %collective-permute-start.6) | collective-permute-done | bytes 393248 | tf_op jit(solution)/shard_map/ppermute | solution.py:35
  48.1 1.5 %shard_map.69.refs_0_ = bf16[192,1024]{1,0:T(8,128)(2,1)S(1)} custom-call(s32[4]{0:T(128)S(1)} %pad_add_fusion.at_ref, bf16[1536,128]{1,0:T(8,128)(2,1)S(1)} %bitcast.15, bf16[1536,128]{1,0:T(8,128)(2,1)S(1)} %collective-permute-done.refs_1_.refs_6_.refs_4_, bf16[1536,128]{1,0:T(8,128)(2,1)S(1)} %collective-permute-done.1.refs_2_.refs_7_.refs_5_, ...), custom_call_target="tpu_custom_call" | custom-call | flops 1 | bytes 1 | tf_op jit(solution)/shard_map/pallas_call | solution.py:293
  49.6 0.0 copy-start.3
  49.6 0.7 copy-done.3
  50.4 0.0 collective-permute-done.10.refs_4_
  50.4 5.8 %shard_map.71 = (f32[4,48,2816]{2,1,0:T(8,128)S(1)}, f32[4,48,2816]{2,1,0:T(8,128)S(1)}) custom-call(s32[4]{0:T(128)S(1)} %pad_add_fusion.at_ref, bf16[4,2,48,1536]{3,2,1,0:T(8,128)(2,1)S(1)} %bitcast.11, bf16[2,2,48,1536]{3,2,1,0:T(8,128)(2,1)S(1)} %collective-permute-done.7.left_ref.refs_1_, ...), custom_call_target="tpu_custom_call" | custom-call | flops 1 | bytes 1 | tf_op jit(solution)/shard_map/pallas_call | solution.py:169
  56.2 4.5 %collective-permute-start.11 = (f32[4,48,2816]{2,1,0:T(8,128)S(1)}, f32[4,48,2816]{2,1,0:T(8,128)S(1)}, u32[]{:S(2)}, u32[]{:S(2)}) collective-permute-start(f32[4,48,2816]{2,1,0:T(8,128)S(1)} %get-tuple-element.43), channel_id=1, source_target_pairs={{0,1},{1,0},{2,3},{3,2},{4,5},{5,4},{6,7},{7,6},{8,9},{9,8},{10,11... | collective-permute-start | bytes 6488072 | tf_op jit(solution)/shard_map/ppermute | solution.py:51
  60.7 2.7 %shard_map.72 = (f32[4,48,1280]{2,1,0:T(8,128)S(1)}, f32[4,48,1280]{2,1,0:T(8,128)S(1)}) custom-call(s32[4]{0:T(128)S(1)} %pad_add_fusion.at_ref, bf16[4,2,48,1536]{3,2,1,0:T(8,128)(2,1)S(1)} %bitcast.12, bf16[2,2,48,1536]{3,2,1,0:T(8,128)(2,1)S(1)} %collective-permute-done.7.left_ref.refs_1_, ...), custom_call_target="tpu_custom_call" | custom-call | flops 1 | bytes 1 | tf_op jit(solution)/shard_map/pallas_call | solution.py:169
  63.4 0.1 collective-permute-start.12
  63.5 2.5 %collective-permute-done.12.recv_ref = f32[4,48,1280]{2,1,0:T(8,128)S(1)} collective-permute-done((f32[4,48,1280]{2,1,0:T(8,128)S(1)}, f32[4,48,1280]{2,1,0:T(8,128)S(1)}, u32[]{:S(2)}, u32[]{:S(2)}) %collective-permute-start.12) | collective-permute-done | bytes 983072 | tf_op jit(solution)/shard_map/ppermute | solution.py:51
  66.1 0.9 shard_map.73.refs_0_
  66.9 2.6 %shard_map.74 = s16[4,48,4224]{2,1,0:T(8,128)(2,1)} custom-call(f32[4,48,2816]{2,1,0:T(8,128)S(1)} %get-tuple-element.42.keep_ref, f32[4,48,2816]{2,1,0:T(8,128)S(1)} %collective-permute-done.11.recv_ref, s16[4,48,1408]{2,1,0:T(8,128)(2,1)S(1)} %shard_map.73.refs_0_), custom_call_target="tpu_custom_call" | custom-call | flops 1 | bytes 1 | tf_op jit(solution)/shard_map/pallas_call | solution.py:130
  69.5 4.2 %all-to-all-start = ((s16[4,48,4224]{2,1,0:T(8,128)(2,1)}), s16[4,48,4224]{2,1,0:T(8,128)(2,1)S(1)}, u32[]{:S(2)}, u32[]{:S(2)}) async-start(s16[4,48,4224]{2,1,0:T(8,128)(2,1)} %shard_map.74), calls=%async_computation | async-start | bytes 3244032 | tf_op jit(solution)/shard_map/all_to_all | solution.py:363
  73.7 0.9 collective-permute-start.13
  74.6 9.1 %collective-permute-done.13.refs_1_ = bf16[192,1024]{1,0:T(8,128)(2,1)S(1)} collective-permute-done((bf16[192,1024]{1,0:T(8,128)(2,1)S(1)}, bf16[192,1024]{1,0:T(8,128)(2,1)S(1)}, u32[]{:S(2)}, u32[]{:S(2)}) %collective-permute-start.13) | collective-permute-done | bytes 393248 | tf_op jit(solution)/shard_map/ppermute | solution.py:39
  83.8 2.1 %collective-permute-start.14 = (bf16[192,1024]{1,0:T(8,128)(2,1)S(1)}, bf16[192,1024]{1,0:T(8,128)(2,1)S(1)}, u32[]{:S(2)}, u32[]{:S(2)}) collective-permute-start(bf16[192,1024]{1,0:T(8,128)(2,1)S(1)} %collective-permute-done.13.refs_1_), channel_id=1, source_target_pairs={{0,24},{8,0},{16,8},{24,16},{1,25},{9,1},{17,9},{25,17},{2,26},{10... | collective-permute-start | bytes 1179656 | tf_op jit(solution)/shard_map/ppermute | solution.py:39
  85.9 1.5 %shard_map.75 = (f32[192,128]{1,0:T(8,128)S(1)}, f32[1,1024]{1,0:T(1,128)S(1)}) custom-call(s32[4]{0:T(128)S(1)} %pad_add_fusion.at_ref, s32[32]{0:T(128)S(1)} %copy-done.5, s32[32]{0:T(128)S(1)} %copy-done.6, s32[32]{0:T(128)S(1)} %copy-done.7), custom_call_target="tpu_custom_call" | custom-call | flops 1 | bytes 1 | tf_op jit(solution)/shard_map/pallas_call | solution.py:203
  87.4 5.5 %collective-permute-done.14.refs_2_ = bf16[192,1024]{1,0:T(8,128)(2,1)S(1)} collective-permute-done((bf16[192,1024]{1,0:T(8,128)(2,1)S(1)}, bf16[192,1024]{1,0:T(8,128)(2,1)S(1)}, u32[]{:S(2)}, u32[]{:S(2)}) %collective-permute-start.14) | collective-permute-done | bytes 393248 | tf_op jit(solution)/shard_map/ppermute | solution.py:39
  92.9 1.5 %all-to-all-done.total_ref = s16[4,48,4224]{2,1,0:T(8,128)(2,1)S(1)} async-done(((s16[4,48,4224]{2,1,0:T(8,128)(2,1)}), s16[4,48,4224]{2,1,0:T(8,128)(2,1)S(1)}, u32[]{:S(2)}, u32[]{:S(2)}) %all-to-all-start) | async-done | bytes 1622048 | tf_op jit(solution)/shard_map/all_to_all | solution.py:363
  94.4 2.7 %shard_map.76 = (bf16[64,1024]{1,0:T(8,128)(2,1)S(1)}, bf16[64,1024]{1,0:T(8,128)(2,1)S(1)}, bf16[64,1024]{1,0:T(8,128)(2,1)S(1)}, bf16[64,1024]{1,0:T(8,128)(2,1)S(1)}) custom-call(s32[4]{0:T(128)S(1)} %pad_add_fusion.at_ref, s16[4,48,4224]{2,1,0:T(8,128)(2,1)S(1)} %all-to-all-done.total_ref, f32[1,1024]{1,0:T(1,128)S(1)} %get-tuple-element.49.mask_ref, ...), custom_call_target="tpu_custom_call" | custom-call | flops 1 | bytes 1 | tf_op jit(solution)/shard_map/pallas_call | solution.py:262
  97.1 1.9 %collective-permute-start.15 = (bf16[64,1024]{1,0:T(8,128)(2,1)S(1)}, bf16[64,1024]{1,0:T(8,128)(2,1)S(1)}, u32[]{:S(2)}, u32[]{:S(2)}) collective-permute-start(bf16[64,1024]{1,0:T(8,128)(2,1)S(1)} %get-tuple-element.53), channel_id=1, source_target_pairs={{0,24},{2,26},{4,12},{6,14},{8,0},{10,2},{12,20},{14,22},{16,8},{1... | collective-permute-start | bytes 393224 | tf_op jit(solution)/shard_map/ppermute | solution.py:47
  99.0 1.3 collective-permute-start.17
  100.3 0.7 collective-permute-done.15.refs_1_
  101.0 4.4 %collective-permute-done.16.refs_2_ = bf16[64,1024]{1,0:T(8,128)(2,1)S(1)} collective-permute-done((bf16[64,1024]{1,0:T(8,128)(2,1)S(1)}, bf16[64,1024]{1,0:T(8,128)(2,1)S(1)}, u32[]{:S(2)}, u32[]{:S(2)}) %collective-permute-start.16) | collective-permute-done | bytes 131104 | tf_op jit(solution)/shard_map/ppermute | solution.py:47
  105.4 1.4 %shard_map.77 = (bf16[32,48,128]{2,1,0:T(8,128)(2,1)}, f32[64,128]{1,0:T(8,128)S(1)}) custom-call(s32[4]{0:T(128)S(1)} %pad_add_fusion.at_ref, bf16[64,1024]{1,0:T(8,128)(2,1)S(1)} %get-tuple-element.52.refs_0_, bf16[64,1024]{1,0:T(8,128)(2,1)S(1)} %collective-permute-done.15.refs_1_, bf16[64,1024]{1,0:T(8,128)(2,1)S(1)} %collective-permute-done.16.refs_2_, ...), custom_call_target="tpu_custom_call" | custom-call | flops 1 | bytes 1 | tf_op jit(solution)/shard_map/pallas_call | solution.py:320
  106.8 20.6 %all_to_all.17 = f32[64,1,128]{2,1,0:T(1,128)S(1)} all-to-all(f32[64,1,128]{2,1,0:T(1,128)S(1)} %bitcast.18), channel_id=1, replica_groups=mesh['z'=8,'y'=4,'x'=4,'c'=2] {'z','x','c'}, dimensions={0} | all-to-all | bytes 65536 | tf_op jit(solution)/shard_map/all_to_all | solution.py:382
  127.5 0.6 reshape.13
  (20 shorter events, 0.1 us)
Async XLA Ops:
  0.6 1.3 copy-start
  1.9 46.2 %copy-start.2 = (bf16[1,1536,128]{2,1,0:T(8,128)(2,1)S(1)}, bf16[1,1536,128]{2,1,0:T(8,128)(2,1)}, u32[]{:S(2)}) copy-start(bf16[1,1536,128]{2,1,0:T(8,128)(2,1)} %param.5) | copy-start | bytes 1179652
  2.0 17.9 %collective-permute-start.7 = (bf16[2,2,48,1536]{3,2,1,0:T(8,128)(2,1)S(1)}, bf16[2,2,48,1536]{3,2,1,0:T(8,128)(2,1)S(1)}, u32[]{:S(2)}, u32[]{:S(2)}) collective-permute-start(bf16[2,2,48,1536]{3,2,1,0:T(8,128)(2,1)S(1)} %get-tuple-element.33.low_ref), channel_id=1, source_target_pairs={{0,8},{8,16},{16,24},{24,0},{1,9},{9,17},{17,25},{25,1},{2,10},{10... | collective-permute-start | bytes 1769480 | tf_op jit(solution)/shard_map/ppermute | solution.py:39
  4.2 15.7 %collective-permute-start.8 = (bf16[2,2,48,1536]{3,2,1,0:T(8,128)(2,1)S(1)}, bf16[2,2,48,1536]{3,2,1,0:T(8,128)(2,1)S(1)}, u32[]{:S(2)}, u32[]{:S(2)}) collective-permute-start(bf16[2,2,48,1536]{3,2,1,0:T(8,128)(2,1)S(1)} %get-tuple-element.34.high_ref), channel_id=1, source_target_pairs={{0,24},{8,0},{16,8},{24,16},{1,25},{9,1},{17,9},{25,17},{2,26},{10... | collective-permute-start | bytes 1769480 | tf_op jit(solution)/shard_map/ppermute | solution.py:39
  5.7 14.2 %collective-permute-start.1 = (bf16[1536,128]{1,0:T(8,128)(2,1)}, bf16[1536,128]{1,0:T(8,128)(2,1)S(1)}, u32[]{:S(2)}, u32[]{:S(2)}) collective-permute-start(bf16[1536,128]{1,0:T(8,128)(2,1)} %bitcast.13), channel_id=1, source_target_pairs={{0,32},{32,64},{64,96},{96,128},{128,160},{160,192},{192,224},{224... | collective-permute-start | bytes 1179656 | tf_op jit(solution)/shard_map/ppermute | solution.py:35
  7.4 15.5 %collective-permute-start = (bf16[1536,128]{1,0:T(8,128)(2,1)}, bf16[1536,128]{1,0:T(8,128)(2,1)S(1)}, u32[]{:S(2)}, u32[]{:S(2)}) collective-permute-start(bf16[1536,128]{1,0:T(8,128)(2,1)} %bitcast.14), channel_id=1, source_target_pairs={{0,224},{32,0},{64,32},{96,64},{128,96},{160,128},{192,160},{224,1... | collective-permute-start | bytes 1179656 | tf_op jit(solution)/shard_map/ppermute | solution.py:35
  19.9 10.2 %collective-permute-start.3 = (bf16[1536,128]{1,0:T(8,128)(2,1)S(1)}, bf16[1536,128]{1,0:T(8,128)(2,1)S(1)}, u32[]{:S(2)}, u32[]{:S(2)}) collective-permute-start(bf16[1536,128]{1,0:T(8,128)(2,1)S(1)} %collective-permute-done.1.refs_2_.refs_7_.refs_5_), channel_id=1, source_target_pairs={{0,32},{32,64},{64,96},{96,128},{128,160},{160,192},{192,224},{224... | collective-permute-start | bytes 1179656 | tf_op jit(solution)/shard_map/ppermute | solution.py:35
  21.4 29.0 %collective-permute-start.10 = (bf16[4,2,48,1536]{3,2,1,0:T(8,128)(2,1)}, bf16[4,2,48,1536]{3,2,1,0:T(8,128)(2,1)}, u32[]{:S(2)}, u32[]{:S(2)}) collective-permute-start(bf16[4,2,48,1536]{3,2,1,0:T(8,128)(2,1)} %get-tuple-element.36), channel_id=1, source_target_pairs={{0,24},{8,0},{16,8},{24,16},{1,25},{9,1},{17,9},{25,17},{2,26},{10... | collective-permute-start | bytes 3538952 | tf_op jit(solution)/shard_map/ppermute | solution.py:39
  22.6 27.7 %collective-permute-start.9 = (bf16[4,2,48,1536]{3,2,1,0:T(8,128)(2,1)}, bf16[4,2,48,1536]{3,2,1,0:T(8,128)(2,1)}, u32[]{:S(2)}, u32[]{:S(2)}) collective-permute-start(bf16[4,2,48,1536]{3,2,1,0:T(8,128)(2,1)} %get-tuple-element.35), channel_id=1, source_target_pairs={{0,8},{8,16},{16,24},{24,0},{1,9},{9,17},{17,25},{25,1},{2,10},{10... | collective-permute-start | bytes 3538952 | tf_op jit(solution)/shard_map/ppermute | solution.py:39
  22.9 11.6 %collective-permute-start.2 = (bf16[1536,128]{1,0:T(8,128)(2,1)S(1)}, bf16[1536,128]{1,0:T(8,128)(2,1)S(1)}, u32[]{:S(2)}, u32[]{:S(2)}) collective-permute-start(bf16[1536,128]{1,0:T(8,128)(2,1)S(1)} %collective-permute-done.refs_1_.refs_6_.refs_4_), channel_id=1, source_target_pairs={{0,224},{32,0},{64,32},{96,64},{128,96},{160,128},{192,160},{224,1... | collective-permute-start | bytes 1179656 | tf_op jit(solution)/shard_map/ppermute | solution.py:35
  30.1 9.4 %collective-permute-start.5 = (bf16[1536,128]{1,0:T(8,128)(2,1)S(1)}, bf16[1536,128]{1,0:T(8,128)(2,1)S(1)}, u32[]{:S(2)}, u32[]{:S(2)}) collective-permute-start(bf16[1536,128]{1,0:T(8,128)(2,1)S(1)} %collective-permute-done.3.refs_4_.refs_9_.refs_7_), channel_id=1, source_target_pairs={{0,32},{32,64},{64,96},{96,128},{128,160},{160,192},{192,224},{224... | collective-permute-start | bytes 1179656 | tf_op jit(solution)/shard_map/ppermute | solution.py:35
  34.5 9.1 %collective-permute-start.4 = (bf16[1536,128]{1,0:T(8,128)(2,1)S(1)}, bf16[1536,128]{1,0:T(8,128)(2,1)}, u32[]{:S(2)}, u32[]{:S(2)}) collective-permute-start(bf16[1536,128]{1,0:T(8,128)(2,1)S(1)} %collective-permute-done.2.refs_3_.refs_8_.refs_6_), channel_id=1, source_target_pairs={{0,224},{32,0},{64,32},{96,64},{128,96},{160,128},{192,160},{224,1... | collective-permute-start | bytes 1179656 | tf_op jit(solution)/shard_map/ppermute | solution.py:35
  39.5 8.6 %collective-permute-start.6 = (bf16[1536,128]{1,0:T(8,128)(2,1)S(1)}, bf16[1536,128]{1,0:T(8,128)(2,1)}, u32[]{:S(2)}, u32[]{:S(2)}) collective-permute-start(bf16[1536,128]{1,0:T(8,128)(2,1)S(1)} %collective-permute-done.5.refs_6_.refs_11_), channel_id=1, source_target_pairs={{0,32},{32,64},{64,96},{96,128},{128,160},{160,192},{192,224},{224... | collective-permute-start | bytes 1179656 | tf_op jit(solution)/shard_map/ppermute | solution.py:35
  39.6 10.8 %copy-start.1 = (bf16[8,1,48,1536]{3,2,1,0:T(8,128)(2,1)S(1)}, bf16[8,1,48,1536]{3,2,1,0:T(8,128)(2,1)}, u32[]{:S(2)}) copy-start(bf16[8,1,48,1536]{3,2,1,0:T(8,128)(2,1)} %param.6) | copy-start | bytes 3538948
  49.6 0.7 copy-start.3
  56.2 10.7 %collective-permute-start.11 = (f32[4,48,2816]{2,1,0:T(8,128)S(1)}, f32[4,48,2816]{2,1,0:T(8,128)S(1)}, u32[]{:S(2)}, u32[]{:S(2)}) collective-permute-start(f32[4,48,2816]{2,1,0:T(8,128)S(1)} %get-tuple-element.43), channel_id=1, source_target_pairs={{0,1},{1,0},{2,3},{3,2},{4,5},{5,4},{6,7},{7,6},{8,9},{9,8},{10,11... | collective-permute-start | bytes 6488072 | tf_op jit(solution)/shard_map/ppermute | solution.py:51
  63.4 2.7 %collective-permute-start.12 = (f32[4,48,1280]{2,1,0:T(8,128)S(1)}, f32[4,48,1280]{2,1,0:T(8,128)S(1)}, u32[]{:S(2)}, u32[]{:S(2)}) collective-permute-start(f32[4,48,1280]{2,1,0:T(8,128)S(1)} %get-tuple-element.48), channel_id=1, source_target_pairs={{0,1},{1,0},{2,3},{3,2},{4,5},{5,4},{6,7},{7,6},{8,9},{9,8},{10,11... | collective-permute-start | bytes 2949128 | tf_op jit(solution)/shard_map/ppermute | solution.py:51
  69.5 4.2 %copy-start.4 = (bf16[192,1024]{1,0:T(8,128)(2,1)S(1)}, bf16[192,1024]{1,0:T(8,128)(2,1)}, u32[]{:S(2)}) copy-start(bf16[192,1024]{1,0:T(8,128)(2,1)} %copy-done.3) | copy-start | bytes 1179652
  69.5 16.4 %copy-start.5 = (s32[32]{0:T(128)S(1)}, s32[32]{0:T(128)}, u32[]{:S(2)}) copy-start(s32[32]{0:T(128)} %pair_ref.1) | copy-start | bytes 388
  69.5 16.4 %copy-start.6 = (s32[32]{0:T(128)S(1)}, s32[32]{0:T(128)}, u32[]{:S(2)}) copy-start(s32[32]{0:T(128)} %block_ref.1) | copy-start | bytes 388
  69.5 16.4 %copy-start.7 = (s32[32]{0:T(128)S(1)}, s32[32]{0:T(128)}, u32[]{:S(2)}) copy-start(s32[32]{0:T(128)} %live_ref.1) | copy-start | bytes 388
  69.5 24.9 %all-to-all-start = ((s16[4,48,4224]{2,1,0:T(8,128)(2,1)}), s16[4,48,4224]{2,1,0:T(8,128)(2,1)S(1)}, u32[]{:S(2)}, u32[]{:S(2)}) async-start(s16[4,48,4224]{2,1,0:T(8,128)(2,1)} %shard_map.74), calls=%async_computation | async-start | bytes 3244032 | tf_op jit(solution)/shard_map/all_to_all | solution.py:363
  73.7 10.1 %collective-permute-start.13 = (bf16[192,1024]{1,0:T(8,128)(2,1)S(1)}, bf16[192,1024]{1,0:T(8,128)(2,1)S(1)}, u32[]{:S(2)}, u32[]{:S(2)}) collective-permute-start(bf16[192,1024]{1,0:T(8,128)(2,1)S(1)} %copy-done.4), channel_id=1, source_target_pairs={{0,24},{8,0},{16,8},{24,16},{1,25},{9,1},{17,9},{25,17},{2,26},{10... | collective-permute-start | bytes 1179656 | tf_op jit(solution)/shard_map/ppermute | solution.py:39
  83.8 9.1 %collective-permute-start.14 = (bf16[192,1024]{1,0:T(8,128)(2,1)S(1)}, bf16[192,1024]{1,0:T(8,128)(2,1)S(1)}, u32[]{:S(2)}, u32[]{:S(2)}) collective-permute-start(bf16[192,1024]{1,0:T(8,128)(2,1)S(1)} %collective-permute-done.13.refs_1_), channel_id=1, source_target_pairs={{0,24},{8,0},{16,8},{24,16},{1,25},{9,1},{17,9},{25,17},{2,26},{10... | collective-permute-start | bytes 1179656 | tf_op jit(solution)/shard_map/ppermute | solution.py:39
  97.1 3.9 %collective-permute-start.15 = (bf16[64,1024]{1,0:T(8,128)(2,1)S(1)}, bf16[64,1024]{1,0:T(8,128)(2,1)S(1)}, u32[]{:S(2)}, u32[]{:S(2)}) collective-permute-start(bf16[64,1024]{1,0:T(8,128)(2,1)S(1)} %get-tuple-element.53), channel_id=1, source_target_pairs={{0,24},{2,26},{4,12},{6,14},{8,0},{10,2},{12,20},{14,22},{16,8},{1... | collective-permute-start | bytes 393224 | tf_op jit(solution)/shard_map/ppermute | solution.py:47
  99.0 6.4 %collective-permute-start.16 = (bf16[64,1024]{1,0:T(8,128)(2,1)S(1)}, bf16[64,1024]{1,0:T(8,128)(2,1)S(1)}, u32[]{:S(2)}, u32[]{:S(2)}) collective-permute-start(bf16[64,1024]{1,0:T(8,128)(2,1)S(1)} %get-tuple-element.54), channel_id=1, source_target_pairs={{0,8},{2,10},{4,28},{6,30},{8,16},{10,18},{12,4},{14,6},{16,24},{1... | collective-permute-start | bytes 393224 | tf_op jit(solution)/shard_map/ppermute | solution.py:47
  99.0 6.4 %collective-permute-start.17 = (bf16[64,1024]{1,0:T(8,128)(2,1)S(1)}, bf16[64,1024]{1,0:T(8,128)(2,1)S(1)}, u32[]{:S(2)}, u32[]{:S(2)}) collective-permute-start(bf16[64,1024]{1,0:T(8,128)(2,1)S(1)} %get-tuple-element.55), channel_id=1, source_target_pairs={{0,16},{2,18},{4,20},{6,22},{8,24},{10,26},{12,28},{14,30},{16,0},... | collective-permute-start | bytes 393224 | tf_op jit(solution)/shard_map/ppermute | solution.py:47

commit v5 on v4

--- a/solution.py
+++ b/solution.py
@@ -372,7 +372,7 @@
 
     rows = [rows_of(at, [slots[e] for e in ORDER], NY * width)]
     rows.append(shift_y(rows[0], -1))
-    rows.append(shift_y(rows[1], -1))
+    rows.append(shift_y(rows[0], 2))
 
     rows[0], *f_arrays = lax.optimization_barrier((rows[0], *f_arrays))
     recv, keep = start(SECOND, ORDER, f_arrays)

time: 128 us -> 127 us (level)
  waiting for transfers between devices: 48.8 us -> 52.1 us
  starting transfers between devices: 34.6 us -> 31.6 us
  blocking collectives: 20.6 us -> 19.3 us
    all_to_all x1, waiting for transfers between devices: 1.53 us -> 8.54 us  [spread(): return lax.all_to_all(total, 'x', 0, 0)]
    ppermute x6, waiting for transfers between devices: 14.6 us -> 9.72 us  [shift_y(): return lax.ppermute(v, 'y', [(y, (y + s) % NY) for y in range(NY)])]
    ppermute x6, starting transfers between devices: 8.36 us -> 6.21 us  [shift_y(): return lax.ppermute(v, 'y', [(y, (y + s) % NY) for y in range(NY)])]
    all_to_all x1, blocking collectives: 20.6 us -> 19.3 us  [on_device(): bmat = lax.all_to_all(bmat, ('z', 'x', 'c'), 0, 0, tiled=True)]
  transfers between devices with their start and end apart: 19 -> 19, of which waited for: 12 -> 13; matrix products, arithmetic and copies ran while one was open for 0% -> 0% of each run, Pallas kernels for 6% -> 6%
where the time goes in v5:
time: 127 us
  waiting for transfers between devices  52.1 us (41%)
  starting transfers between devices  31.6 us (25%)
  Pallas kernels  20.5 us (16%)
  blocking collectives  19.3 us (15%)
  local copies, waits for them, and re-layouts  2.67 us (2%)
    ppermute x7, waiting for transfers between devices, shift_z(): return lax.ppermute(v, 'z', [(z, (z + s) % NZ) for z in range(NZ)])  25 us
    all_to_all x1, blocking collectives, on_device(): bmat = lax.all_to_all(bmat, ('z', 'x', 'c'), 0, 0, tiled=True)  19.3 us
    ppermute x7, starting transfers between devices, shift_z(): return lax.ppermute(v, 'z', [(z, (z + s) % NZ) for z in range(NZ)])  14.3 us
    ppermute x6, waiting for transfers between devices, shift_y(): return lax.ppermute(v, 'y', [(y, (y + s) % NY) for y in range(NY)])  9.72 us
    all_to_all x1, waiting for transfers between devices, spread(): return lax.all_to_all(total, 'x', 0, 0)  8.54 us
    pallas_call x2, Pallas kernels, products(): pl.pallas_call(functools.partial(products_kernel, plan, len(f_arrays), le...  8.5 us
    ppermute x3, waiting for transfers between devices, to_owner(): return lax.ppermute(v, ('y', 'x'), moves) if j else v  6.27 us
    ppermute x6, starting transfers between devices, shift_y(): return lax.ppermute(v, 'y', [(y, (y + s) % NY) for y in range(NY)])  6.21 us
  transfers between devices with their start and end apart: 19, of which 13 were waited for; matrix products, arithmetic and copies ran while one was open for 0% of the time, Pallas kernels for 6%

profile of v5, /device:TPU:1, one launch (start us, length us, event | category | flops | bytes accessed | tf_op | source)
XLA Modules:
  0.0 127.0 jit_solution(4442270139939371157)
XLA Ops:
  0.6 0.0 copy-start
  0.6 1.3 copy-done
  1.9 0.1 shard_map.68
  2.0 2.2 %collective-permute-start.7 = (bf16[2,2,48,1536]{3,2,1,0:T(8,128)(2,1)S(1)}, bf16[2,2,48,1536]{3,2,1,0:T(8,128)(2,1)S(1)}, u32[]{:S(2)}, u32[]{:S(2)}) collective-permute-start(bf16[2,2,48,1536]{3,2,1,0:T(8,128)(2,1)S(1)} %get-tuple-element.33.low_ref), channel_id=1, source_target_pairs={{0,8},{8,16},{16,24},{24,0},{1,9},{9,17},{17,25},{25,1},{2,10},{10... | collective-permute-start | bytes 1769480 | tf_op jit(solution)/shard_map/ppermute | solution.py:39
  4.2 1.5 %collective-permute-start.8 = (bf16[2,2,48,1536]{3,2,1,0:T(8,128)(2,1)S(1)}, bf16[2,2,48,1536]{3,2,1,0:T(8,128)(2,1)S(1)}, u32[]{:S(2)}, u32[]{:S(2)}) collective-permute-start(bf16[2,2,48,1536]{3,2,1,0:T(8,128)(2,1)S(1)} %get-tuple-element.34.high_ref), channel_id=1, source_target_pairs={{0,24},{8,0},{16,8},{24,16},{1,25},{9,1},{17,9},{25,17},{2,26},{10... | collective-permute-start | bytes 1769480 | tf_op jit(solution)/shard_map/ppermute | solution.py:39
  5.7 1.6 %collective-permute-start.1 = (bf16[1536,128]{1,0:T(8,128)(2,1)}, bf16[1536,128]{1,0:T(8,128)(2,1)S(1)}, u32[]{:S(2)}, u32[]{:S(2)}) collective-permute-start(bf16[1536,128]{1,0:T(8,128)(2,1)} %bitcast.13), channel_id=1, source_target_pairs={{0,32},{32,64},{64,96},{96,128},{128,160},{160,192},{192,224},{224... | collective-permute-start | bytes 1179656 | tf_op jit(solution)/shard_map/ppermute | solution.py:35
  7.4 3.9 %collective-permute-start = (bf16[1536,128]{1,0:T(8,128)(2,1)}, bf16[1536,128]{1,0:T(8,128)(2,1)S(1)}, u32[]{:S(2)}, u32[]{:S(2)}) collective-permute-start(bf16[1536,128]{1,0:T(8,128)(2,1)} %bitcast.14), channel_id=1, source_target_pairs={{0,224},{32,0},{64,32},{96,64},{128,96},{160,128},{192,160},{224,1... | collective-permute-start | bytes 1179656 | tf_op jit(solution)/shard_map/ppermute | solution.py:35
  11.3 8.6 %collective-permute-done.1.refs_2_.refs_7_.refs_5_ = bf16[1536,128]{1,0:T(8,128)(2,1)S(1)} collective-permute-done((bf16[1536,128]{1,0:T(8,128)(2,1)}, bf16[1536,128]{1,0:T(8,128)(2,1)S(1)}, u32[]{:S(2)}, u32[]{:S(2)}) %collective-permute-start.1) | collective-permute-done | bytes 393248 | tf_op jit(solution)/shard_map/ppermute | solution.py:35
  19.9 0.0 collective-permute-start.3
  19.9 0.0 collective-permute-done.7.left_ref.refs_1_
  19.9 0.0 collective-permute-done.8.right_ref.refs_2_
  19.9 1.5 %shard_map.70 = (bf16[4,2,48,1536]{3,2,1,0:T(8,128)(2,1)}, bf16[4,2,48,1536]{3,2,1,0:T(8,128)(2,1)}) custom-call(bf16[2,2,48,1536]{3,2,1,0:T(8,128)(2,1)S(1)} %get-tuple-element.33.low_ref, bf16[2,2,48,1536]{3,2,1,0:T(8,128)(2,1)S(1)} %get-tuple-element.34.high_ref, bf16[2,2,48,1536]{3,2,1,0:T(8,128)(2,1)S(1)} %collective-permute-done.7.left_ref.refs_1_, ...), custom_call_target="tpu_custom_call" | custom-call | flops 1 | bytes 1 | tf_op jit(solution)/shard_map/pallas_call | solution.py:89
  21.4 1.3 %collective-permute-start.10 = (bf16[4,2,48,1536]{3,2,1,0:T(8,128)(2,1)}, bf16[4,2,48,1536]{3,2,1,0:T(8,128)(2,1)}, u32[]{:S(2)}, u32[]{:S(2)}) collective-permute-start(bf16[4,2,48,1536]{3,2,1,0:T(8,128)(2,1)} %get-tuple-element.36), channel_id=1, source_target_pairs={{0,24},{8,0},{16,8},{24,16},{1,25},{9,1},{17,9},{25,17},{2,26},{10... | collective-permute-start | bytes 3538952 | tf_op jit(solution)/shard_map/ppermute | solution.py:39
  22.6 0.3 collective-permute-start.9
  22.9 5.2 %collective-permute-start.2 = (bf16[1536,128]{1,0:T(8,128)(2,1)S(1)}, bf16[1536,128]{1,0:T(8,128)(2,1)S(1)}, u32[]{:S(2)}, u32[]{:S(2)}) collective-permute-start(bf16[1536,128]{1,0:T(8,128)(2,1)S(1)} %collective-permute-done.refs_1_.refs_6_.refs_4_), channel_id=1, source_target_pairs={{0,224},{32,0},{64,32},{96,64},{128,96},{160,128},{192,160},{224,1... | collective-permute-start | bytes 1179656 | tf_op jit(solution)/shard_map/ppermute | solution.py:35
  28.1 2.0 %collective-permute-done.3.refs_4_.refs_9_.refs_7_ = bf16[1536,128]{1,0:T(8,128)(2,1)S(1)} collective-permute-done((bf16[1536,128]{1,0:T(8,128)(2,1)S(1)}, bf16[1536,128]{1,0:T(8,128)(2,1)S(1)}, u32[]{:S(2)}, u32[]{:S(2)}) %collective-permute-start.3) | collective-permute-done | bytes 393248 | tf_op jit(solution)/shard_map/ppermute | solution.py:35
  30.1 4.4 %collective-permute-done.2.refs_3_.refs_8_.refs_6_ = bf16[1536,128]{1,0:T(8,128)(2,1)S(1)} collective-permute-done((bf16[1536,128]{1,0:T(8,128)(2,1)S(1)}, bf16[1536,128]{1,0:T(8,128)(2,1)S(1)}, u32[]{:S(2)}, u32[]{:S(2)}) %collective-permute-start.2) | collective-permute-done | bytes 393248 | tf_op jit(solution)/shard_map/ppermute | solution.py:35
  34.5 3.5 %collective-permute-start.4 = (bf16[1536,128]{1,0:T(8,128)(2,1)S(1)}, bf16[1536,128]{1,0:T(8,128)(2,1)}, u32[]{:S(2)}, u32[]{:S(2)}) collective-permute-start(bf16[1536,128]{1,0:T(8,128)(2,1)S(1)} %collective-permute-done.2.refs_3_.refs_8_.refs_6_), channel_id=1, source_target_pairs={{0,224},{32,0},{64,32},{96,64},{128,96},{160,128},{192,160},{224,1... | collective-permute-start | bytes 1179656 | tf_op jit(solution)/shard_map/ppermute | solution.py:35
  38.0 1.5 %collective-permute-done.5.refs_6_.refs_11_ = bf16[1536,128]{1,0:T(8,128)(2,1)S(1)} collective-permute-done((bf16[1536,128]{1,0:T(8,128)(2,1)S(1)}, bf16[1536,128]{1,0:T(8,128)(2,1)S(1)}, u32[]{:S(2)}, u32[]{:S(2)}) %collective-permute-start.5) | collective-permute-done | bytes 393248 | tf_op jit(solution)/shard_map/ppermute | solution.py:35
  39.5 0.1 pad_add_fusion.at_ref
  39.6 4.1 %collective-permute-done.4.refs_5_.refs_10_ = bf16[1536,128]{1,0:T(8,128)(2,1)} collective-permute-done((bf16[1536,128]{1,0:T(8,128)(2,1)S(1)}, bf16[1536,128]{1,0:T(8,128)(2,1)}, u32[]{:S(2)}, u32[]{:S(2)}) %collective-permute-start.4) | collective-permute-done | bytes 393248 | tf_op jit(solution)/shard_map/ppermute | solution.py:35
  43.6 4.4 %collective-permute-done.6.refs_7_.refs_12_ = bf16[1536,128]{1,0:T(8,128)(2,1)} collective-permute-done((bf16[1536,128]{1,0:T(8,128)(2,1)S(1)}, bf16[1536,128]{1,0:T(8,128)(2,1)}, u32[]{:S(2)}, u32[]{:S(2)}) %collective-permute-start.6) | collective-permute-done | bytes 393248 | tf_op jit(solution)/shard_map/ppermute | solution.py:35
  48.1 1.5 %shard_map.69.refs_0_ = bf16[192,1024]{1,0:T(8,128)(2,1)S(1)} custom-call(s32[4]{0:T(128)S(1)} %pad_add_fusion.at_ref, bf16[1536,128]{1,0:T(8,128)(2,1)S(1)} %bitcast.15, bf16[1536,128]{1,0:T(8,128)(2,1)S(1)} %collective-permute-done.refs_1_.refs_6_.refs_4_, bf16[1536,128]{1,0:T(8,128)(2,1)S(1)} %collective-permute-done.1.refs_2_.refs_7_.refs_5_, ...), custom_call_target="tpu_custom_call" | custom-call | flops 1 | bytes 1 | tf_op jit(solution)/shard_map/pallas_call | solution.py:293
  49.6 0.0 copy-start.3
  49.6 0.7 copy-done.3
  50.4 5.8 %shard_map.71 = (f32[4,48,2816]{2,1,0:T(8,128)S(1)}, f32[4,48,2816]{2,1,0:T(8,128)S(1)}) custom-call(s32[4]{0:T(128)S(1)} %pad_add_fusion.at_ref, bf16[4,2,48,1536]{3,2,1,0:T(8,128)(2,1)S(1)} %bitcast.11, bf16[2,2,48,1536]{3,2,1,0:T(8,128)(2,1)S(1)} %collective-permute-done.7.left_ref.refs_1_, ...), custom_call_target="tpu_custom_call" | custom-call | flops 1 | bytes 1 | tf_op jit(solution)/shard_map/pallas_call | solution.py:169
  56.2 4.5 %collective-permute-start.11 = (f32[4,48,2816]{2,1,0:T(8,128)S(1)}, f32[4,48,2816]{2,1,0:T(8,128)S(1)}, u32[]{:S(2)}, u32[]{:S(2)}) collective-permute-start(f32[4,48,2816]{2,1,0:T(8,128)S(1)} %get-tuple-element.43), channel_id=1, source_target_pairs={{0,1},{1,0},{2,3},{3,2},{4,5},{5,4},{6,7},{7,6},{8,9},{9,8},{10,11... | collective-permute-start | bytes 6488072 | tf_op jit(solution)/shard_map/ppermute | solution.py:51
  60.7 2.7 %shard_map.72 = (f32[4,48,1280]{2,1,0:T(8,128)S(1)}, f32[4,48,1280]{2,1,0:T(8,128)S(1)}) custom-call(s32[4]{0:T(128)S(1)} %pad_add_fusion.at_ref, bf16[4,2,48,1536]{3,2,1,0:T(8,128)(2,1)S(1)} %bitcast.12, bf16[2,2,48,1536]{3,2,1,0:T(8,128)(2,1)S(1)} %collective-permute-done.7.left_ref.refs_1_, ...), custom_call_target="tpu_custom_call" | custom-call | flops 1 | bytes 1 | tf_op jit(solution)/shard_map/pallas_call | solution.py:169
  63.4 0.1 collective-permute-start.12
  63.5 2.5 %collective-permute-done.12.recv_ref = f32[4,48,1280]{2,1,0:T(8,128)S(1)} collective-permute-done((f32[4,48,1280]{2,1,0:T(8,128)S(1)}, f32[4,48,1280]{2,1,0:T(8,128)S(1)}, u32[]{:S(2)}, u32[]{:S(2)}) %collective-permute-start.12) | collective-permute-done | bytes 983072 | tf_op jit(solution)/shard_map/ppermute | solution.py:51
  66.1 0.9 shard_map.73.refs_0_
  66.9 2.6 %shard_map.74 = s16[4,48,4224]{2,1,0:T(8,128)(2,1)} custom-call(f32[4,48,2816]{2,1,0:T(8,128)S(1)} %get-tuple-element.42.keep_ref, f32[4,48,2816]{2,1,0:T(8,128)S(1)} %collective-permute-done.11.recv_ref, s16[4,48,1408]{2,1,0:T(8,128)(2,1)S(1)} %shard_map.73.refs_0_), custom_call_target="tpu_custom_call" | custom-call | flops 1 | bytes 1 | tf_op jit(solution)/shard_map/pallas_call | solution.py:130
  69.5 4.2 %all-to-all-start = ((s16[4,48,4224]{2,1,0:T(8,128)(2,1)}), s16[4,48,4224]{2,1,0:T(8,128)(2,1)S(1)}, u32[]{:S(2)}, u32[]{:S(2)}) async-start(s16[4,48,4224]{2,1,0:T(8,128)(2,1)} %shard_map.74), calls=%async_computation | async-start | bytes 3244032 | tf_op jit(solution)/shard_map/all_to_all | solution.py:363
  73.7 0.9 collective-permute-start.13
  74.7 1.5 %shard_map.75 = (f32[192,128]{1,0:T(8,128)S(1)}, f32[1,1024]{1,0:T(1,128)S(1)}) custom-call(s32[4]{0:T(128)S(1)} %pad_add_fusion.at_ref, s32[32]{0:T(128)S(1)} %copy-done.5, s32[32]{0:T(128)S(1)} %copy-done.6, s32[32]{0:T(128)S(1)} %copy-done.7), custom_call_target="tpu_custom_call" | custom-call | flops 1 | bytes 1 | tf_op jit(solution)/shard_map/pallas_call | solution.py:203
  76.2 7.6 %collective-permute-done.13.refs_1_ = bf16[192,1024]{1,0:T(8,128)(2,1)S(1)} collective-permute-done((bf16[192,1024]{1,0:T(8,128)(2,1)S(1)}, bf16[192,1024]{1,0:T(8,128)(2,1)S(1)}, u32[]{:S(2)}, u32[]{:S(2)}) %collective-permute-start.13) | collective-permute-done | bytes 393248 | tf_op jit(solution)/shard_map/ppermute | solution.py:39
  83.8 2.1 %collective-permute-done.14.refs_2_ = bf16[192,1024]{1,0:T(8,128)(2,1)S(1)} collective-permute-done((bf16[192,1024]{1,0:T(8,128)(2,1)S(1)}, bf16[192,1024]{1,0:T(8,128)(2,1)S(1)}, u32[]{:S(2)}, u32[]{:S(2)}) %collective-permute-start.14) | collective-permute-done | bytes 393248 | tf_op jit(solution)/shard_map/ppermute | solution.py:39
  85.9 8.5 %all-to-all-done.total_ref = s16[4,48,4224]{2,1,0:T(8,128)(2,1)S(1)} async-done(((s16[4,48,4224]{2,1,0:T(8,128)(2,1)}), s16[4,48,4224]{2,1,0:T(8,128)(2,1)S(1)}, u32[]{:S(2)}, u32[]{:S(2)}) %all-to-all-start) | async-done | bytes 1622048 | tf_op jit(solution)/shard_map/all_to_all | solution.py:363
  94.4 2.7 %shard_map.76 = (bf16[64,1024]{1,0:T(8,128)(2,1)S(1)}, bf16[64,1024]{1,0:T(8,128)(2,1)S(1)}, bf16[64,1024]{1,0:T(8,128)(2,1)S(1)}, bf16[64,1024]{1,0:T(8,128)(2,1)S(1)}) custom-call(s32[4]{0:T(128)S(1)} %pad_add_fusion.at_ref, s16[4,48,4224]{2,1,0:T(8,128)(2,1)S(1)} %all-to-all-done.total_ref, f32[1,1024]{1,0:T(1,128)S(1)} %get-tuple-element.49.mask_ref, ...), custom_call_target="tpu_custom_call" | custom-call | flops 1 | bytes 1 | tf_op jit(solution)/shard_map/pallas_call | solution.py:262
  97.1 1.0 collective-permute-start.15
  98.1 0.5 collective-permute-start.16
  98.6 0.7 collective-permute-start.17
  99.4 1.6 %collective-permute-done.15.refs_1_ = bf16[64,1024]{1,0:T(8,128)(2,1)S(1)} collective-permute-done((bf16[64,1024]{1,0:T(8,128)(2,1)S(1)}, bf16[64,1024]{1,0:T(8,128)(2,1)S(1)}, u32[]{:S(2)}, u32[]{:S(2)}) %collective-permute-start.15) | collective-permute-done | bytes 131104 | tf_op jit(solution)/shard_map/ppermute | solution.py:47
  101.0 2.7 %collective-permute-done.16.refs_2_ = bf16[64,1024]{1,0:T(8,128)(2,1)S(1)} collective-permute-done((bf16[64,1024]{1,0:T(8,128)(2,1)S(1)}, bf16[64,1024]{1,0:T(8,128)(2,1)S(1)}, u32[]{:S(2)}, u32[]{:S(2)}) %collective-permute-start.16) | collective-permute-done | bytes 131104 | tf_op jit(solution)/shard_map/ppermute | solution.py:47
  103.7 1.9 %collective-permute-done.17.refs_3_ = bf16[64,1024]{1,0:T(8,128)(2,1)S(1)} collective-permute-done((bf16[64,1024]{1,0:T(8,128)(2,1)S(1)}, bf16[64,1024]{1,0:T(8,128)(2,1)S(1)}, u32[]{:S(2)}, u32[]{:S(2)}) %collective-permute-start.17) | collective-permute-done | bytes 131104 | tf_op jit(solution)/shard_map/ppermute | solution.py:47
  105.7 1.4 %shard_map.77 = (bf16[32,48,128]{2,1,0:T(8,128)(2,1)}, f32[64,128]{1,0:T(8,128)S(1)}) custom-call(s32[4]{0:T(128)S(1)} %pad_add_fusion.at_ref, bf16[64,1024]{1,0:T(8,128)(2,1)S(1)} %get-tuple-element.52.refs_0_, bf16[64,1024]{1,0:T(8,128)(2,1)S(1)} %collective-permute-done.15.refs_1_, bf16[64,1024]{1,0:T(8,128)(2,1)S(1)} %collective-permute-done.16.refs_2_, ...), custom_call_target="tpu_custom_call" | custom-call | flops 1 | bytes 1 | tf_op jit(solution)/shard_map/pallas_call | solution.py:320
  107.0 19.3 %all_to_all.17 = f32[64,1,128]{2,1,0:T(1,128)S(1)} all-to-all(f32[64,1,128]{2,1,0:T(1,128)S(1)} %bitcast.18), channel_id=1, replica_groups=mesh['z'=8,'y'=4,'x'=4,'c'=2] {'z','x','c'}, dimensions={0} | all-to-all | bytes 65536 | tf_op jit(solution)/shard_map/all_to_all | solution.py:382
  126.3 0.6 reshape.13
  (20 shorter events, 0.1 us)
Async XLA Ops:
  0.6 1.3 %copy-start = (bf16[8,1,48,1536]{3,2,1,0:T(8,128)(2,1)S(1)}, bf16[8,1,48,1536]{3,2,1,0:T(8,128)(2,1)}, u32[]{:S(2)}) copy-start(bf16[8,1,48,1536]{3,2,1,0:T(8,128)(2,1)} %param.6) | copy-start | bytes 3538948
  1.9 46.2 %copy-start.2 = (bf16[1,1536,128]{2,1,0:T(8,128)(2,1)S(1)}, bf16[1,1536,128]{2,1,0:T(8,128)(2,1)}, u32[]{:S(2)}) copy-start(bf16[1,1536,128]{2,1,0:T(8,128)(2,1)} %param.5) | copy-start | bytes 1179652
  2.0 17.9 %collective-permute-start.7 = (bf16[2,2,48,1536]{3,2,1,0:T(8,128)(2,1)S(1)}, bf16[2,2,48,1536]{3,2,1,0:T(8,128)(2,1)S(1)}, u32[]{:S(2)}, u32[]{:S(2)}) collective-permute-start(bf16[2,2,48,1536]{3,2,1,0:T(8,128)(2,1)S(1)} %get-tuple-element.33.low_ref), channel_id=1, source_target_pairs={{0,8},{8,16},{16,24},{24,0},{1,9},{9,17},{17,25},{25,1},{2,10},{10... | collective-permute-start | bytes 1769480 | tf_op jit(solution)/shard_map/ppermute | solution.py:39
  4.2 15.7 %collective-permute-start.8 = (bf16[2,2,48,1536]{3,2,1,0:T(8,128)(2,1)S(1)}, bf16[2,2,48,1536]{3,2,1,0:T(8,128)(2,1)S(1)}, u32[]{:S(2)}, u32[]{:S(2)}) collective-permute-start(bf16[2,2,48,1536]{3,2,1,0:T(8,128)(2,1)S(1)} %get-tuple-element.34.high_ref), channel_id=1, source_target_pairs={{0,24},{8,0},{16,8},{24,16},{1,25},{9,1},{17,9},{25,17},{2,26},{10... | collective-permute-start | bytes 1769480 | tf_op jit(solution)/shard_map/ppermute | solution.py:39
  5.7 14.2 %collective-permute-start.1 = (bf16[1536,128]{1,0:T(8,128)(2,1)}, bf16[1536,128]{1,0:T(8,128)(2,1)S(1)}, u32[]{:S(2)}, u32[]{:S(2)}) collective-permute-start(bf16[1536,128]{1,0:T(8,128)(2,1)} %bitcast.13), channel_id=1, source_target_pairs={{0,32},{32,64},{64,96},{96,128},{128,160},{160,192},{192,224},{224... | collective-permute-start | bytes 1179656 | tf_op jit(solution)/shard_map/ppermute | solution.py:35
  7.4 15.5 %collective-permute-start = (bf16[1536,128]{1,0:T(8,128)(2,1)}, bf16[1536,128]{1,0:T(8,128)(2,1)S(1)}, u32[]{:S(2)}, u32[]{:S(2)}) collective-permute-start(bf16[1536,128]{1,0:T(8,128)(2,1)} %bitcast.14), channel_id=1, source_target_pairs={{0,224},{32,0},{64,32},{96,64},{128,96},{160,128},{192,160},{224,1... | collective-permute-start | bytes 1179656 | tf_op jit(solution)/shard_map/ppermute | solution.py:35
  19.9 10.2 %collective-permute-start.3 = (bf16[1536,128]{1,0:T(8,128)(2,1)S(1)}, bf16[1536,128]{1,0:T(8,128)(2,1)S(1)}, u32[]{:S(2)}, u32[]{:S(2)}) collective-permute-start(bf16[1536,128]{1,0:T(8,128)(2,1)S(1)} %collective-permute-done.1.refs_2_.refs_7_.refs_5_), channel_id=1, source_target_pairs={{0,32},{32,64},{64,96},{96,128},{128,160},{160,192},{192,224},{224... | collective-permute-start | bytes 1179656 | tf_op jit(solution)/shard_map/ppermute | solution.py:35
  21.4 29.0 %collective-permute-start.10 = (bf16[4,2,48,1536]{3,2,1,0:T(8,128)(2,1)}, bf16[4,2,48,1536]{3,2,1,0:T(8,128)(2,1)}, u32[]{:S(2)}, u32[]{:S(2)}) collective-permute-start(bf16[4,2,48,1536]{3,2,1,0:T(8,128)(2,1)} %get-tuple-element.36), channel_id=1, source_target_pairs={{0,24},{8,0},{16,8},{24,16},{1,25},{9,1},{17,9},{25,17},{2,26},{10... | collective-permute-start | bytes 3538952 | tf_op jit(solution)/shard_map/ppermute | solution.py:39
  22.6 27.7 %collective-permute-start.9 = (bf16[4,2,48,1536]{3,2,1,0:T(8,128)(2,1)}, bf16[4,2,48,1536]{3,2,1,0:T(8,128)(2,1)}, u32[]{:S(2)}, u32[]{:S(2)}) collective-permute-start(bf16[4,2,48,1536]{3,2,1,0:T(8,128)(2,1)} %get-tuple-element.35), channel_id=1, source_target_pairs={{0,8},{8,16},{16,24},{24,0},{1,9},{9,17},{17,25},{25,1},{2,10},{10... | collective-permute-start | bytes 3538952 | tf_op jit(solution)/shard_map/ppermute | solution.py:39
  22.9 11.6 %collective-permute-start.2 = (bf16[1536,128]{1,0:T(8,128)(2,1)S(1)}, bf16[1536,128]{1,0:T(8,128)(2,1)S(1)}, u32[]{:S(2)}, u32[]{:S(2)}) collective-permute-start(bf16[1536,128]{1,0:T(8,128)(2,1)S(1)} %collective-permute-done.refs_1_.refs_6_.refs_4_), channel_id=1, source_target_pairs={{0,224},{32,0},{64,32},{96,64},{128,96},{160,128},{192,160},{224,1... | collective-permute-start | bytes 1179656 | tf_op jit(solution)/shard_map/ppermute | solution.py:35
  30.1 9.4 %collective-permute-start.5 = (bf16[1536,128]{1,0:T(8,128)(2,1)S(1)}, bf16[1536,128]{1,0:T(8,128)(2,1)S(1)}, u32[]{:S(2)}, u32[]{:S(2)}) collective-permute-start(bf16[1536,128]{1,0:T(8,128)(2,1)S(1)} %collective-permute-done.3.refs_4_.refs_9_.refs_7_), channel_id=1, source_target_pairs={{0,32},{32,64},{64,96},{96,128},{128,160},{160,192},{192,224},{224... | collective-permute-start | bytes 1179656 | tf_op jit(solution)/shard_map/ppermute | solution.py:35
  34.5 9.1 %collective-permute-start.4 = (bf16[1536,128]{1,0:T(8,128)(2,1)S(1)}, bf16[1536,128]{1,0:T(8,128)(2,1)}, u32[]{:S(2)}, u32[]{:S(2)}) collective-permute-start(bf16[1536,128]{1,0:T(8,128)(2,1)S(1)} %collective-permute-done.2.refs_3_.refs_8_.refs_6_), channel_id=1, source_target_pairs={{0,224},{32,0},{64,32},{96,64},{128,96},{160,128},{192,160},{224,1... | collective-permute-start | bytes 1179656 | tf_op jit(solution)/shard_map/ppermute | solution.py:35
  39.5 8.6 %collective-permute-start.6 = (bf16[1536,128]{1,0:T(8,128)(2,1)S(1)}, bf16[1536,128]{1,0:T(8,128)(2,1)}, u32[]{:S(2)}, u32[]{:S(2)}) collective-permute-start(bf16[1536,128]{1,0:T(8,128)(2,1)S(1)} %collective-permute-done.5.refs_6_.refs_11_), channel_id=1, source_target_pairs={{0,32},{32,64},{64,96},{96,128},{128,160},{160,192},{192,224},{224... | collective-permute-start | bytes 1179656 | tf_op jit(solution)/shard_map/ppermute | solution.py:35
  39.6 10.8 %copy-start.1 = (bf16[8,1,48,1536]{3,2,1,0:T(8,128)(2,1)S(1)}, bf16[8,1,48,1536]{3,2,1,0:T(8,128)(2,1)}, u32[]{:S(2)}) copy-start(bf16[8,1,48,1536]{3,2,1,0:T(8,128)(2,1)} %param.6) | copy-start | bytes 3538948
  49.6 0.7 copy-start.3
  56.2 10.7 %collective-permute-start.11 = (f32[4,48,2816]{2,1,0:T(8,128)S(1)}, f32[4,48,2816]{2,1,0:T(8,128)S(1)}, u32[]{:S(2)}, u32[]{:S(2)}) collective-permute-start(f32[4,48,2816]{2,1,0:T(8,128)S(1)} %get-tuple-element.43), channel_id=1, source_target_pairs={{0,1},{1,0},{2,3},{3,2},{4,5},{5,4},{6,7},{7,6},{8,9},{9,8},{10,11... | collective-permute-start | bytes 6488072 | tf_op jit(solution)/shard_map/ppermute | solution.py:51
  63.4 2.7 %collective-permute-start.12 = (f32[4,48,1280]{2,1,0:T(8,128)S(1)}, f32[4,48,1280]{2,1,0:T(8,128)S(1)}, u32[]{:S(2)}, u32[]{:S(2)}) collective-permute-start(f32[4,48,1280]{2,1,0:T(8,128)S(1)} %get-tuple-element.48), channel_id=1, source_target_pairs={{0,1},{1,0},{2,3},{3,2},{4,5},{5,4},{6,7},{7,6},{8,9},{9,8},{10,11... | collective-permute-start | bytes 2949128 | tf_op jit(solution)/shard_map/ppermute | solution.py:51
  69.5 4.2 %copy-start.4 = (bf16[192,1024]{1,0:T(8,128)(2,1)S(1)}, bf16[192,1024]{1,0:T(8,128)(2,1)}, u32[]{:S(2)}) copy-start(bf16[192,1024]{1,0:T(8,128)(2,1)} %copy-done.3) | copy-start | bytes 1179652
  69.5 5.1 %copy-start.5 = (s32[32]{0:T(128)S(1)}, s32[32]{0:T(128)}, u32[]{:S(2)}) copy-start(s32[32]{0:T(128)} %pair_ref.1) | copy-start | bytes 388
  69.5 5.1 %copy-start.6 = (s32[32]{0:T(128)S(1)}, s32[32]{0:T(128)}, u32[]{:S(2)}) copy-start(s32[32]{0:T(128)} %block_ref.1) | copy-start | bytes 388
  69.5 5.1 %copy-start.7 = (s32[32]{0:T(128)S(1)}, s32[32]{0:T(128)}, u32[]{:S(2)}) copy-start(s32[32]{0:T(128)} %live_ref.1) | copy-start | bytes 388
  69.5 24.9 %all-to-all-start = ((s16[4,48,4224]{2,1,0:T(8,128)(2,1)}), s16[4,48,4224]{2,1,0:T(8,128)(2,1)S(1)}, u32[]{:S(2)}, u32[]{:S(2)}) async-start(s16[4,48,4224]{2,1,0:T(8,128)(2,1)} %shard_map.74), calls=%async_computation | async-start | bytes 3244032 | tf_op jit(solution)/shard_map/all_to_all | solution.py:363
  73.7 10.1 %collective-permute-start.13 = (bf16[192,1024]{1,0:T(8,128)(2,1)S(1)}, bf16[192,1024]{1,0:T(8,128)(2,1)S(1)}, u32[]{:S(2)}, u32[]{:S(2)}) collective-permute-start(bf16[192,1024]{1,0:T(8,128)(2,1)S(1)} %copy-done.4), channel_id=1, source_target_pairs={{0,24},{8,0},{16,8},{24,16},{1,25},{9,1},{17,9},{25,17},{2,26},{10... | collective-permute-start | bytes 1179656 | tf_op jit(solution)/shard_map/ppermute | solution.py:39
  74.6 11.2 %collective-permute-start.14 = (bf16[192,1024]{1,0:T(8,128)(2,1)S(1)}, bf16[192,1024]{1,0:T(8,128)(2,1)S(1)}, u32[]{:S(2)}, u32[]{:S(2)}) collective-permute-start(bf16[192,1024]{1,0:T(8,128)(2,1)S(1)} %copy-done.4), channel_id=1, source_target_pairs={{0,16},{8,24},{16,0},{24,8},{1,17},{9,25},{17,1},{25,9},{2,18},{10... | collective-permute-start | bytes 1179656 | tf_op jit(solution)/shard_map/ppermute | solution.py:39
  97.1 3.9 %collective-permute-start.15 = (bf16[64,1024]{1,0:T(8,128)(2,1)S(1)}, bf16[64,1024]{1,0:T(8,128)(2,1)S(1)}, u32[]{:S(2)}, u32[]{:S(2)}) collective-permute-start(bf16[64,1024]{1,0:T(8,128)(2,1)S(1)} %get-tuple-element.53), channel_id=1, source_target_pairs={{0,24},{2,26},{4,12},{6,14},{8,0},{10,2},{12,20},{14,22},{16,8},{1... | collective-permute-start | bytes 393224 | tf_op jit(solution)/shard_map/ppermute | solution.py:47
  98.1 5.6 %collective-permute-start.16 = (bf16[64,1024]{1,0:T(8,128)(2,1)S(1)}, bf16[64,1024]{1,0:T(8,128)(2,1)S(1)}, u32[]{:S(2)}, u32[]{:S(2)}) collective-permute-start(bf16[64,1024]{1,0:T(8,128)(2,1)S(1)} %get-tuple-element.54), channel_id=1, source_target_pairs={{0,8},{2,10},{4,28},{6,30},{8,16},{10,18},{12,4},{14,6},{16,24},{1... | collective-permute-start | bytes 393224 | tf_op jit(solution)/shard_map/ppermute | solution.py:47
  98.6 7.0 %collective-permute-start.17 = (bf16[64,1024]{1,0:T(8,128)(2,1)S(1)}, bf16[64,1024]{1,0:T(8,128)(2,1)S(1)}, u32[]{:S(2)}, u32[]{:S(2)}) collective-permute-start(bf16[64,1024]{1,0:T(8,128)(2,1)S(1)} %get-tuple-element.55), channel_id=1, source_target_pairs={{0,16},{2,18},{4,20},{6,22},{8,24},{10,26},{12,28},{14,30},{16,0},... | collective-permute-start | bytes 393224 | tf_op jit(solution)/shard_map/ppermute | solution.py:47

commit v6 on v5

--- a/solution.py
+++ b/solution.py
@@ -302,32 +302,55 @@
 
 
 def place_kernel(at_ref, *refs):
-    *piece_refs, out_ref, bmat_ref = refs
+    *piece_refs, out_ref = refs
     _, width, columns = out_ref.shape
-    bmat = 0.0
     for k, piece_ref in enumerate(piece_refs):
         owner = lax.rem(at_ref[2] + NY - offset_at(k, at_ref[3]), NY)
         for j, e in enumerate(ORDER):
             slot = lax.rem(at_ref[1] + e, NZ) * NY + owner
             out_ref[slot] = piece_ref[:width, j * columns : (j + 1) * columns]
-        tail = piece_ref[width:, :columns].astype(jnp.float32)
-        bmat = bmat + tail.sum(0, keepdims=True)
-    bmat_ref[...] = jnp.broadcast_to(bmat, bmat_ref.shape)
 
 
 def place(at, pieces, columns):
     width = pieces[0].shape[0] - TAIL
     return pl.pallas_call(
         place_kernel,
-        out_shape=[
-            jax.ShapeDtypeStruct((NZ * NY, width, columns), jnp.bfloat16),
-            jax.ShapeDtypeStruct((NZ * NX * NC, columns), jnp.float32),
+        out_shape=jax.ShapeDtypeStruct((NZ * NY, width, columns), jnp.bfloat16),
+        in_specs=[SMEM] + [VMEM] * len(pieces),
+        out_specs=VMEM,
+        compiler_params=pltpu.CompilerParams(vmem_limit_bytes=8 * 2**20),
+        cost_estimate=CHEAP,
+    )(at, *pieces)
+
+
+def terms_kernel(*refs):
+    *piece_refs, bmat_ref, held, arrived = refs
+    width, columns = held.shape[1:]
+    copies = [
+        pltpu.make_async_copy(ref.at[ref.shape[0] - width :, :columns], held.at[i], arrived.at[i])
+        for i, ref in enumerate(piece_refs)
+    ]
+    for copy in copies:
+        copy.start()
+    for copy in copies:
+        copy.wait()
+    bmat = held[...].astype(jnp.float32).sum(0).sum(0, keepdims=True)
+    bmat_ref[...] = jnp.broadcast_to(bmat, bmat_ref.shape)
+
+
+def terms(pieces, columns):
+    return pl.pallas_call(
+        terms_kernel,
+        out_shape=jax.ShapeDtypeStruct((NZ * NX * NC, columns), jnp.float32),
+        in_specs=[ANY] * len(pieces),
+        out_specs=VMEM,
+        scratch_shapes=[
+            pltpu.VMEM((len(pieces), TAIL, columns), jnp.bfloat16),
+            pltpu.SemaphoreType.DMA((len(pieces),)),
         ],
-        in_specs=[SMEM] + [VMEM] * len(pieces),
-        out_specs=[VMEM] * 2,
-        compiler_params=pltpu.CompilerParams(vmem_limit_bytes=8 * 2**20),
-        cost_estimate=CHEAP,
-    )(at, *pieces)
+        compiler_params=pltpu.CompilerParams(vmem_limit_bytes=4 * 2**20),
+        cost_estimate=CHEAP,
+    )(*pieces)
 
 
 def on_device(geminal, fock_matrix, slot_occupied_pair, slot_column_block, slot_live):
@@ -378,8 +401,9 @@
     recv, keep = start(SECOND, ORDER, f_arrays)
     total = spread(pack(keep, recv, (packed,)))
     done = finish(places(FIRST + SECOND), at, total, mask, weight, rows)
-    out, bmat = place(at, [to_owner(v, j) for j, v in enumerate(done)], columns)
-    bmat = lax.all_to_all(bmat, ("z", "x", "c"), 0, 0, tiled=True)
+    pieces = [to_owner(v, j) for j, v in enumerate(done)]
+    out = place(at, pieces, columns)
+    bmat = lax.all_to_all(terms(pieces, columns), ("z", "x", "c"), 0, 0, tiled=True)
     return out, bmat[:, :4].sum(0).reshape(2, 2)
 
 

time: 127 us -> 127 us (level)
  blocking collectives: 19.3 us -> 0 us
  starting transfers between devices: 31.6 us -> 41.7 us
  waiting for transfers between devices: 52.1 us -> 60.1 us
    all_to_all x1 -> x0, blocking collectives: 19.3 us -> none  [on_device(): bmat = lax.all_to_all(bmat, ('z', 'x', 'c'), 0, 0, tiled=True)]
    all_to_all x0 -> x1, starting transfers between devices: none -> 10.1 us  [on_device(): lax.all_to_all(terms(pieces, columns), ('z', 'x', 'c'), 0, 0, tiled=True)]
    all_to_all x0 -> x1, waiting for transfers between devices: none -> 8 us  [on_device(): lax.all_to_all(terms(pieces, columns), ('z', 'x', 'c'), 0, 0, tiled=True)]
  transfers between devices with their start and end apart: 19 -> 20, of which waited for: 13 -> 14; matrix products, arithmetic and copies ran while one was open for 0% -> 0% of each run, Pallas kernels for 6% -> 7%
where the time goes in v6:
time: 127 us
  waiting for transfers between devices  60.1 us (47%)
  starting transfers between devices  41.7 us (33%)
  Pallas kernels  21.2 us (17%)
  local copies, waits for them, and re-layouts  2.67 us (2%)
    ppermute x7, waiting for transfers between devices, shift_z(): return lax.ppermute(v, 'z', [(z, (z + s) % NZ) for z in range(NZ)])  25 us
    ppermute x7, starting transfers between devices, shift_z(): return lax.ppermute(v, 'z', [(z, (z + s) % NZ) for z in range(NZ)])  14.3 us
    all_to_all x1, starting transfers between devices, on_device(): lax.all_to_all(terms(pieces, columns), ('z', 'x', 'c'), 0, 0, tiled=True)  10.1 us
    ppermute x6, waiting for transfers between devices, shift_y(): return lax.ppermute(v, 'y', [(y, (y + s) % NY) for y in range(NY)])  9.72 us
    all_to_all x1, waiting for transfers between devices, spread(): return lax.all_to_all(total, 'x', 0, 0)  8.55 us
    pallas_call x2, Pallas kernels, products(): pl.pallas_call(functools.partial(products_kernel, plan, len(f_arrays), le...  8.5 us
    all_to_all x1, waiting for transfers between devices, on_device(): lax.all_to_all(terms(pieces, columns), ('z', 'x', 'c'), 0, 0, tiled=True)  8 us
    ppermute x3, waiting for transfers between devices, to_owner(): return lax.ppermute(v, ('y', 'x'), moves) if j else v  6.27 us
  transfers between devices with their start and end apart: 20, of which 14 were waited for; matrix products, arithmetic and copies ran while one was open for 0% of the time, Pallas kernels for 7%

profile of v6, /device:TPU:1, one launch (start us, length us, event | category | flops | bytes accessed | tf_op | source)
XLA Modules:
  0.0 126.5 jit_solution(11368124900899517763)
XLA Ops:
  0.6 0.0 copy-start
  0.6 1.3 copy-done
  1.9 0.1 shard_map.68
  2.0 2.2 %collective-permute-start.7 = (bf16[2,2,48,1536]{3,2,1,0:T(8,128)(2,1)S(1)}, bf16[2,2,48,1536]{3,2,1,0:T(8,128)(2,1)S(1)}, u32[]{:S(2)}, u32[]{:S(2)}) collective-permute-start(bf16[2,2,48,1536]{3,2,1,0:T(8,128)(2,1)S(1)} %get-tuple-element.31.low_ref), channel_id=1, source_target_pairs={{0,8},{8,16},{16,24},{24,0},{1,9},{9,17},{17,25},{25,1},{2,10},{10... | collective-permute-start | bytes 1769480 | tf_op jit(solution)/shard_map/ppermute | solution.py:39
  4.2 1.5 %collective-permute-start.8 = (bf16[2,2,48,1536]{3,2,1,0:T(8,128)(2,1)S(1)}, bf16[2,2,48,1536]{3,2,1,0:T(8,128)(2,1)S(1)}, u32[]{:S(2)}, u32[]{:S(2)}) collective-permute-start(bf16[2,2,48,1536]{3,2,1,0:T(8,128)(2,1)S(1)} %get-tuple-element.32.high_ref), channel_id=1, source_target_pairs={{0,24},{8,0},{16,8},{24,16},{1,25},{9,1},{17,9},{25,17},{2,26},{10... | collective-permute-start | bytes 1769480 | tf_op jit(solution)/shard_map/ppermute | solution.py:39
  5.7 1.6 %collective-permute-start.1 = (bf16[1536,128]{1,0:T(8,128)(2,1)}, bf16[1536,128]{1,0:T(8,128)(2,1)S(1)}, u32[]{:S(2)}, u32[]{:S(2)}) collective-permute-start(bf16[1536,128]{1,0:T(8,128)(2,1)} %bitcast.13), channel_id=1, source_target_pairs={{0,32},{32,64},{64,96},{96,128},{128,160},{160,192},{192,224},{224... | collective-permute-start | bytes 1179656 | tf_op jit(solution)/shard_map/ppermute | solution.py:35
  7.4 3.9 %collective-permute-start = (bf16[1536,128]{1,0:T(8,128)(2,1)}, bf16[1536,128]{1,0:T(8,128)(2,1)S(1)}, u32[]{:S(2)}, u32[]{:S(2)}) collective-permute-start(bf16[1536,128]{1,0:T(8,128)(2,1)} %bitcast.14), channel_id=1, source_target_pairs={{0,224},{32,0},{64,32},{96,64},{128,96},{160,128},{192,160},{224,1... | collective-permute-start | bytes 1179656 | tf_op jit(solution)/shard_map/ppermute | solution.py:35
  11.3 8.6 %collective-permute-done.1.refs_2_.refs_7_.refs_5_ = bf16[1536,128]{1,0:T(8,128)(2,1)S(1)} collective-permute-done((bf16[1536,128]{1,0:T(8,128)(2,1)}, bf16[1536,128]{1,0:T(8,128)(2,1)S(1)}, u32[]{:S(2)}, u32[]{:S(2)}) %collective-permute-start.1) | collective-permute-done | bytes 393248 | tf_op jit(solution)/shard_map/ppermute | solution.py:35
  19.9 0.0 collective-permute-start.3
  19.9 1.5 %shard_map.70 = (bf16[4,2,48,1536]{3,2,1,0:T(8,128)(2,1)}, bf16[4,2,48,1536]{3,2,1,0:T(8,128)(2,1)}) custom-call(bf16[2,2,48,1536]{3,2,1,0:T(8,128)(2,1)S(1)} %get-tuple-element.31.low_ref, bf16[2,2,48,1536]{3,2,1,0:T(8,128)(2,1)S(1)} %get-tuple-element.32.high_ref, bf16[2,2,48,1536]{3,2,1,0:T(8,128)(2,1)S(1)} %collective-permute-done.7.left_ref.refs_1_, ...), custom_call_target="tpu_custom_call" | custom-call | flops 1 | bytes 1 | tf_op jit(solution)/shard_map/pallas_call | solution.py:89
  21.3 1.3 %collective-permute-start.10 = (bf16[4,2,48,1536]{3,2,1,0:T(8,128)(2,1)}, bf16[4,2,48,1536]{3,2,1,0:T(8,128)(2,1)}, u32[]{:S(2)}, u32[]{:S(2)}) collective-permute-start(bf16[4,2,48,1536]{3,2,1,0:T(8,128)(2,1)} %get-tuple-element.34), channel_id=1, source_target_pairs={{0,24},{8,0},{16,8},{24,16},{1,25},{9,1},{17,9},{25,17},{2,26},{10... | collective-permute-start | bytes 3538952 | tf_op jit(solution)/shard_map/ppermute | solution.py:39
  22.6 0.3 collective-permute-start.9
  22.9 5.2 %collective-permute-start.2 = (bf16[1536,128]{1,0:T(8,128)(2,1)S(1)}, bf16[1536,128]{1,0:T(8,128)(2,1)S(1)}, u32[]{:S(2)}, u32[]{:S(2)}) collective-permute-start(bf16[1536,128]{1,0:T(8,128)(2,1)S(1)} %collective-permute-done.refs_1_.refs_6_.refs_4_), channel_id=1, source_target_pairs={{0,224},{32,0},{64,32},{96,64},{128,96},{160,128},{192,160},{224,1... | collective-permute-start | bytes 1179656 | tf_op jit(solution)/shard_map/ppermute | solution.py:35
  28.1 2.0 %collective-permute-done.3.refs_4_.refs_9_.refs_7_ = bf16[1536,128]{1,0:T(8,128)(2,1)S(1)} collective-permute-done((bf16[1536,128]{1,0:T(8,128)(2,1)S(1)}, bf16[1536,128]{1,0:T(8,128)(2,1)S(1)}, u32[]{:S(2)}, u32[]{:S(2)}) %collective-permute-start.3) | collective-permute-done | bytes 393248 | tf_op jit(solution)/shard_map/ppermute | solution.py:35
  30.1 4.4 %collective-permute-done.2.refs_3_.refs_8_.refs_6_ = bf16[1536,128]{1,0:T(8,128)(2,1)S(1)} collective-permute-done((bf16[1536,128]{1,0:T(8,128)(2,1)S(1)}, bf16[1536,128]{1,0:T(8,128)(2,1)S(1)}, u32[]{:S(2)}, u32[]{:S(2)}) %collective-permute-start.2) | collective-permute-done | bytes 393248 | tf_op jit(solution)/shard_map/ppermute | solution.py:35
  34.5 3.5 %collective-permute-start.4 = (bf16[1536,128]{1,0:T(8,128)(2,1)S(1)}, bf16[1536,128]{1,0:T(8,128)(2,1)}, u32[]{:S(2)}, u32[]{:S(2)}) collective-permute-start(bf16[1536,128]{1,0:T(8,128)(2,1)S(1)} %collective-permute-done.2.refs_3_.refs_8_.refs_6_), channel_id=1, source_target_pairs={{0,224},{32,0},{64,32},{96,64},{128,96},{160,128},{192,160},{224,1... | collective-permute-start | bytes 1179656 | tf_op jit(solution)/shard_map/ppermute | solution.py:35
  38.0 1.5 %collective-permute-done.5.refs_6_.refs_11_ = bf16[1536,128]{1,0:T(8,128)(2,1)S(1)} collective-permute-done((bf16[1536,128]{1,0:T(8,128)(2,1)S(1)}, bf16[1536,128]{1,0:T(8,128)(2,1)S(1)}, u32[]{:S(2)}, u32[]{:S(2)}) %collective-permute-start.5) | collective-permute-done | bytes 393248 | tf_op jit(solution)/shard_map/ppermute | solution.py:35
  39.5 0.1 pad_add_fusion.at_ref
  39.6 4.1 %collective-permute-done.4.refs_5_.refs_10_ = bf16[1536,128]{1,0:T(8,128)(2,1)} collective-permute-done((bf16[1536,128]{1,0:T(8,128)(2,1)S(1)}, bf16[1536,128]{1,0:T(8,128)(2,1)}, u32[]{:S(2)}, u32[]{:S(2)}) %collective-permute-start.4) | collective-permute-done | bytes 393248 | tf_op jit(solution)/shard_map/ppermute | solution.py:35
  43.6 4.4 %collective-permute-done.6.refs_7_.refs_12_ = bf16[1536,128]{1,0:T(8,128)(2,1)} collective-permute-done((bf16[1536,128]{1,0:T(8,128)(2,1)S(1)}, bf16[1536,128]{1,0:T(8,128)(2,1)}, u32[]{:S(2)}, u32[]{:S(2)}) %collective-permute-start.6) | collective-permute-done | bytes 393248 | tf_op jit(solution)/shard_map/ppermute | solution.py:35
  48.1 1.5 %shard_map.69.refs_0_ = bf16[192,1024]{1,0:T(8,128)(2,1)S(1)} custom-call(s32[4]{0:T(128)S(1)} %pad_add_fusion.at_ref, bf16[1536,128]{1,0:T(8,128)(2,1)S(1)} %bitcast.15, bf16[1536,128]{1,0:T(8,128)(2,1)S(1)} %collective-permute-done.refs_1_.refs_6_.refs_4_, bf16[1536,128]{1,0:T(8,128)(2,1)S(1)} %collective-permute-done.1.refs_2_.refs_7_.refs_5_, ...), custom_call_target="tpu_custom_call" | custom-call | flops 1 | bytes 1 | tf_op jit(solution)/shard_map/pallas_call | solution.py:293
  49.6 0.0 copy-start.3
  49.6 0.7 copy-done.3
  50.4 5.8 %shard_map.71 = (f32[4,48,2816]{2,1,0:T(8,128)S(1)}, f32[4,48,2816]{2,1,0:T(8,128)S(1)}) custom-call(s32[4]{0:T(128)S(1)} %pad_add_fusion.at_ref, bf16[4,2,48,1536]{3,2,1,0:T(8,128)(2,1)S(1)} %bitcast.11, bf16[2,2,48,1536]{3,2,1,0:T(8,128)(2,1)S(1)} %collective-permute-done.7.left_ref.refs_1_, ...), custom_call_target="tpu_custom_call" | custom-call | flops 1 | bytes 1 | tf_op jit(solution)/shard_map/pallas_call | solution.py:169
  56.2 4.5 %collective-permute-start.11 = (f32[4,48,2816]{2,1,0:T(8,128)S(1)}, f32[4,48,2816]{2,1,0:T(8,128)S(1)}, u32[]{:S(2)}, u32[]{:S(2)}) collective-permute-start(f32[4,48,2816]{2,1,0:T(8,128)S(1)} %get-tuple-element.41), channel_id=1, source_target_pairs={{0,1},{1,0},{2,3},{3,2},{4,5},{5,4},{6,7},{7,6},{8,9},{9,8},{10,11... | collective-permute-start | bytes 6488072 | tf_op jit(solution)/shard_map/ppermute | solution.py:51
  60.7 2.7 %shard_map.72 = (f32[4,48,1280]{2,1,0:T(8,128)S(1)}, f32[4,48,1280]{2,1,0:T(8,128)S(1)}) custom-call(s32[4]{0:T(128)S(1)} %pad_add_fusion.at_ref, bf16[4,2,48,1536]{3,2,1,0:T(8,128)(2,1)S(1)} %bitcast.12, bf16[2,2,48,1536]{3,2,1,0:T(8,128)(2,1)S(1)} %collective-permute-done.7.left_ref.refs_1_, ...), custom_call_target="tpu_custom_call" | custom-call | flops 1 | bytes 1 | tf_op jit(solution)/shard_map/pallas_call | solution.py:169
  63.4 0.1 collective-permute-start.12
  63.5 2.5 %collective-permute-done.12.recv_ref = f32[4,48,1280]{2,1,0:T(8,128)S(1)} collective-permute-done((f32[4,48,1280]{2,1,0:T(8,128)S(1)}, f32[4,48,1280]{2,1,0:T(8,128)S(1)}, u32[]{:S(2)}, u32[]{:S(2)}) %collective-permute-start.12) | collective-permute-done | bytes 983072 | tf_op jit(solution)/shard_map/ppermute | solution.py:51
  66.1 0.9 shard_map.73.refs_0_
  66.9 2.6 %shard_map.74 = s16[4,48,4224]{2,1,0:T(8,128)(2,1)} custom-call(f32[4,48,2816]{2,1,0:T(8,128)S(1)} %get-tuple-element.40.keep_ref, f32[4,48,2816]{2,1,0:T(8,128)S(1)} %collective-permute-done.11.recv_ref, s16[4,48,1408]{2,1,0:T(8,128)(2,1)S(1)} %shard_map.73.refs_0_), custom_call_target="tpu_custom_call" | custom-call | flops 1 | bytes 1 | tf_op jit(solution)/shard_map/pallas_call | solution.py:130
  69.5 4.2 %all-to-all-start = ((s16[4,48,4224]{2,1,0:T(8,128)(2,1)}), s16[4,48,4224]{2,1,0:T(8,128)(2,1)S(1)}, u32[]{:S(2)}, u32[]{:S(2)}) async-start(s16[4,48,4224]{2,1,0:T(8,128)(2,1)} %shard_map.74), calls=%async_computation | async-start | bytes 3244032 | tf_op jit(solution)/shard_map/all_to_all | solution.py:386
  73.7 0.9 collective-permute-start.13
  74.6 1.5 %shard_map.75 = (f32[192,128]{1,0:T(8,128)S(1)}, f32[1,1024]{1,0:T(1,128)S(1)}) custom-call(s32[4]{0:T(128)S(1)} %pad_add_fusion.at_ref, s32[32]{0:T(128)S(1)} %copy-done.5, s32[32]{0:T(128)S(1)} %copy-done.6, s32[32]{0:T(128)S(1)} %copy-done.7), custom_call_target="tpu_custom_call" | custom-call | flops 1 | bytes 1 | tf_op jit(solution)/shard_map/pallas_call | solution.py:203
  76.2 7.6 %collective-permute-done.13.refs_1_ = bf16[192,1024]{1,0:T(8,128)(2,1)S(1)} collective-permute-done((bf16[192,1024]{1,0:T(8,128)(2,1)S(1)}, bf16[192,1024]{1,0:T(8,128)(2,1)S(1)}, u32[]{:S(2)}, u32[]{:S(2)}) %collective-permute-start.13) | collective-permute-done | bytes 393248 | tf_op jit(solution)/shard_map/ppermute | solution.py:39
  83.8 2.1 %collective-permute-done.14.refs_2_ = bf16[192,1024]{1,0:T(8,128)(2,1)S(1)} collective-permute-done((bf16[192,1024]{1,0:T(8,128)(2,1)S(1)}, bf16[192,1024]{1,0:T(8,128)(2,1)S(1)}, u32[]{:S(2)}, u32[]{:S(2)}) %collective-permute-start.14) | collective-permute-done | bytes 393248 | tf_op jit(solution)/shard_map/ppermute | solution.py:39
  85.9 8.5 %all-to-all-done.total_ref = s16[4,48,4224]{2,1,0:T(8,128)(2,1)S(1)} async-done(((s16[4,48,4224]{2,1,0:T(8,128)(2,1)}), s16[4,48,4224]{2,1,0:T(8,128)(2,1)S(1)}, u32[]{:S(2)}, u32[]{:S(2)}) %all-to-all-start) | async-done | bytes 1622048 | tf_op jit(solution)/shard_map/all_to_all | solution.py:386
  94.4 2.7 %shard_map.76 = (bf16[64,1024]{1,0:T(8,128)(2,1)S(1)}, bf16[64,1024]{1,0:T(8,128)(2,1)S(1)}, bf16[64,1024]{1,0:T(8,128)(2,1)S(1)}, bf16[64,1024]{1,0:T(8,128)(2,1)S(1)}) custom-call(s32[4]{0:T(128)S(1)} %pad_add_fusion.at_ref, s16[4,48,4224]{2,1,0:T(8,128)(2,1)S(1)} %all-to-all-done.total_ref, f32[1,1024]{1,0:T(1,128)S(1)} %get-tuple-element.47.mask_ref, ...), custom_call_target="tpu_custom_call" | custom-call | flops 1 | bytes 1 | tf_op jit(solution)/shard_map/pallas_call | solution.py:262
  97.1 1.0 collective-permute-start.15
  98.1 0.5 collective-permute-start.16
  98.6 0.7 collective-permute-start.17
  99.4 1.6 %collective-permute-done.15.refs_1_ = bf16[64,1024]{1,0:T(8,128)(2,1)S(1)} collective-permute-done((bf16[64,1024]{1,0:T(8,128)(2,1)S(1)}, bf16[64,1024]{1,0:T(8,128)(2,1)S(1)}, u32[]{:S(2)}, u32[]{:S(2)}) %collective-permute-start.15) | collective-permute-done | bytes 131104 | tf_op jit(solution)/shard_map/ppermute | solution.py:47
  101.0 2.7 %collective-permute-done.16.refs_2_ = bf16[64,1024]{1,0:T(8,128)(2,1)S(1)} collective-permute-done((bf16[64,1024]{1,0:T(8,128)(2,1)S(1)}, bf16[64,1024]{1,0:T(8,128)(2,1)S(1)}, u32[]{:S(2)}, u32[]{:S(2)}) %collective-permute-start.16) | collective-permute-done | bytes 131104 | tf_op jit(solution)/shard_map/ppermute | solution.py:47
  103.7 2.0 %collective-permute-done.17.refs_3_ = bf16[64,1024]{1,0:T(8,128)(2,1)S(1)} collective-permute-done((bf16[64,1024]{1,0:T(8,128)(2,1)S(1)}, bf16[64,1024]{1,0:T(8,128)(2,1)S(1)}, u32[]{:S(2)}, u32[]{:S(2)}) %collective-permute-start.17) | collective-permute-done | bytes 131104 | tf_op jit(solution)/shard_map/ppermute | solution.py:47
  105.6 0.7 shard_map.78
  106.3 10.1 %all-to-all-start.1 = ((f32[64,1,128]{2,1,0:T(1,128)}), f32[64,1,128]{2,1,0:T(1,128)S(1)}, u32[]{:S(2)}, u32[]{:S(2)}) async-start(f32[64,1,128]{2,1,0:T(1,128)} %bitcast.7), calls=%async_computation.1 | async-start | bytes 65536 | tf_op jit(solution)/shard_map/all_to_all | solution.py:406
  116.5 1.4 %shard_map.77 = bf16[32,48,128]{2,1,0:T(8,128)(2,1)} custom-call(s32[4]{0:T(128)S(1)} %pad_add_fusion.at_ref, bf16[64,1024]{1,0:T(8,128)(2,1)S(1)} %get-tuple-element.50.refs_0_, bf16[64,1024]{1,0:T(8,128)(2,1)S(1)} %collective-permute-done.15.refs_1_, bf16[64,1024]{1,0:T(8,128)(2,1)S(1)} %collective-permute-done.16.refs_2_, ...), custom_call_target="tpu_custom_call" | custom-call | flops 1 | bytes 1 | tf_op jit(solution)/shard_map/pallas_call | solution.py:316
  117.8 8.0 %all-to-all-done.1 = f32[64,1,128]{2,1,0:T(1,128)S(1)} async-done(((f32[64,1,128]{2,1,0:T(1,128)}), f32[64,1,128]{2,1,0:T(1,128)S(1)}, u32[]{:S(2)}, u32[]{:S(2)}) %all-to-all-start.1) | async-done | bytes 32800 | tf_op jit(solution)/shard_map/all_to_all | solution.py:406
  125.9 0.6 reshape.13
  (22 shorter events, 0.1 us)
Async XLA Ops:
  0.6 1.3 %copy-start = (bf16[8,1,48,1536]{3,2,1,0:T(8,128)(2,1)S(1)}, bf16[8,1,48,1536]{3,2,1,0:T(8,128)(2,1)}, u32[]{:S(2)}) copy-start(bf16[8,1,48,1536]{3,2,1,0:T(8,128)(2,1)} %param.6) | copy-start | bytes 3538948
  1.9 46.2 %copy-start.2 = (bf16[1,1536,128]{2,1,0:T(8,128)(2,1)S(1)}, bf16[1,1536,128]{2,1,0:T(8,128)(2,1)}, u32[]{:S(2)}) copy-start(bf16[1,1536,128]{2,1,0:T(8,128)(2,1)} %param.5) | copy-start | bytes 1179652
  2.0 17.9 %collective-permute-start.7 = (bf16[2,2,48,1536]{3,2,1,0:T(8,128)(2,1)S(1)}, bf16[2,2,48,1536]{3,2,1,0:T(8,128)(2,1)S(1)}, u32[]{:S(2)}, u32[]{:S(2)}) collective-permute-start(bf16[2,2,48,1536]{3,2,1,0:T(8,128)(2,1)S(1)} %get-tuple-element.31.low_ref), channel_id=1, source_target_pairs={{0,8},{8,16},{16,24},{24,0},{1,9},{9,17},{17,25},{25,1},{2,10},{10... | collective-permute-start | bytes 1769480 | tf_op jit(solution)/shard_map/ppermute | solution.py:39
  4.2 15.7 %collective-permute-start.8 = (bf16[2,2,48,1536]{3,2,1,0:T(8,128)(2,1)S(1)}, bf16[2,2,48,1536]{3,2,1,0:T(8,128)(2,1)S(1)}, u32[]{:S(2)}, u32[]{:S(2)}) collective-permute-start(bf16[2,2,48,1536]{3,2,1,0:T(8,128)(2,1)S(1)} %get-tuple-element.32.high_ref), channel_id=1, source_target_pairs={{0,24},{8,0},{16,8},{24,16},{1,25},{9,1},{17,9},{25,17},{2,26},{10... | collective-permute-start | bytes 1769480 | tf_op jit(solution)/shard_map/ppermute | solution.py:39
  5.7 14.2 %collective-permute-start.1 = (bf16[1536,128]{1,0:T(8,128)(2,1)}, bf16[1536,128]{1,0:T(8,128)(2,1)S(1)}, u32[]{:S(2)}, u32[]{:S(2)}) collective-permute-start(bf16[1536,128]{1,0:T(8,128)(2,1)} %bitcast.13), channel_id=1, source_target_pairs={{0,32},{32,64},{64,96},{96,128},{128,160},{160,192},{192,224},{224... | collective-permute-start | bytes 1179656 | tf_op jit(solution)/shard_map/ppermute | solution.py:35
  7.4 15.5 %collective-permute-start = (bf16[1536,128]{1,0:T(8,128)(2,1)}, bf16[1536,128]{1,0:T(8,128)(2,1)S(1)}, u32[]{:S(2)}, u32[]{:S(2)}) collective-permute-start(bf16[1536,128]{1,0:T(8,128)(2,1)} %bitcast.14), channel_id=1, source_target_pairs={{0,224},{32,0},{64,32},{96,64},{128,96},{160,128},{192,160},{224,1... | collective-permute-start | bytes 1179656 | tf_op jit(solution)/shard_map/ppermute | solution.py:35
  19.9 10.2 %collective-permute-start.3 = (bf16[1536,128]{1,0:T(8,128)(2,1)S(1)}, bf16[1536,128]{1,0:T(8,128)(2,1)S(1)}, u32[]{:S(2)}, u32[]{:S(2)}) collective-permute-start(bf16[1536,128]{1,0:T(8,128)(2,1)S(1)} %collective-permute-done.1.refs_2_.refs_7_.refs_5_), channel_id=1, source_target_pairs={{0,32},{32,64},{64,96},{96,128},{128,160},{160,192},{192,224},{224... | collective-permute-start | bytes 1179656 | tf_op jit(solution)/shard_map/ppermute | solution.py:35
  21.3 29.0 %collective-permute-start.10 = (bf16[4,2,48,1536]{3,2,1,0:T(8,128)(2,1)}, bf16[4,2,48,1536]{3,2,1,0:T(8,128)(2,1)}, u32[]{:S(2)}, u32[]{:S(2)}) collective-permute-start(bf16[4,2,48,1536]{3,2,1,0:T(8,128)(2,1)} %get-tuple-element.34), channel_id=1, source_target_pairs={{0,24},{8,0},{16,8},{24,16},{1,25},{9,1},{17,9},{25,17},{2,26},{10... | collective-permute-start | bytes 3538952 | tf_op jit(solution)/shard_map/ppermute | solution.py:39
  22.6 27.7 %collective-permute-start.9 = (bf16[4,2,48,1536]{3,2,1,0:T(8,128)(2,1)}, bf16[4,2,48,1536]{3,2,1,0:T(8,128)(2,1)}, u32[]{:S(2)}, u32[]{:S(2)}) collective-permute-start(bf16[4,2,48,1536]{3,2,1,0:T(8,128)(2,1)} %get-tuple-element.33), channel_id=1, source_target_pairs={{0,8},{8,16},{16,24},{24,0},{1,9},{9,17},{17,25},{25,1},{2,10},{10... | collective-permute-start | bytes 3538952 | tf_op jit(solution)/shard_map/ppermute | solution.py:39
  22.9 11.6 %collective-permute-start.2 = (bf16[1536,128]{1,0:T(8,128)(2,1)S(1)}, bf16[1536,128]{1,0:T(8,128)(2,1)S(1)}, u32[]{:S(2)}, u32[]{:S(2)}) collective-permute-start(bf16[1536,128]{1,0:T(8,128)(2,1)S(1)} %collective-permute-done.refs_1_.refs_6_.refs_4_), channel_id=1, source_target_pairs={{0,224},{32,0},{64,32},{96,64},{128,96},{160,128},{192,160},{224,1... | collective-permute-start | bytes 1179656 | tf_op jit(solution)/shard_map/ppermute | solution.py:35
  30.1 9.4 %collective-permute-start.5 = (bf16[1536,128]{1,0:T(8,128)(2,1)S(1)}, bf16[1536,128]{1,0:T(8,128)(2,1)S(1)}, u32[]{:S(2)}, u32[]{:S(2)}) collective-permute-start(bf16[1536,128]{1,0:T(8,128)(2,1)S(1)} %collective-permute-done.3.refs_4_.refs_9_.refs_7_), channel_id=1, source_target_pairs={{0,32},{32,64},{64,96},{96,128},{128,160},{160,192},{192,224},{224... | collective-permute-start | bytes 1179656 | tf_op jit(solution)/shard_map/ppermute | solution.py:35
  34.5 9.1 %collective-permute-start.4 = (bf16[1536,128]{1,0:T(8,128)(2,1)S(1)}, bf16[1536,128]{1,0:T(8,128)(2,1)}, u32[]{:S(2)}, u32[]{:S(2)}) collective-permute-start(bf16[1536,128]{1,0:T(8,128)(2,1)S(1)} %collective-permute-done.2.refs_3_.refs_8_.refs_6_), channel_id=1, source_target_pairs={{0,224},{32,0},{64,32},{96,64},{128,96},{160,128},{192,160},{224,1... | collective-permute-start | bytes 1179656 | tf_op jit(solution)/shard_map/ppermute | solution.py:35
  39.5 8.6 %collective-permute-start.6 = (bf16[1536,128]{1,0:T(8,128)(2,1)S(1)}, bf16[1536,128]{1,0:T(8,128)(2,1)}, u32[]{:S(2)}, u32[]{:S(2)}) collective-permute-start(bf16[1536,128]{1,0:T(8,128)(2,1)S(1)} %collective-permute-done.5.refs_6_.refs_11_), channel_id=1, source_target_pairs={{0,32},{32,64},{64,96},{96,128},{128,160},{160,192},{192,224},{224... | collective-permute-start | bytes 1179656 | tf_op jit(solution)/shard_map/ppermute | solution.py:35
  39.6 10.8 %copy-start.1 = (bf16[8,1,48,1536]{3,2,1,0:T(8,128)(2,1)S(1)}, bf16[8,1,48,1536]{3,2,1,0:T(8,128)(2,1)}, u32[]{:S(2)}) copy-start(bf16[8,1,48,1536]{3,2,1,0:T(8,128)(2,1)} %param.6) | copy-start | bytes 3538948
  49.6 0.7 copy-start.3
  56.2 10.7 %collective-permute-start.11 = (f32[4,48,2816]{2,1,0:T(8,128)S(1)}, f32[4,48,2816]{2,1,0:T(8,128)S(1)}, u32[]{:S(2)}, u32[]{:S(2)}) collective-permute-start(f32[4,48,2816]{2,1,0:T(8,128)S(1)} %get-tuple-element.41), channel_id=1, source_target_pairs={{0,1},{1,0},{2,3},{3,2},{4,5},{5,4},{6,7},{7,6},{8,9},{9,8},{10,11... | collective-permute-start | bytes 6488072 | tf_op jit(solution)/shard_map/ppermute | solution.py:51
  63.4 2.7 %collective-permute-start.12 = (f32[4,48,1280]{2,1,0:T(8,128)S(1)}, f32[4,48,1280]{2,1,0:T(8,128)S(1)}, u32[]{:S(2)}, u32[]{:S(2)}) collective-permute-start(f32[4,48,1280]{2,1,0:T(8,128)S(1)} %get-tuple-element.46), channel_id=1, source_target_pairs={{0,1},{1,0},{2,3},{3,2},{4,5},{5,4},{6,7},{7,6},{8,9},{9,8},{10,11... | collective-permute-start | bytes 2949128 | tf_op jit(solution)/shard_map/ppermute | solution.py:51
  69.5 4.2 %copy-start.4 = (bf16[192,1024]{1,0:T(8,128)(2,1)S(1)}, bf16[192,1024]{1,0:T(8,128)(2,1)}, u32[]{:S(2)}) copy-start(bf16[192,1024]{1,0:T(8,128)(2,1)} %copy-done.3) | copy-start | bytes 1179652
  69.5 5.1 %copy-start.5 = (s32[32]{0:T(128)S(1)}, s32[32]{0:T(128)}, u32[]{:S(2)}) copy-start(s32[32]{0:T(128)} %pair_ref.1) | copy-start | bytes 388
  69.5 5.1 %copy-start.6 = (s32[32]{0:T(128)S(1)}, s32[32]{0:T(128)}, u32[]{:S(2)}) copy-start(s32[32]{0:T(128)} %block_ref.1) | copy-start | bytes 388
  69.5 5.1 %copy-start.7 = (s32[32]{0:T(128)S(1)}, s32[32]{0:T(128)}, u32[]{:S(2)}) copy-start(s32[32]{0:T(128)} %live_ref.1) | copy-start | bytes 388
  69.5 24.9 %all-to-all-start = ((s16[4,48,4224]{2,1,0:T(8,128)(2,1)}), s16[4,48,4224]{2,1,0:T(8,128)(2,1)S(1)}, u32[]{:S(2)}, u32[]{:S(2)}) async-start(s16[4,48,4224]{2,1,0:T(8,128)(2,1)} %shard_map.74), calls=%async_computation | async-start | bytes 3244032 | tf_op jit(solution)/shard_map/all_to_all | solution.py:386
  73.7 10.1 %collective-permute-start.13 = (bf16[192,1024]{1,0:T(8,128)(2,1)S(1)}, bf16[192,1024]{1,0:T(8,128)(2,1)S(1)}, u32[]{:S(2)}, u32[]{:S(2)}) collective-permute-start(bf16[192,1024]{1,0:T(8,128)(2,1)S(1)} %copy-done.4), channel_id=1, source_target_pairs={{0,24},{8,0},{16,8},{24,16},{1,25},{9,1},{17,9},{25,17},{2,26},{10... | collective-permute-start | bytes 1179656 | tf_op jit(solution)/shard_map/ppermute | solution.py:39
  74.6 11.2 %collective-permute-start.14 = (bf16[192,1024]{1,0:T(8,128)(2,1)S(1)}, bf16[192,1024]{1,0:T(8,128)(2,1)S(1)}, u32[]{:S(2)}, u32[]{:S(2)}) collective-permute-start(bf16[192,1024]{1,0:T(8,128)(2,1)S(1)} %copy-done.4), channel_id=1, source_target_pairs={{0,16},{8,24},{16,0},{24,8},{1,17},{9,25},{17,1},{25,9},{2,18},{10... | collective-permute-start | bytes 1179656 | tf_op jit(solution)/shard_map/ppermute | solution.py:39
  97.1 3.9 %collective-permute-start.15 = (bf16[64,1024]{1,0:T(8,128)(2,1)S(1)}, bf16[64,1024]{1,0:T(8,128)(2,1)S(1)}, u32[]{:S(2)}, u32[]{:S(2)}) collective-permute-start(bf16[64,1024]{1,0:T(8,128)(2,1)S(1)} %get-tuple-element.51), channel_id=1, source_target_pairs={{0,24},{2,26},{4,12},{6,14},{8,0},{10,2},{12,20},{14,22},{16,8},{1... | collective-permute-start | bytes 393224 | tf_op jit(solution)/shard_map/ppermute | solution.py:47
  98.1 5.6 %collective-permute-start.16 = (bf16[64,1024]{1,0:T(8,128)(2,1)S(1)}, bf16[64,1024]{1,0:T(8,128)(2,1)S(1)}, u32[]{:S(2)}, u32[]{:S(2)}) collective-permute-start(bf16[64,1024]{1,0:T(8,128)(2,1)S(1)} %get-tuple-element.52), channel_id=1, source_target_pairs={{0,8},{2,10},{4,28},{6,30},{8,16},{10,18},{12,4},{14,6},{16,24},{1... | collective-permute-start | bytes 393224 | tf_op jit(solution)/shard_map/ppermute | solution.py:47
  98.6 7.0 %collective-permute-start.17 = (bf16[64,1024]{1,0:T(8,128)(2,1)S(1)}, bf16[64,1024]{1,0:T(8,128)(2,1)S(1)}, u32[]{:S(2)}, u32[]{:S(2)}) collective-permute-start(bf16[64,1024]{1,0:T(8,128)(2,1)S(1)} %get-tuple-element.53), channel_id=1, source_target_pairs={{0,16},{2,18},{4,20},{6,22},{8,24},{10,26},{12,28},{14,30},{16,0},... | collective-permute-start | bytes 393224 | tf_op jit(solution)/shard_map/ppermute | solution.py:47
  106.3 19.5 %all-to-all-start.1 = ((f32[64,1,128]{2,1,0:T(1,128)}), f32[64,1,128]{2,1,0:T(1,128)S(1)}, u32[]{:S(2)}, u32[]{:S(2)}) async-start(f32[64,1,128]{2,1,0:T(1,128)} %bitcast.7), calls=%async_computation.1 | async-start | bytes 65536 | tf_op jit(solution)/shard_map/all_to_all | solution.py:406
